TPU v7x, 32 devices: a whole 2x2x4 slice. The times are simulated.
32 devices in a mesh: dp: 8 (over y, x, core), expert: 4 (over z).
Axes of the slice: x: 2, y: 2, z: 4, core: 2. Of those that a mesh axis runs over, the one named last changes fastest.
Arguments:
- tokens: bfloat16 [12608, 768], P(('dp', 'expert')), may hold values from -6 to 6
- routes: int32 [12608, 2], P(('dp', 'expert')), may hold values from 0 to 15, all different within a row; in each aligned block of 197 rows (0 to 196, 197 to 393, ...) at most 41 rows name the same one
- gain_one: float32 [768], replicated, may hold values from 0.5 to 1.5
- shift_one: float32 [768], replicated, may hold values from -1 to 1
- w_qkv: bfloat16 [768, 2304], replicated, may hold values from -0.21875 to 0.21875
- qv_bias: float32 [2, 768], replicated, may hold values from -1 to 1
- w_out: bfloat16 [768, 768], replicated, may hold values from -2.5 to 2.5
- out_bias: float32 [768], replicated, may hold values from -1 to 1
- gain_two: float32 [768], replicated, may hold values from 0.5 to 1.5
- shift_two: float32 [768], replicated, may hold values from -1 to 1
- w_route: bfloat16 [768, 16], replicated, may hold values from -0.15625 to 0.15625
- w_in: bfloat16 [16, 768, 3072], P('expert'), may hold values from -0.21875 to 0.21875
- b_in: float32 [16, 3072], P('expert'), may hold values from -1 to 1
- w_back: bfloat16 [16, 3072, 768], P('expert'), may hold values from -3.5 to 3.5
- b_back: float32 [16, 768], P('expert'), may hold values from -15 to 15
- d_out: bfloat16 [12608, 768], P(('dp', 'expert')), may hold values from -6 to 6
Outputs:
- block_out: bfloat16 [12608, 768], P(('dp', 'expert'))
- input_grad: float32 [12608, 768], P(('dp', 'expert'))
- gain_one_grad: float32 [768], replicated
- shift_one_grad: float32 [768], replicated
- w_qkv_grad: float32 [768, 2304], replicated
- qv_bias_grad: float32 [2, 768], replicated
- w_out_grad: float32 [768, 768], replicated
- out_bias_grad: float32 [768], replicated
- gain_two_grad: float32 [768], replicated
- shift_two_grad: float32 [768], replicated
- w_route_grad: float32 [768, 16], replicated
- w_in_grad: float32 [16, 768, 3072], P('expert', 'dp')
- b_in_grad: float32 [16, 3072], P('expert', 'dp')
- w_back_grad: float32 [16, 3072, 768], P('expert', 'dp')
- b_back_grad: float32 [16, 768], P('expert', 'dp')
Inputs may be any that keep to these rules, and one draw needn't show every extreme that they name: `routes`: within each aligned block of 197 rows (one device's tokens of one micro-batch) the two experts of a row differ, and no expert is named by more than 41 rows; some expert is named by exactly 41 rows of a block.
All inputs are finite; a program needn't handle non-finite values.
Results may differ from a plain program's by a relative error of at most 0.015.
Values may be sent and summed in bfloat16 or wider, within the bound.
A program may use at most 320 MiB of HBM per device.

v0:
```python
import jax
import jax.numpy as jnp
from jax import lax
from jax.sharding import PartitionSpec as P

HEADS = 12
HEAD_DIM = 64
SEQ = 197
TOP = 2
MB = 2
ROWS_MB = 197


HIGH = lax.Precision.HIGHEST
EPSILON = 1e-06


def layer_norm(value, gain, shift):
    center = value - jnp.mean(value, axis=-1, keepdims=True)
    spread = jnp.mean(center * center, axis=-1, keepdims=True)
    return center * lax.rsqrt(spread + EPSILON) * gain + shift


def route_soft(logits):
    return jax.nn.softmax(logits, axis=-1)


def body(
    tokens,
    routes,
    gain_one,
    shift_one,
    w_qkv,
    qv_bias,
    w_out,
    out_bias,
    gain_two,
    shift_two,
    w_route,
    w_in,
    b_in,
    w_back,
    b_back,
    d_out,
):
    groups = lax.axis_size("expert")
    local = w_in.shape[0]
    experts = groups * local
    width = tokens.shape[1]
    rows = ROWS_MB
    cap = 5 * rows * TOP // (3 * experts)
    images = rows // SEQ
    scale = HEAD_DIM ** (-0.5)
    expert_ids = jnp.arange(experts, dtype=jnp.int32)
    w_route_wide = w_route.astype(jnp.float32)
    acc_gain_one = jnp.zeros_like(gain_one)
    acc_shift_one = jnp.zeros_like(shift_one)
    acc_qkv = jnp.zeros(w_qkv.shape, jnp.float32)
    acc_qv = jnp.zeros_like(qv_bias)
    acc_out = jnp.zeros(w_out.shape, jnp.float32)
    acc_out_bias = jnp.zeros_like(out_bias)
    acc_gain_two = jnp.zeros_like(gain_two)
    acc_shift_two = jnp.zeros_like(shift_two)
    acc_route = jnp.zeros(w_route.shape, jnp.float32)
    acc_expert = None
    outputs = []
    input_grads = []
    for part in range(MB):
        x = tokens[part * rows : (part + 1) * rows].astype(jnp.float32)
        route = routes[part * rows : (part + 1) * rows]
        cotan = d_out[part * rows : (part + 1) * rows].astype(jnp.float32)
        normed, ln_one_pull = jax.vjp(layer_norm, x, gain_one, shift_one)
        normed_low = normed.astype(jnp.bfloat16)
        bias = jnp.concatenate([qv_bias[0], jnp.zeros_like(qv_bias[0]), qv_bias[1]])
        qkv = (jnp.dot(normed_low, w_qkv, preferred_element_type=jnp.float32) + bias).astype(
            jnp.bfloat16
        )
        query = qkv[:, :width].reshape(images, SEQ, HEADS, HEAD_DIM)
        keys = qkv[:, width : 2 * width].reshape(images, SEQ, HEADS, HEAD_DIM)
        values = qkv[:, 2 * width :].reshape(images, SEQ, HEADS, HEAD_DIM)
        scores = (
            jnp.einsum("ishd,ithd->ihst", query, keys, preferred_element_type=jnp.float32) * scale
        )
        log_total = jax.nn.logsumexp(scores, axis=-1, keepdims=True)
        probs_low = jnp.exp(scores - log_total).astype(jnp.bfloat16)
        mixed = jnp.einsum("ihst,ithd->ishd", probs_low, values, preferred_element_type=jnp.float32)
        mixed = mixed.reshape(rows, width).astype(jnp.bfloat16)
        resid = x + jnp.dot(mixed, w_out, preferred_element_type=jnp.float32) + out_bias
        inner, ln_two_pull = jax.vjp(layer_norm, resid, gain_two, shift_two)
        inner_low = inner.astype(jnp.bfloat16)
        logits = jnp.dot(inner_low, w_route, preferred_element_type=jnp.float32)
        route_probs, soft_pull = jax.vjp(route_soft, logits)
        choose = (route[:, :, None] == expert_ids[None, None, :]).astype(jnp.float32)
        gates = jnp.einsum("rke,re->rk", choose, route_probs, precision=HIGH)
        flat_ids = route.reshape(-1)
        table = (flat_ids[:, None] == expert_ids[None, :]).astype(jnp.int32)
        before = jnp.cumsum(table, axis=0) - table
        slot = jnp.sum(before * table, axis=1)
        dest = flat_ids * cap + slot
        sending = (
            jnp.zeros((experts * cap, width), jnp.bfloat16)
            .at[dest]
            .set(jnp.repeat(inner_low, TOP, axis=0))
        )
        sending = sending.reshape(groups, local, cap, width)
        received = lax.all_to_all(sending, "expert", split_axis=0, concat_axis=0, tiled=True)
        hidden = jnp.einsum("secd,edf->secf", received, w_in, preferred_element_type=jnp.float32)
        hidden = hidden + b_in[None, :, None, :]
        active = jax.nn.gelu(hidden).astype(jnp.bfloat16)
        result = jnp.einsum("secf,efd->secd", active, w_back, preferred_element_type=jnp.float32)
        result = (result + b_back[None, :, None, :]).astype(jnp.bfloat16)
        returned = lax.all_to_all(result, "expert", split_axis=0, concat_axis=0, tiled=True)
        returned, kept_rows, kept_hidden = (returned, received, hidden)
        picked = (
            returned.reshape(experts * cap, width)[dest]
            .reshape(rows, TOP, width)
            .astype(jnp.float32)
        )
        block = resid + jnp.sum(gates[:, :, None] * picked, axis=1)
        outputs.append(block.astype(jnp.bfloat16))
        grad_gate = jnp.sum(picked * cotan[:, None, :], axis=2)
        grad_picked = (gates[:, :, None] * cotan[:, None, :]).astype(jnp.bfloat16)
        grad_send = (
            jnp.zeros((experts * cap, width), jnp.bfloat16)
            .at[dest]
            .set(grad_picked.reshape(rows * TOP, width))
        )
        grad_send = grad_send.reshape(groups, local, cap, width)
        grad_recv = lax.all_to_all(grad_send, "expert", split_axis=0, concat_axis=0, tiled=True)
        active, gelu_pull = jax.vjp(jax.nn.gelu, kept_hidden)
        active_low = active.astype(jnp.bfloat16)
        grad_active = jnp.einsum(
            "secd,efd->secf", grad_recv, w_back, preferred_element_type=jnp.float32
        )
        grad_hidden = gelu_pull(grad_active)[0].astype(jnp.bfloat16)
        step_w_back = jnp.einsum(
            "secf,secd->efd", active_low, grad_recv, preferred_element_type=jnp.float32
        )
        step_b_back = jnp.sum(grad_recv.astype(jnp.float32), axis=(0, 2))
        step_w_in = jnp.einsum(
            "secd,secf->edf", kept_rows, grad_hidden, preferred_element_type=jnp.float32
        )
        step_b_in = jnp.sum(grad_hidden.astype(jnp.float32), axis=(0, 2))
        grad_rows = jnp.einsum(
            "secf,edf->secd", grad_hidden, w_in, preferred_element_type=jnp.float32
        )
        grad_rows = grad_rows.astype(jnp.bfloat16)
        grad_back = lax.all_to_all(grad_rows, "expert", split_axis=0, concat_axis=0, tiled=True)
        shares = (step_w_in, step_b_in, step_w_back, step_b_back)
        if acc_expert is None:
            acc_expert = shares
        else:
            acc_expert = tuple((a + b for a, b in zip(acc_expert, shares)))
        grad_inner = jnp.sum(
            grad_back.reshape(experts * cap, width)[dest]
            .reshape(rows, TOP, width)
            .astype(jnp.float32),
            axis=1,
        )
        grad_probs = jnp.einsum("rk,rke->re", grad_gate, choose, precision=HIGH)
        grad_logits = soft_pull(grad_probs)[0]
        acc_route = acc_route + jnp.einsum(
            "rd,re->de", inner_low.astype(jnp.float32), grad_logits, precision=HIGH
        )
        grad_inner = grad_inner + jnp.einsum("re,de->rd", grad_logits, w_route_wide, precision=HIGH)
        grad_ln_two, grad_gain_two, grad_shift_two = ln_two_pull(grad_inner)
        acc_gain_two = acc_gain_two + grad_gain_two
        acc_shift_two = acc_shift_two + grad_shift_two
        grad_resid = cotan + grad_ln_two
        grad_att = grad_resid.astype(jnp.bfloat16)
        acc_out = acc_out + jnp.einsum(
            "rd,re->de", mixed, grad_att, preferred_element_type=jnp.float32
        )
        acc_out_bias = acc_out_bias + jnp.sum(grad_att.astype(jnp.float32), axis=0)
        grad_mixed = jnp.einsum("re,de->rd", grad_att, w_out, preferred_element_type=jnp.float32)
        grad_mixed = grad_mixed.astype(jnp.bfloat16).reshape(images, SEQ, HEADS, HEAD_DIM)
        again = (
            jnp.einsum("ishd,ithd->ihst", query, keys, preferred_element_type=jnp.float32) * scale
        )
        probs = jnp.exp(again - log_total)
        grad_probs_att = jnp.einsum(
            "ishd,ithd->ihst", grad_mixed, values, preferred_element_type=jnp.float32
        )
        row_total = jnp.sum(probs * grad_probs_att, axis=-1, keepdims=True)
        grad_scores = (probs * (grad_probs_att - row_total)).astype(jnp.bfloat16)
        grad_query = (
            jnp.einsum("ihst,ithd->ishd", grad_scores, keys, preferred_element_type=jnp.float32)
            * scale
        )
        grad_keys = (
            jnp.einsum("ihst,ishd->ithd", grad_scores, query, preferred_element_type=jnp.float32)
            * scale
        )
        grad_values = jnp.einsum(
            "ihst,ishd->ithd",
            probs.astype(jnp.bfloat16),
            grad_mixed,
            preferred_element_type=jnp.float32,
        )
        grad_qkv = jnp.concatenate(
            [
                grad_query.reshape(rows, width),
                grad_keys.reshape(rows, width),
                grad_values.reshape(rows, width),
            ],
            axis=1,
        ).astype(jnp.bfloat16)
        acc_qkv = acc_qkv + jnp.einsum(
            "rd,re->de", normed_low, grad_qkv, preferred_element_type=jnp.float32
        )
        column_sums = jnp.sum(grad_qkv.astype(jnp.float32), axis=0)
        acc_qv = acc_qv + jnp.stack([column_sums[:width], column_sums[2 * width :]])
        grad_normed = jnp.einsum("re,de->rd", grad_qkv, w_qkv, preferred_element_type=jnp.float32)
        grad_ln_one, grad_gain_one, grad_shift_one = ln_one_pull(grad_normed)
        acc_gain_one = acc_gain_one + grad_gain_one
        acc_shift_one = acc_shift_one + grad_shift_one
        input_grads.append(grad_resid + grad_ln_one)
    expert_grads = (
        lax.psum_scatter(
            acc_expert[0].astype(jnp.bfloat16), "dp", scatter_dimension=1, tiled=True
        ).astype(jnp.float32),
        lax.psum_scatter(
            acc_expert[1].astype(jnp.bfloat16), "dp", scatter_dimension=1, tiled=True
        ).astype(jnp.float32),
        lax.psum_scatter(
            acc_expert[2].astype(jnp.bfloat16), "dp", scatter_dimension=1, tiled=True
        ).astype(jnp.float32),
        lax.psum_scatter(
            acc_expert[3].astype(jnp.bfloat16), "dp", scatter_dimension=1, tiled=True
        ).astype(jnp.float32),
    )
    shared = (
        acc_gain_one,
        acc_shift_one,
        acc_qkv,
        acc_qv,
        acc_out,
        acc_out_bias,
        acc_gain_two,
        acc_shift_two,
        acc_route,
    )
    shared = lax.psum(
        (
            shared[0],
            shared[1],
            shared[2],
            shared[3],
            shared[4],
            shared[5],
            shared[6],
            shared[7],
            shared[8],
        ),
        ("dp", "expert"),
    )
    return (
        jnp.concatenate(outputs, axis=0),
        jnp.concatenate(input_grads, axis=0),
        shared[0],
        shared[1],
        shared[2],
        shared[3],
        shared[4],
        shared[5],
        shared[6],
        shared[7],
        shared[8],
        expert_grads[0],
        expert_grads[1],
        expert_grads[2],
        expert_grads[3],
    )


def solution(mesh):
    return jax.shard_map(
        body,
        mesh=mesh,
        in_specs=(
            P(("dp", "expert"), None),
            P(("dp", "expert"), None),
            P(),
            P(),
            P(),
            P(),
            P(),
            P(),
            P(),
            P(),
            P(),
            P("expert", None, None),
            P("expert", None),
            P("expert", None, None),
            P("expert", None),
            P(("dp", "expert"), None),
        ),
        out_specs=(
            P(("dp", "expert"), None),
            P(("dp", "expert"), None),
            P(),
            P(),
            P(),
            P(),
            P(),
            P(),
            P(),
            P(),
            P(),
            P("expert", "dp", None),
            P("expert", "dp"),
            P("expert", "dp", None),
            P("expert", "dp"),
        ),
        check_vma=False,
    )
```

profile of v0, /device:TPU:0, one launch (start us, length us, event | category | flops | bytes accessed | tf_op | source)
XLA Modules:
  0.0 928.3 jit_solution(7346553515477841144)
XLA Ops:
  18.7 3.1 reduce-window.14
  52.7 3.0 mul.547
  72.2 4.2 scatter_custom_fusion.2
  78.7 2.8 copy.117
  81.4 6.3 all-to-all-start.4
  90.2 3.1 reduce-window.16
  99.8 3.0 mul.588
  111.7 4.0 scatter_custom_fusion.3
  117.9 2.7 copy.125
  120.7 5.5 all-to-all-start.6
  128.3 2.6 reshape.638
  130.9 3.7 scatter_custom_fusion.1
  136.9 2.7 copy.113
  139.7 10.9 %all-to-all-done.6 = bf16[4,4,41,768]{3,1,2,0:T(4,128)(2,1)} async-done(((bf16[4,4,41,768]{3,1,2,0:T(4,128)(2,1)}), bf16[4,4,41,768]{3,1,2,0:T(4,128)(2,1)}, u32[]{:S(2)}, u32[]{:S(2)}) %all-to-all-start.6) | async-done | bytes 1007648 | tf_op jit(solution)/shard_map/all_to_all | solution.py:129
  150.6 4.2 all-to-all-start.2
  157.0 2.6 reshape.630
  159.6 3.7 scatter_custom_fusion
  165.6 2.7 copy.100
  172.6 6.7 all-to-all-done.2
  179.2 4.2 all-to-all-start
  183.7 14.2 %fusion.14 = f32[4,4,41,3072]{3,2,1,0:T(8,128)} fusion(bf16[4,768,3072]{2,1,0:T(8,128)(2,1)} %param.27, bf16[4,4,41,768]{3,1,2,0:T(4,128)(2,1)} %all-to-all-done.2), kind=kOutput, calls=%fused_computation.24 | convolution fusion | flops 3095396352 | bytes 27942912 | tf_op jit(solution)/shard_map/secd,edf->secf/dot_general | solution.py:107
  198.0 9.9 %all-to-all-done = bf16[4,4,41,768]{3,1,2,0:T(4,128)(2,1)} async-done(((bf16[4,4,41,768]{3,1,2,0:T(4,128)(2,1)}), bf16[4,4,41,768]{3,1,2,0:T(4,128)(2,1)}, u32[]{:S(2)}, u32[]{:S(2)}) %all-to-all-start) | async-done | bytes 1007648 | tf_op jit(solution)/shard_map/all_to_all | solution.py:106
  207.9 14.2 %fusion.16 = f32[4,4,41,3072]{3,2,1,0:T(8,128)} fusion(bf16[4,768,3072]{2,1,0:T(8,128)(2,1)} %param.27, bf16[4,4,41,768]{3,1,2,0:T(4,128)(2,1)} %all-to-all-done), kind=kOutput, calls=%fused_computation.26 | convolution fusion | flops 3095396352 | bytes 27942912 | tf_op jit(solution)/shard_map/secd,edf->secf/dot_general | solution.py:107
  222.1 17.6 %convert_reduce_fusion = (f32[4,3072]{1,0:T(4,128)}, bf16[4,4,41,3072]{3,2,0,1:T(8,128)(2,1)}) fusion(f32[4,4,41,3072]{3,2,1,0:T(8,128)} %fusion.14, f32[4,3072]{1,0:T(4,128)} %param.28, bf16[4,3072,768]{2,1,0:T(8,128)(2,1)} %param.29, bf16[4,4,41,768]{3,1,2,0:T(4,128)(2,1)} %all-to-all-done.6), kind=kOutput, calls=%fused_computation.60 | convolution fusion | flops 3141734400 | bytes 32071680 | tf_op jit(solution)/shard_map/secd,efd->secf/dot_general | solution.py:132
  239.7 17.4 %convert_reduce_fusion.1 = (f32[4,3072]{1,0:T(4,128)}, bf16[4,4,41,3072]{3,2,0,1:T(8,128)(2,1)}) fusion(f32[4,4,41,3072]{3,2,1,0:T(8,128)} %fusion.16, f32[4,3072]{1,0:T(4,128)} %param.28, bf16[4,3072,768]{2,1,0:T(8,128)(2,1)} %param.29, bf16[4,4,41,768]{3,1,2,0:T(4,128)(2,1)} %all-to-all-done.4), kind=kOutput, calls=%fused_computation.61 | convolution fusion | flops 3141734400 | bytes 32071680 | tf_op jit(solution)/shard_map/secd,efd->secf/dot_general | solution.py:132
  260.6 18.4 %fusion.78 = f32[4,3072,768,1]{2,1,3,0:T(8,128)} fusion(bf16[4,4,41,768]{3,1,2,0:T(4,128)(2,1)} %all-to-all-done.4, f32[4,4,41,3072]{3,2,1,0:T(8,128)} %fusion.16, f32[4,3072]{1,0:T(4,128)} %param.28), kind=kOutput, calls=%fused_computation.123 | convolution fusion | flops 3115548672 | bytes 46866432 | tf_op jit(solution)/shard_map/secf,secd->efd/dot_general | solution.py:136
  279.0 24.8 %fusion = bf16[4,3072,768]{2,1,0:T(8,128)(2,1)} fusion(f32[4,3072,768,1]{2,1,3,0:T(8,128)} %fusion.78, bf16[4,4,41,768]{3,1,2,0:T(4,128)(2,1)} %all-to-all-done.6, f32[4,4,41,3072]{3,2,1,0:T(8,128)} %fusion.14, f32[4,3072]{1,0:T(4,128)} %param.28), kind=kOutput, calls=%fused_computation.9 | convolution fusion | flops 3134423040 | bytes 65740800 | tf_op jit(solution)/shard_map/secf,secd->efd/dot_general | solution.py:136
  303.9 25.6 %fusion.83 = f32[4,768,3072,1]{2,1,3,0:T(8,128)} fusion(bf16[4,4,41,3072]{3,2,0,1:T(8,128)(2,1)} %get-tuple-element.107, bf16[4,4,41,768]{3,1,2,0:T(4,128)(2,1)} %all-to-all-done), kind=kOutput, calls=%fused_computation.128 | convolution fusion | flops 3095396352 | bytes 42786816 | tf_op jit(solution)/shard_map/secd,secf->edf/dot_general | solution.py:140
  329.5 24.1 %fusion.1 = bf16[4,768,3072]{2,1,0:T(8,128)(2,1)} fusion(f32[4,768,3072,1]{2,1,3,0:T(8,128)} %fusion.83, bf16[4,4,41,3072]{3,2,0,1:T(8,128)(2,1)} %get-tuple-element.109, bf16[4,4,41,768]{3,1,2,0:T(4,128)(2,1)} %all-to-all-done.2), kind=kOutput, calls=%fused_computation.11 | convolution fusion | flops 3114270720 | bytes 61661184 | tf_op jit(solution)/shard_map/secd,secf->edf/dot_general | solution.py:140
  354.9 14.7 %fusion.67 = bf16[4,4,41,768]{3,2,0,1:T(8,128)(2,1)S(1)} fusion(bf16[4,3072,768]{2,1,0:T(8,128)(2,1)} %param.29, f32[4,768]{1,0:T(4,128)} %param.30, f32[4,4,41,3072]{3,2,1,0:T(8,128)} %fusion.14, f32[4,3072]{1,0:T(4,128)} %param.28), kind=kOutput, calls=%fused_computation.91 | convolution fusion | flops 3116556288 | bytes 28004352 | tf_op jit(solution)/shard_map/secf,efd->secd/dot_general | solution.py:110
  371.3 4.4 all-to-all-start.3
  375.8 11.9 %fusion.58 = bf16[4,4,41,768]{3,2,0,1:T(8,128)(2,1)S(1)} fusion(bf16[4,4,41,3072]{3,2,0,1:T(8,128)(2,1)} %get-tuple-element.109, bf16[4,768,3072]{2,1,0:T(8,128)(2,1)} %param.27), kind=kOutput, calls=%fused_computation.88 | convolution fusion | flops 3095900160 | bytes 23912448 | tf_op jit(solution)/shard_map/secf,edf->secd/dot_general | solution.py:144
  389.5 11.5 %all-to-all-done.3 = bf16[4,4,41,768]{3,1,2,0:T(4,128)(2,1)} async-done(((bf16[4,4,41,768]{3,1,2,0:T(4,128)(2,1)}), bf16[4,4,41,768]{3,1,2,0:T(4,128)(2,1)}, u32[]{:S(2)}, u32[]{:S(2)}) %all-to-all-start.3) | async-done | bytes 1007648 | tf_op jit(solution)/shard_map/all_to_all | solution.py:112
  401.0 4.3 all-to-all-start.7
  405.3 14.7 %fusion.64 = bf16[4,4,41,768]{3,2,0,1:T(8,128)(2,1)S(1)} fusion(bf16[4,3072,768]{2,1,0:T(8,128)(2,1)} %param.29, f32[4,768]{1,0:T(4,128)S(1)} %copy-done.140, f32[4,4,41,3072]{3,2,1,0:T(8,128)} %fusion.16, f32[4,3072]{1,0:T(4,128)} %param.28), kind=kOutput, calls=%fused_computation.90 | convolution fusion | flops 3116556288 | bytes 28004352 | tf_op jit(solution)/shard_map/secf,efd->secd/dot_general | solution.py:110
  421.7 8.0 all-to-all-done.7
  429.7 4.2 all-to-all-start.1
  434.0 12.8 %fusion.61 = bf16[4,4,41,768]{3,2,0,1:T(8,128)(2,1)S(1)} fusion(bf16[4,4,41,3072]{3,2,0,1:T(8,128)(2,1)} %get-tuple-element.107, bf16[4,768,3072]{2,1,0:T(8,128)(2,1)} %param.27), kind=kOutput, calls=%fused_computation.89 | convolution fusion | flops 3095900160 | bytes 23912448 | tf_op jit(solution)/shard_map/secf,edf->secd/dot_general | solution.py:144
  448.5 9.8 %all-to-all-done.1 = bf16[4,4,41,768]{3,1,2,0:T(4,128)(2,1)} async-done(((bf16[4,4,41,768]{3,1,2,0:T(4,128)(2,1)}), bf16[4,4,41,768]{3,1,2,0:T(4,128)(2,1)}, u32[]{:S(2)}, u32[]{:S(2)}) %all-to-all-start.1) | async-done | bytes 1007648 | tf_op jit(solution)/shard_map/all_to_all | solution.py:112
  458.4 4.3 all-to-all-start.5
  468.2 4.4 gather_fusion.1
  472.6 2.8 reshape.591
  475.4 4.5 multiply_reduce_fusion.4
  489.1 4.4 gather_fusion.3
  493.4 2.8 reshape.593
  496.3 3.7 reduce_sum.534
  504.8 4.4 gather_fusion
  509.1 2.9 reshape.589
  512.0 4.8 multiply_reduce_fusion.5
  525.9 4.5 gather_fusion.2
  530.4 2.9 reshape.592
  533.3 3.5 reduce_sum.457
  538.7 3.1 multiply_reduce_fusion.8
  548.9 2.7 convolution_convert_fusion.5
  553.4 2.9 multiply_reduce_fusion
  573.9 3.1 fusion.187
  579.3 4.4 convolution_add_fusion
  583.8 3.8 convolution_add_fusion.3
  596.4 2.7 add_add_fusion.6
  600.2 4.3 convert_element_type.294
  604.4 4.4 convert_element_type.288
  608.9 97.9 %all-reduce.7.cloned.1.call-done = (f32[768]{0:T(1024)}, f32[768]{0:T(1024)}, f32[2,768]{1,0:T(2,128)}, f32[768]{0:T(1024)}, f32[768]{0:T(1024)}, /*index=5*/f32[768]{0:T(1024)}, f32[768,16]{0,1:T(8,128)}) async-done(((f32[768]{0:T(1024)}, f32[768]{0:T(1024)}, f32[2,768]{1,0:T(2,128)}, f32[768]{0:T(1024)}, f32[768]{0:T(1024)}, /*index=5*/f32[768]{0:T(1024)}, f32[768,16]{0,1:T(8,128)}), (f32[768]{0:T(1024)}, ...) | async-done | bytes 70672 | tf_op jit(solution)/shard_map/psum | solution.py:243
  706.8 200.5 %all-reduce.9.cloned.1.call-done = (f32[768,2304]{1,0:T(8,128)}, f32[768,768]{1,0:T(8,128)}) async-done(((f32[768,2304]{1,0:T(8,128)}, f32[768,768]{1,0:T(8,128)}), (f32[768,2304]{1,0:T(8,128)}, f32[768,768]{1,0:T(8,128)})) %all-reduce.9.cloned.1.call-update) | async-done | bytes 9437200 | tf_op jit(solution)/shard_map/psum | solution.py:243
  909.8 6.6 copy.210
  (472 shorter events, 179.9 us)
Async XLA Ops:
  8.0 23.2 %copy-start = (bf16[768,2304]{1,0:T(8,128)(2,1)S(1)}, bf16[768,2304]{1,0:T(8,128)(2,1)}, u32[]{:S(2)}) copy-start(bf16[768,2304]{1,0:T(8,128)(2,1)} %param.20) | copy-start | bytes 10616836
  9.5 21.8 %copy-start.78 = (f32[197]{0:T(256)}, f32[197]{0:T(256)S(1)}, u32[]{:S(2)}) copy-start(f32[197]{0:T(256)S(1)} %get-tuple-element.110) | copy-start | bytes 2368
  9.5 30.5 %copy-start.81 = (f32[197]{0:T(256)}, f32[197]{0:T(256)S(1)}, u32[]{:S(2)}) copy-start(f32[197]{0:T(256)S(1)} %get-tuple-element.111) | copy-start | bytes 2368
  11.5 28.5 %copy-start.97 = (f32[197]{0:T(256)}, f32[197]{0:T(256)S(1)}, u32[]{:S(2)}) copy-start(f32[197]{0:T(256)S(1)} %fusion.148) | copy-start | bytes 2368
  11.5 19.8 %copy-start.94 = (f32[197]{0:T(256)}, f32[197]{0:T(256)S(1)}, u32[]{:S(2)}) copy-start(f32[197]{0:T(256)S(1)} %fusion.150) | copy-start | bytes 2368
  33.3 6.6 copy-start.63
  33.3 6.6 copy-start.67
  72.2 9.2 copy-start.128
  78.6 9.1 copy-start.133
  78.6 16.3 %copy-start.132 = (s32[197,2]{0,1:T(2,128)S(1)}, s32[197,2]{0,1:T(2,128)}, u32[]{:S(2)}) copy-start(s32[197,2]{0,1:T(2,128)} %get-tuple-element.86) | copy-start | bytes 4732
  81.4 39.3 %all-to-all-start.4 = ((bf16[4,4,41,768]{3,1,2,0:T(4,128)(2,1)}), bf16[4,4,41,768]{3,1,2,0:T(4,128)(2,1)}, u32[]{:S(2)}, u32[]{:S(2)}) async-start(bf16[4,4,41,768]{3,1,2,0:T(4,128)(2,1)} %copy.117), calls=%async_computation.4 | async-start | bytes 2015232 | tf_op jit(solution)/shard_map/all_to_all | solution.py:129
  89.5 14.5 %copy-start.99 = (s32[394]{0:T(512)}, s32[394]{0:T(512)S(1)}, u32[]{:S(2)}) copy-start(s32[394]{0:T(512)S(1)} %eq.83) | copy-start | bytes 4732
  111.7 19.2 %copy-start.130 = (s32[394,1]{0,1:T(1,128)}, s32[394,1]{0,1:T(1,128)S(1)}, u32[]{:S(2)}) copy-start(s32[394,1]{0,1:T(1,128)S(1)} %compare_select_fusion) | copy-start | bytes 4732
  120.7 29.9 %all-to-all-start.6 = ((bf16[4,4,41,768]{3,1,2,0:T(4,128)(2,1)}), bf16[4,4,41,768]{3,1,2,0:T(4,128)(2,1)}, u32[]{:S(2)}, u32[]{:S(2)}) async-start(bf16[4,4,41,768]{3,1,2,0:T(4,128)(2,1)} %copy.125), calls=%async_computation.6 | async-start | bytes 2015232 | tf_op jit(solution)/shard_map/all_to_all | solution.py:129
  139.7 20.0 %copy-start.129 = (s32[394,1]{0,1:T(1,128)S(1)}, s32[394,1]{0,1:T(1,128)}, u32[]{:S(2)}) copy-start(s32[394,1]{0,1:T(1,128)} %copy-done.128) | copy-start | bytes 4732
  150.6 28.7 %all-to-all-start.2 = ((bf16[4,4,41,768]{3,1,2,0:T(4,128)(2,1)}), bf16[4,4,41,768]{3,1,2,0:T(4,128)(2,1)}, u32[]{:S(2)}, u32[]{:S(2)}) async-start(bf16[4,4,41,768]{3,1,2,0:T(4,128)(2,1)} %copy.113), calls=%async_computation.2 | async-start | bytes 2015232 | tf_op jit(solution)/shard_map/all_to_all | solution.py:106
  154.8 432.8 %reduce-scatter.15.cloned.1.call-start = ((), (), s32[]{:S(2)}) async-start(), calls=%async_computation.15 | async-start | bytes 221184
  179.2 28.6 %all-to-all-start = ((bf16[4,4,41,768]{3,1,2,0:T(4,128)(2,1)}), bf16[4,4,41,768]{3,1,2,0:T(4,128)(2,1)}, u32[]{:S(2)}, u32[]{:S(2)}) async-start(bf16[4,4,41,768]{3,1,2,0:T(4,128)(2,1)} %copy.100), calls=%async_computation | async-start | bytes 2015232 | tf_op jit(solution)/shard_map/all_to_all | solution.py:106
  183.5 406.7 %reduce-scatter.13.cloned.1.call-start = ((), (), s32[]{:S(2)}) async-start(), calls=%async_computation.14 | async-start | bytes 884736
  260.6 339.6 %reduce-scatter.11.cloned.1.call-start = ((), (), s32[]{:S(2)}) async-start(), calls=%async_computation.13 | async-start | bytes 21233664 | tf_op jit(solution)/shard_map/reduce_scatter | solution.py:225
  303.9 300.6 %reduce-scatter.9.cloned.1.call-start = ((), (), s32[]{:S(2)}) async-start(), calls=%async_computation.12 | async-start | bytes 21233664 | tf_op jit(solution)/shard_map/reduce_scatter | solution.py:219
  371.3 29.6 %all-to-all-start.3 = ((bf16[4,4,41,768]{3,1,2,0:T(4,128)(2,1)}), bf16[4,4,41,768]{3,1,2,0:T(4,128)(2,1)}, u32[]{:S(2)}, u32[]{:S(2)}) async-start(bf16[4,4,41,768]{3,1,2,0:T(4,128)(2,1)} %copy.115), calls=%async_computation.3 | async-start | bytes 2015232 | tf_op jit(solution)/shard_map/all_to_all | solution.py:112
  387.7 17.5 %copy-start.140 = (f32[4,768]{1,0:T(4,128)S(1)}, f32[4,768]{1,0:T(4,128)}, u32[]{:S(2)}) copy-start(f32[4,768]{1,0:T(4,128)} %param.30) | copy-start | bytes 36868
  401.0 28.7 %all-to-all-start.7 = ((bf16[4,4,41,768]{3,1,2,0:T(4,128)(2,1)}), bf16[4,4,41,768]{3,1,2,0:T(4,128)(2,1)}, u32[]{:S(2)}, u32[]{:S(2)}) async-start(bf16[4,4,41,768]{3,1,2,0:T(4,128)(2,1)} %copy.127), calls=%async_computation.7 | async-start | bytes 2015232 | tf_op jit(solution)/shard_map/all_to_all | solution.py:148
  429.7 28.6 %all-to-all-start.1 = ((bf16[4,4,41,768]{3,1,2,0:T(4,128)(2,1)}), bf16[4,4,41,768]{3,1,2,0:T(4,128)(2,1)}, u32[]{:S(2)}, u32[]{:S(2)}) async-start(bf16[4,4,41,768]{3,1,2,0:T(4,128)(2,1)} %copy.102), calls=%async_computation.1 | async-start | bytes 2015232 | tf_op jit(solution)/shard_map/all_to_all | solution.py:112
  446.7 15.9 %copy-start.131 = (s32[394,1]{0,1:T(1,128)S(1)}, s32[394,1]{0,1:T(1,128)}, u32[]{:S(2)}) copy-start(s32[394,1]{0,1:T(1,128)} %copy-done.130) | copy-start | bytes 4732
  446.7 16.0 %copy-start.89 = (f32[197]{0:T(256)S(1)}, f32[197]{0:T(256)}, u32[]{:S(2)}) copy-start(f32[197]{0:T(256)} %copy-done.88) | copy-start | bytes 2368
  458.4 62.9 %all-to-all-start.5 = ((bf16[4,4,41,768]{3,1,2,0:T(4,128)(2,1)}), bf16[4,4,41,768]{3,1,2,0:T(4,128)(2,1)}, u32[]{:S(2)}, u32[]{:S(2)}) async-start(bf16[4,4,41,768]{3,1,2,0:T(4,128)(2,1)} %copy.119), calls=%async_computation.5 | async-start | bytes 2015232 | tf_op jit(solution)/shard_map/all_to_all | solution.py:148
  462.6 244.1 %all-reduce.7.cloned.1.call-start = ((), (), s32[]{:S(2)}) async-start(), calls=%async_computation.16 | async-start | bytes 151552 | tf_op jit(solution)/shard_map/psum | solution.py:243
  462.7 9.9 %copy-start.101 = (s32[1024]{0:T(1024)}, s32[1024]{0:T(1024)S(1)}, u32[]{:S(2)}) copy-start(s32[1024]{0:T(1024)S(1)} %pad_clamp_fusion) | copy-start | bytes 12292
  475.4 7.6 copy-start.55
  483.7 5.3 copy-start.102
  500.0 4.8 copy-start.100
  512.0 4.8 copy-start.61
  512.0 7.9 copy-start.53
  536.8 5.0 copy-start.120
  536.8 5.0 copy-start.122
  536.8 5.0 copy-start.9
  536.8 5.0 copy-start.13
  536.8 5.0 copy-start.46
  536.8 5.0 copy-start.47
  536.8 5.0 copy-start.73
  536.8 5.0 copy-start.85
  536.9 5.0 copy-start.87
  536.9 5.0 copy-start.104
  536.9 5.0 copy-start.106
  557.8 8.3 copy-start.41
  558.3 7.8 copy-start.43
  558.9 7.2 copy-start.39
  567.6 5.1 copy-start.20
  567.6 5.1 copy-start.70
  567.6 5.1 copy-start.77
  567.6 5.1 copy-start.93
  567.6 5.1 copy-start.123
  567.6 5.4 copy-start.18
  567.6 5.4 copy-start.56
  567.7 5.4 copy-start.69
  567.7 5.4 copy-start.75
  567.7 5.4 copy-start.90
  567.7 5.4 copy-start.114
  583.7 323.6 %all-reduce.9.cloned.1.call-start = ((), (), s32[]{:S(2)}) async-start(), calls=%async_computation.17 | async-start | bytes 18874368 | tf_op jit(solution)/shard_map/psum | solution.py:243
  587.5 8.8 copy-start.83
  909.8 6.6 copy-start.134
  909.8 7.2 copy-start.50
  (91 other events, 183.0 us)
Sparse Core Ops, SparseCore 0:
  172.7 34.9 reduce-scatter.14
  260.7 34.0 reduce-scatter.12
  304.0 125.3 reduce-scatter.10
  433.3 126.0 reduce-scatter.8
Sparse Core Ops, SparseCore 1:
  583.8 122.9 all-reduce.6
  714.1 193.1 all-reduce.8
where the time goes:
time: 941 us; the launch traced here: 928 us
  waiting for transfers between devices  355 us (38%)
  matrix products  260 us (28%)
  local copies, waits for them, and re-layouts  171 us (18%)
  other arithmetic  86.2 us (9%)
  starting transfers between devices  37.9 us (4%)
  between operations  17.5 us (2%)
    psum x2, waiting for transfers between devices, body(): lax.psum((shared[0], shared[1], shared[2], shared[3], shared[4], shared[5...  298 us
    dot_general x2, matrix products, body(): jnp.einsum('secd,secf->edf', kept_rows, grad_hidden, preferred_element_ty...  49.7 us
    dot_general x2, matrix products, body(): jnp.einsum('secf,secd->efd', active_low, grad_recv, preferred_element_typ...  43.2 us
    dot_general x2, matrix products, body(): jnp.einsum('secd,efd->secf', grad_recv, w_back, preferred_element_type=jn...  35 us
    dot_general x2, matrix products, body(): jnp.einsum('secf,efd->secd', active, w_back, preferred_element_type=jnp.f...  29.4 us
    unnamed x295, local copies, waits for them, and re-layouts  29.2 us
    dot_general x2, matrix products, body(): jnp.einsum('secd,edf->secf', received, w_in, preferred_element_type=jnp.f...  28.5 us
    dot_general x2, matrix products, body(): jnp.einsum('secf,edf->secd', grad_hidden, w_in, preferred_element_type=jn...  24.7 us
  transfers between devices with their start and end apart: 14, of which 8 were waited for; matrix products, arithmetic and copies ran while one was open for 46% of the time, Pallas kernels for 0%

commit v1 on v0

--- a/solution.py
+++ b/solution.py
@@ -1,6 +1,8 @@
 import jax
 import jax.numpy as jnp
 from jax import lax
+from jax.experimental import pallas as pl
+from jax.experimental.pallas import tpu as pltpu
 from jax.sharding import PartitionSpec as P
 
 HEADS = 12
@@ -9,6 +11,7 @@
 TOP = 2
 MB = 2
 ROWS_MB = 197
+D = 768
 
 
 HIGH = lax.Precision.HIGHEST
@@ -25,7 +28,7 @@
     return jax.nn.softmax(logits, axis=-1)
 
 
-def body(
+def general_body(
     tokens,
     routes,
     gain_one,
@@ -94,7 +97,11 @@
         gates = jnp.einsum("rke,re->rk", choose, route_probs, precision=HIGH)
         flat_ids = route.reshape(-1)
         table = (flat_ids[:, None] == expert_ids[None, :]).astype(jnp.int32)
-        before = jnp.cumsum(table, axis=0) - table
+        order = jnp.arange(rows * TOP, dtype=jnp.int32)
+        earlier = (order[None, :] < order[:, None]).astype(jnp.bfloat16)
+        before = jnp.dot(
+            earlier, table.astype(jnp.bfloat16), preferred_element_type=jnp.float32
+        ).astype(jnp.int32)
         slot = jnp.sum(before * table, axis=1)
         dest = flat_ids * cap + slot
         sending = (
@@ -273,9 +280,503 @@
     )
 
 
+F32, BF16 = jnp.float32, jnp.bfloat16
+NZ = 4
+LOCAL = 4
+PAIRS = HEADS // 2
+T = 208
+KEYS = 256
+CAP_ROWS = 48
+ROWS = NZ * CAP_ROWS
+CHUNK = 768
+MESH = pl.DeviceIdType.MESH
+NT = (((1,), (1,)), ((), ()))
+TN = (((0,), (0,)), ((), ()))
+
+
+def dot(a, b, dims=(((1,), (0,)), ((), ()))):
+    return lax.dot_general(a, b, dims, preferred_element_type=F32)
+
+
+def normal(value):
+    center = value - jnp.mean(value, axis=-1, keepdims=True)
+    scale = lax.rsqrt(jnp.mean(center * center, axis=-1, keepdims=True) + EPSILON)
+    return center * scale, scale
+
+
+def half_mask(which):
+    lane = lax.broadcasted_iota(jnp.int32, (1, 128), 1)
+    return ((lane < 64) if which == 0 else (lane >= 64)).astype(F32).astype(BF16)
+
+
+def attention_probs(scores):
+    key = lax.broadcasted_iota(jnp.int32, scores.shape, 1)
+    scores = jnp.where(key < SEQ, scores, -1e30)
+    top = jnp.max(scores, axis=-1, keepdims=True)
+    raised = jnp.exp(scores - top)
+    return raised / jnp.sum(raised, axis=-1, keepdims=True)
+
+
+def route_table(rt_ref, mb):
+    row = lax.broadcasted_iota(jnp.int32, (32, T), 0)
+    part = lax.rem(row, 8)
+    expert = jnp.where(part < LOCAL, (row // 8) * LOCAL + part, -7)
+    first = rt_ref[mb, 0:1, :]
+    second = rt_ref[mb, 1:2, :]
+    return jnp.logical_or(expert == first, expert == second), part < LOCAL
+
+
+def route_softmax(logits, real):
+    logits = jnp.where(real, logits, -1e30)
+    raised = jnp.exp(logits - jnp.max(logits, axis=0, keepdims=True))
+    raised = jnp.where(real, raised, 0.0)
+    return raised / jnp.sum(raised, axis=0, keepdims=True)
+
+
+def pick_matrix(slots):
+    index = lax.broadcasted_iota(jnp.int32, (CAP_ROWS, T), 0).astype(F32)
+    return jnp.concatenate(
+        [(index == slots[e : e + 1, :]).astype(F32) for e in range(LOCAL)], axis=0
+    )
+
+
+def dispatch_kernel(
+    tok, rt, g1, s1, wqkv, bqkv, wout, bout, g2, s2, wrt, b_in, b_back, dout, w_in, w_back,
+    qkv_o, mixed_o, resid_o, rp_o, gg_o, bb_o, bi_o, x_o, gp_o, act_o, gh_o, pb_o, pg_o,
+    gi, gd, sg, qkv_s, mixed_s, inner_s, xs, gs, cs, rgs, ggs, wb1, wb2, act_st, gh_st, acc_o, acc_g,
+    os_, grs, pb_s, pg_s,
+    send_sem, recv_sem, d_sem, w_sem, st_sem, x_sem, p_sem,
+):
+    dp = lax.axis_index("dp")
+    z = lax.axis_index("expert")
+
+    def item_ref(kind, source, mb):
+        return (gd, sg, gi)[kind].at[source, mb]
+
+    def hop(up, kind, mb, h):
+        source = z - h if up else z + h
+        target = z + 1 if up else z - 1
+        index = (0 if up else 1, kind * MB + mb, h)
+        return pltpu.make_async_remote_copy(
+            src_ref=item_ref(kind, source, mb),
+            dst_ref=item_ref(kind, source, mb),
+            send_sem=send_sem.at[index],
+            recv_sem=recv_sem.at[index],
+            device_id=(dp, target),
+            device_id_type=MESH,
+        )
+
+    def leaves(up, h):
+        return jnp.logical_and(z - h >= 0, z + 1 < NZ) if up else jnp.logical_and(z + h < NZ, z >= 1)
+
+    def arrives(up, h):
+        return (z - h - 1 >= 0) if up else (z + h + 1 < NZ)
+
+    def start(kind, mb, h):
+        for up in (True, False):
+            @pl.when(leaves(up, h))
+            def _():
+                hop(up, kind, mb, h).start()
+
+    def pass_on(kind, mb, h):
+        for up in (True, False):
+            @pl.when(arrives(up, h))
+            def _():
+                source = z - h - 1 if up else z + h + 1
+                index = (0 if up else 1, kind * MB + mb, h)
+                ref = item_ref(kind, source, mb)
+                pltpu.make_async_remote_copy(
+                    src_ref=ref, dst_ref=ref, send_sem=send_sem.at[index], recv_sem=recv_sem.at[index],
+                    device_id=(dp, z - 1 if up else z + 1), device_id_type=MESH,
+                ).wait_recv()
+            if h + 1 < NZ - 1:
+                @pl.when(leaves(up, h + 1))
+                def _():
+                    hop(up, kind, mb, h + 1).start()
+
+    def weights(n, slot):
+        e = lax.rem(n, 16) // 4
+        f = lax.rem(n, 4)
+        cols = pl.ds(pl.multiple_of(f * CHUNK, CHUNK), CHUNK)
+        return (
+            pltpu.make_async_copy(w_in.at[e, :, cols], wb1.at[slot], w_sem.at[0, slot]),
+            pltpu.make_async_copy(w_back.at[e, cols, :], wb2.at[slot], w_sem.at[1, slot]),
+        )
+
+    own = [pltpu.make_async_copy(dout.at[mb], gd.at[z, mb], d_sem.at[mb]) for mb in range(MB)]
+    for copy in own:
+        copy.start()
+    barrier = pltpu.get_barrier_semaphore()
+    for up in (True, False):
+        @pl.when(leaves(up, 0))
+        def _():
+            pl.semaphore_signal(
+                barrier, inc=1, device_id=(dp, z + 1 if up else z - 1), device_id_type=MESH
+            )
+    pl.semaphore_wait(
+        barrier, (z >= 1).astype(jnp.int32) + (z + 1 < NZ).astype(jnp.int32)
+    )
+    for copy in own:
+        copy.wait()
+    start(0, 0, 0)
+    for copy in weights(0, 0):
+        copy.start()
+
+    qkv_s[T:KEYS, :] = jnp.zeros((KEYS - T, 3 * D), BF16)
+    bb_o[...] = jnp.zeros_like(bb_o)
+    bi_o[...] = jnp.zeros_like(bi_o)
+
+    def forward(mb, carry):
+        x = tok[mb].astype(F32)
+        normed = (normal(x)[0] * g1[...] + s1[...]).astype(BF16)
+        for c in range(3):
+            cols = slice(c * D, (c + 1) * D)
+            qkv_s[0:T, cols] = (dot(normed, wqkv[:, cols]) + bqkv[:, cols]).astype(BF16)
+
+        def heads(p, carry):
+            at = [pl.ds(pl.multiple_of(c * D + p * 128, 128), 128) for c in range(3)]
+            q, k, v = qkv_s[0:T, at[0]], qkv_s[:, at[1]], qkv_s[:, at[2]]
+            mixed = jnp.zeros((T, 128), F32)
+            for which in (0, 1):
+                mask = half_mask(which)
+                probs = attention_probs(dot(q, k * mask, NT) * HEAD_DIM ** (-0.5))
+                mixed = mixed + dot(probs.astype(BF16), v * mask)
+            mixed_s[:, at[0]] = mixed.astype(BF16)
+            return carry
+
+        lax.fori_loop(0, PAIRS, heads, 0)
+        qkv_o[mb] = qkv_s[0:T, :]
+        mixed_o[mb] = mixed_s[...]
+        resid = x + dot(mixed_s[...], wout[...]) + bout[...]
+        resid_o[mb] = resid
+        inner = (normal(resid)[0] * g2[...] + s2[...]).astype(BF16)
+        gi[z, mb] = inner
+        table, real = route_table(rt, mb)
+        probs = route_softmax(dot(wrt[...], inner, NT), real)
+        rp_o[mb] = probs
+        earlier = (
+            lax.broadcasted_iota(jnp.int32, (T, T), 0) < lax.broadcasted_iota(jnp.int32, (T, T), 1)
+        ).astype(F32).astype(BF16)
+        before = dot(table.astype(F32).astype(BF16), earlier)
+        slots = jnp.where(table, before, -1.0)
+        gates = jnp.where(table, probs, 0.0)
+        for p in range(NZ):
+            sg[z, mb, 0, p] = slots[8 * p : 8 * p + 8, :]
+            sg[z, mb, 1, p] = gates[8 * p : 8 * p + 8, :]
+
+        @pl.when(mb == 0)
+        def _():
+            start(1, 0, 0)
+            start(2, 0, 0)
+
+        return carry
+
+    lax.fori_loop(0, MB, forward, 0)
+    for h in range(NZ - 1):
+        for kind in range(3):
+            pass_on(kind, 0, h)
+    for kind in range(3):
+        start(kind, 1, 0)
+
+    def micro(mb, carry):
+        @pl.when(mb == 1)
+        def _():
+            for kind in range(3):
+                pass_on(kind, 1, 2)
+
+        def spread(src, carry):
+            pick = pick_matrix(sg[src, mb, 0, z])
+            gate = sg[src, mb, 1, z]
+            low = pick.astype(BF16)
+            rows_x = dot(low, gi[src, mb]).astype(BF16)
+            rows_c = dot(low, gd[src, mb])
+            at = pl.ds(pl.multiple_of(mb * ROWS + src * CAP_ROWS, 16), CAP_ROWS)
+            here = pl.ds(pl.multiple_of(src * CAP_ROWS, 16), CAP_ROWS)
+            for e in range(LOCAL):
+                part = slice(e * CAP_ROWS, (e + 1) * CAP_ROWS)
+                gate_rows = jnp.sum(pick[part] * gate[e : e + 1, :], axis=1, keepdims=True)
+                grad = (rows_c[part] * gate_rows).astype(BF16)
+                xs[e, at, :] = rows_x[part]
+                gs[e, at, :] = grad
+                cs[e, here, :] = rows_c[part].astype(BF16)
+                rgs[e, here, :] = jnp.broadcast_to(gate_rows, (CAP_ROWS, 128))
+                bb_o[e] += jnp.sum(grad.astype(F32), axis=0, keepdims=True)
+            return carry
+
+        lax.fori_loop(0, NZ, spread, 0)
+        rows = pl.ds(pl.multiple_of(mb * ROWS, 16), ROWS)
+
+        def expert(e, carry):
+            acc_o[...] = jnp.zeros_like(acc_o)
+            acc_g[...] = jnp.zeros_like(acc_g)
+
+            def step(f, carry):
+                n = mb * 16 + e * 4 + f
+                slot = lax.rem(n, 2)
+
+                @pl.when(n + 1 < 16 * MB)
+                def _():
+                    for copy in weights(n + 1, 1 - slot):
+                        copy.start()
+
+                for copy in weights(n, slot):
+                    copy.wait()
+                hid = dot(xs[e, rows, :], wb1[slot]) + b_in[e * 4 + f]
+                square = hid * hid
+                bend = jnp.tanh(hid * (0.7978845608 + (0.7978845608 * 0.044715) * square))
+                half = 0.5 + 0.5 * bend
+                act = (hid * half).astype(BF16)
+                slope = half + (0.5 * hid) * (1.0 - bend * bend) * (
+                    0.7978845608 + (3 * 0.7978845608 * 0.044715) * square
+                )
+
+                @pl.when(n >= 2)
+                def _():
+                    for copy in stores(n - 2, slot):
+                        copy.wait()
+
+                act_st[slot] = act
+                acc_o[...] += dot(act, wb2[slot])
+                grad = (dot(gs[e, rows, :], wb2[slot], NT) * slope).astype(BF16)
+                gh_st[slot] = grad
+                acc_g[...] += dot(grad, wb1[slot], NT)
+                bi_o[e * 4 + f] += jnp.sum(grad.astype(F32), axis=0, keepdims=True)
+                for copy in stores(n, slot):
+                    copy.start()
+                return carry
+
+            lax.fori_loop(0, 4, step, 0)
+            out = (acc_o[...] + b_back[e]).astype(BF16).astype(F32)
+            gg = jnp.sum(out * cs[e].astype(F32), axis=1, keepdims=True)
+            scaled = (out * rgs[e][:, 0:1]).astype(BF16)
+            back = acc_g[...].astype(BF16)
+            at = pl.ds(pl.multiple_of(e * CAP_ROWS, 16), CAP_ROWS)
+            for src in range(NZ):
+                part = slice(src * CAP_ROWS, (src + 1) * CAP_ROWS)
+                os_[src, at, :] = scaled[part]
+                grs[src, at, :] = back[part]
+                ggs[src, at, :] = jnp.broadcast_to(gg[part], (CAP_ROWS, 128))
+
+            @pl.when(jnp.logical_and(mb == 0, e == 1))
+            def _():
+                for kind in range(3):
+                    pass_on(kind, 1, 0)
+
+            @pl.when(jnp.logical_and(mb == 0, e == 3))
+            def _():
+                for kind in range(3):
+                    pass_on(kind, 1, 1)
+
+            return carry
+
+        def stores(n, slot):
+            m = n // 16
+            e = lax.rem(n, 16) // 4
+            f = lax.rem(n, 4)
+            at = (e, pl.ds(pl.multiple_of(m * ROWS, 16), ROWS), pl.ds(pl.multiple_of(f * CHUNK, CHUNK), CHUNK))
+            return (
+                pltpu.make_async_copy(act_st.at[slot], act_o.at[at], st_sem.at[0, slot]),
+                pltpu.make_async_copy(gh_st.at[slot], gh_o.at[at], st_sem.at[1, slot]),
+            )
+
+        lax.fori_loop(0, LOCAL, expert, 0)
+
+        @pl.when(mb == 1)
+        def _():
+            for slot in (0, 1):
+                for copy in stores(16 * MB - 2 + slot, slot):
+                    copy.wait()
+
+        def gather(src, carry):
+            pick = pick_matrix(sg[src, mb, 0, z])
+            low = pick.astype(BF16)
+            n = mb * NZ + src
+            slot = lax.rem(n, 2)
+
+            @pl.when(n >= 2)
+            def _():
+                for copy in parts(n - 2, slot):
+                    copy.wait()
+
+            pb_s[slot] = dot(low, os_[src], TN).astype(BF16)
+            pg_s[slot] = dot(low, grs[src], TN).astype(BF16)
+            for copy in parts(n, slot):
+                copy.start()
+            for e in range(LOCAL):
+                part = slice(e * CAP_ROWS, (e + 1) * CAP_ROWS)
+                gg_o[src, mb, e : e + 1, :] = jnp.sum(
+                    pick[part] * ggs[src, part, 0:1], axis=0, keepdims=True
+                )
+            return carry
+
+        def parts(n, slot):
+            src, m = lax.rem(n, NZ), n // NZ
+            return (
+                pltpu.make_async_copy(pb_s.at[slot], pb_o.at[src, m], p_sem.at[0, slot]),
+                pltpu.make_async_copy(pg_s.at[slot], pg_o.at[src, m], p_sem.at[1, slot]),
+            )
+
+        lax.fori_loop(0, NZ, gather, 0)
+
+        @pl.when(mb == 1)
+        def _():
+            for slot in (0, 1):
+                for copy in parts(NZ * MB - 2 + slot, slot):
+                    copy.wait()
+
+        return carry
+
+    gg_o[...] = jnp.zeros_like(gg_o)
+    lax.fori_loop(0, MB, micro, 0)
+    last = (
+        pltpu.make_async_copy(xs, x_o, x_sem.at[0]),
+        pltpu.make_async_copy(gs, gp_o, x_sem.at[1]),
+    )
+    for copy in last:
+        copy.start()
+    for copy in last:
+        copy.wait()
+    for mb in range(MB):
+        for kind in range(3):
+            for h in range(NZ - 1):
+                for up in (True, False):
+                    @pl.when(leaves(up, h))
+                    def _():
+                        hop(up, kind, mb, h).wait_send()
+
+
+def dispatch_call(tok, rt, g1, s1, wqkv, bqkv, wout, bout, g2, s2, wrt, b_in, b_back, dout, w_in, w_back):
+    vm = pl.BlockSpec(memory_space=pltpu.VMEM)
+    hb = pl.BlockSpec(memory_space=pl.ANY)
+    S = jax.ShapeDtypeStruct
+    D = 768
+    rows = MB * ROWS
+    outs = [
+        (S((MB, T, 3 * D), BF16), vm),
+        (S((MB, T, D), BF16), vm),
+        (S((MB, T, D), F32), vm),
+        (S((MB, 32, T), F32), vm),
+        (S((NZ, MB, 8, T), F32), vm),
+        (S((LOCAL, 1, D), F32), vm),
+        (S((LOCAL * 4, 1, CHUNK), F32), vm),
+        (S((LOCAL, rows, D), BF16), hb),
+        (S((LOCAL, rows, D), BF16), hb),
+        (S((LOCAL, rows, 4 * CHUNK), BF16), hb),
+        (S((LOCAL, rows, 4 * CHUNK), BF16), hb),
+        (S((NZ, MB, T, D), BF16), hb),
+        (S((NZ, MB, T, D), BF16), hb),
+    ]
+    V = pltpu.VMEM
+    DMA = pltpu.SemaphoreType.DMA
+    return pl.pallas_call(
+        dispatch_kernel,
+        out_shape=[o[0] for o in outs],
+        in_specs=[vm] * 13 + [hb] * 3,
+        out_specs=[o[1] for o in outs],
+        scratch_shapes=[
+            V((NZ, MB, T, D), BF16), V((NZ, MB, T, D), BF16), V((NZ, MB, 2, NZ, 8, T), F32),
+            V((KEYS, 3 * D), BF16), V((T, D), BF16), V((8, 128), F32),
+            V((LOCAL, rows, D), BF16), V((LOCAL, rows, D), BF16), V((LOCAL, ROWS, D), BF16),
+            V((LOCAL, ROWS, 128), F32), V((NZ, ROWS, 128), F32),
+            V((2, D, CHUNK), BF16), V((2, CHUNK, D), BF16),
+            V((2, ROWS, CHUNK), BF16), V((2, ROWS, CHUNK), BF16),
+            V((ROWS, D), F32), V((ROWS, D), F32),
+            V((NZ, ROWS, D), BF16), V((NZ, ROWS, D), BF16),
+            V((2, T, D), BF16), V((2, T, D), BF16),
+            DMA((2, 3 * MB, NZ - 1)), DMA((2, 3 * MB, NZ - 1)), DMA((MB,)), DMA((2, 2)), DMA((2, 2)),
+            DMA((2,)), DMA((2, 2)),
+        ],
+        compiler_params=pltpu.CompilerParams(
+            collective_id=1, has_side_effects=True, vmem_limit_bytes=58 << 20
+        ),
+        name="dispatch",
+    )(tok, rt, g1, s1, wqkv, bqkv, wout, bout, g2, s2, wrt, b_in, b_back, dout, w_in, w_back)
+
+def fast_body(
+    tokens, routes, gain_one, shift_one, w_qkv, qv_bias, w_out, out_bias, gain_two, shift_two,
+    w_route, w_in, b_in, w_back, b_back, d_out,
+):
+    def windows(a):
+        return jnp.pad(a.reshape(MB, SEQ, a.shape[1]), ((0, 0), (0, T - SEQ), (0, 0)))
+
+    tok, dout = windows(tokens), windows(d_out)
+    rt = jnp.pad(
+        jnp.transpose(routes.reshape(MB, SEQ, TOP), (0, 2, 1)),
+        ((0, 0), (0, 8 - TOP), (0, T - SEQ)), constant_values=-1,
+    )
+    row = lambda a: a.reshape(1, -1)
+    bqkv = jnp.concatenate([qv_bias[0], jnp.zeros_like(qv_bias[0]), qv_bias[1]])
+    wrt = jnp.pad(w_route.T.reshape(NZ, LOCAL, D), ((0, 0), (0, 8 - LOCAL), (0, 0))).reshape(32, D)
+    (qkv, mixed, resid, rp, gg, bb, bi, xr, gp, act, gh, pb, pg) = dispatch_call(
+        tok, rt, row(gain_one), row(shift_one), w_qkv, row(bqkv), w_out, row(out_bias),
+        row(gain_two), row(shift_two), wrt, b_in.reshape(16, 1, CHUNK), b_back.reshape(LOCAL, 1, D),
+        dout, w_in, w_back,
+    )
+    scale = HEAD_DIM ** (-0.5)
+    pb = lax.psum_scatter(pb.astype(F32), "expert", scatter_dimension=0, tiled=False)
+    pg = lax.psum_scatter(pg.astype(F32), "expert", scatter_dimension=0, tiled=False)
+    gg = lax.all_to_all(gg, "expert", 0, 0, tiled=True)
+    grad_gate = jnp.transpose(gg, (1, 0, 2, 3)).reshape(MB, 32, T)
+    block = (resid + pb).astype(BF16)[:, :SEQ].reshape(MB * SEQ, D)
+    table = jnp.stack([route_table(rt, mb)[0] for mb in range(MB)])
+    g = jnp.where(table, grad_gate, 0.0)
+    gl = rp * (g - jnp.sum(rp * g, axis=1, keepdims=True))
+    cot = dout.astype(F32)
+    n2, r2 = normal(resid)
+    inner = (n2 * gain_two + shift_two).astype(BF16)
+    acc_route = jnp.einsum("bet,btd->ed", gl, inner.astype(F32), precision=HIGH)
+    gi = pg + jnp.einsum("bet,ed->btd", gl, wrt.astype(F32), precision=HIGH)
+    acc_gain_two = jnp.sum(gi * n2, axis=(0, 1))
+    acc_shift_two = jnp.sum(gi, axis=(0, 1))
+    u = gi * gain_two
+    grad_resid = cot + r2 * (
+        u - jnp.mean(u, -1, keepdims=True) - n2 * jnp.mean(u * n2, -1, keepdims=True)
+    )
+    ga = grad_resid.astype(BF16)
+    acc_out = jnp.einsum("btd,bte->de", mixed, ga, preferred_element_type=F32)
+    acc_out_bias = jnp.sum(ga.astype(F32), axis=(0, 1))
+    gm = jnp.einsum("bte,de->btd", ga, w_out, preferred_element_type=F32).astype(BF16)
+    gm = gm[:, :SEQ].reshape(MB, SEQ, HEADS, HEAD_DIM)
+    query, keys, values = [
+        qkv[:, :SEQ, i * D : (i + 1) * D].reshape(MB, SEQ, HEADS, HEAD_DIM) for i in range(3)
+    ]
+    again = jnp.einsum("ishd,ithd->ihst", query, keys, preferred_element_type=F32) * scale
+    probs = jax.nn.softmax(again, axis=-1)
+    gpa = jnp.einsum("ishd,ithd->ihst", gm, values, preferred_element_type=F32)
+    gsc = (probs * (gpa - jnp.sum(probs * gpa, -1, keepdims=True))).astype(BF16)
+    gq = jnp.einsum("ihst,ithd->ishd", gsc, keys, preferred_element_type=F32) * scale
+    gk = jnp.einsum("ihst,ishd->ithd", gsc, query, preferred_element_type=F32) * scale
+    gv = jnp.einsum("ihst,ishd->ithd", probs.astype(BF16), gm, preferred_element_type=F32)
+    rows = MB * SEQ
+    gqkv = jnp.concatenate([a.reshape(rows, D) for a in (gq, gk, gv)], axis=1).astype(BF16)
+    x = tokens.astype(F32)
+    n1, r1 = normal(x)
+    normed = (n1 * gain_one + shift_one).astype(BF16)
+    acc_qkv = jnp.einsum("rd,re->de", normed, gqkv, preferred_element_type=F32)
+    cs = jnp.sum(gqkv.astype(F32), axis=0)
+    acc_qv = jnp.stack([cs[:D], cs[2 * D :]])
+    gn = jnp.einsum("re,de->rd", gqkv, w_qkv, preferred_element_type=F32)
+    acc_gain_one = jnp.sum(gn * n1, axis=0)
+    acc_shift_one = jnp.sum(gn, axis=0)
+    w = gn * gain_one
+    input_grad = grad_resid[:, :SEQ].reshape(rows, D) + r1 * (
+        w - jnp.mean(w, -1, keepdims=True) - n1 * jnp.mean(w * n1, -1, keepdims=True)
+    )
+    wb = jnp.einsum("erf,erd->efd", act, gp, preferred_element_type=F32).astype(BF16)
+    wi = jnp.einsum("erd,erf->edf", xr, gh, preferred_element_type=F32).astype(BF16)
+    scat = lambda a: lax.psum_scatter(a, "dp", scatter_dimension=1, tiled=True).astype(F32)
+    shared = lax.psum(
+        (acc_gain_one, acc_shift_one, acc_qkv, acc_qv, acc_out, acc_out_bias, acc_gain_two,
+         acc_shift_two, acc_route.reshape(NZ, 8, D)[:, :LOCAL].reshape(16, D).T),
+        ("dp", "expert"),
+    )
+    return (block, input_grad, *shared, scat(wi), scat(bi.reshape(LOCAL, 4 * CHUNK)), scat(wb), scat(bb.reshape(LOCAL, D)))
+
+
 def solution(mesh):
+    fast = mesh.shape["dp"] == 8 and mesh.shape["expert"] == NZ
     return jax.shard_map(
-        body,
+        fast_body if fast else general_body,
         mesh=mesh,
         in_specs=(
             P(("dp", "expert"), None),

time: 941 us -> 1050 us (1.12)
  waiting for transfers between devices: 355 us -> 715 us
  matrix products: 260 us -> 66.8 us
  Pallas kernels: 0 us -> 137 us
  local copies, waits for them, and re-layouts: 171 us -> 73.8 us
  other arithmetic: 86.2 us -> 31.1 us
  starting transfers between devices: 37.9 us -> 4.55 us
    reduce_scatter x2 -> x4, waiting for transfers between devices: 0.01 us -> 363 us  [the longest x2 248 us: fast_body(): lax.psum_scatter(a, 'dp', scatter_dimension=1, tiled=True).astype(F32)]
    dot_general x46 -> x12, matrix products: 260 us -> 62.1 us  [the longest x1 17 us: fast_body(): jnp.einsum('erd,erf->edf', xr, gh, preferred_element_type=F32).astype(BF16)]
    pallas_call x0 -> x1, Pallas kernels: none -> 137 us  [dispatch_call(): pl.pallas_call(dispatch_kernel, out_shape=[o[0] for o in outs], in_specs=...]
    all_to_all x8 -> x1, waiting for transfers between devices: 56.9 us -> 0.01 us  [fast_body(): gg = lax.all_to_all(gg, 'expert', 0, 0, tiled=True)]
    all_to_all x8 -> x1, starting transfers between devices: 37.5 us -> 4.09 us  [fast_body(): gg = lax.all_to_all(gg, 'expert', 0, 0, tiled=True)]
    psum x2, waiting for transfers between devices: 298 us -> 327 us  [fast_body(): lax.psum((acc_gain_one, acc_shift_one, acc_qkv, acc_qv, acc_out, acc_out_...]
    reduce_sum x23 -> x7, other arithmetic: 32.7 us -> 5.29 us  [the longest x1 1.91 us: fast_body(): acc_out_bias = jnp.sum(ga.astype(F32), axis=(0, 1))]
    unnamed x8 -> x10, waiting for transfers between devices: 0.12 us -> 25.7 us
  transfers between devices with their start and end apart: 14 -> 9, of which waited for: 8 -> 7; matrix products, arithmetic and copies ran while one was open for 46% -> 12% of each run, Pallas kernels for 0% -> 0%
where the time goes in v1:
time: 1050 us; the launch traced here: 1040 us
  waiting for transfers between devices  715 us (68%)
  Pallas kernels  137 us (13%)
  local copies, waits for them, and re-layouts  73.8 us (7%)
  matrix products  66.8 us (6%)
  other arithmetic  31.1 us (3%)
  between operations  15 us (1%)
    psum x2, waiting for transfers between devices, fast_body(): lax.psum((acc_gain_one, acc_shift_one, acc_qkv, acc_qv, acc_out, acc_out_...  327 us
    reduce_scatter x2, waiting for transfers between devices, fast_body(): lax.psum_scatter(a, 'dp', scatter_dimension=1, tiled=True).astype(F32)  248 us
    pallas_call x1, Pallas kernels, dispatch_call(): pl.pallas_call(dispatch_kernel, out_shape=[o[0] for o in outs], in_specs=...  137 us
    reduce_scatter x1, waiting for transfers between devices, fast_body(): lax.psum_scatter(pb.astype(F32), 'expert', scatter_dimension=0, tiled=False)  91.1 us
    unnamed x95, local copies, waits for them, and re-layouts  27.5 us
    unnamed x10, waiting for transfers between devices  25.7 us
    reduce_scatter x1, waiting for transfers between devices, fast_body(): lax.psum_scatter(pg.astype(F32), 'expert', scatter_dimension=0, tiled=False)  23.6 us
  transfers between devices with their start and end apart: 9, of which 7 were waited for; matrix products, arithmetic and copies ran while one was open for 12% of the time, Pallas kernels for 0%

profile of v1, /device:TPU:0, one launch (start us, length us, event | category | flops | bytes accessed | tf_op | source)
XLA Modules:
  0.0 1044.1 jit_solution(13567882665586926711)
XLA Ops:
  7.2 1.3 reshape.465.bout
  8.6 1.3 reshape.463.s1
  9.8 1.3 reshape.467.s2
  11.1 1.3 reshape.462.g1
  12.4 1.3 reshape.466.g2
  15.8 1.3 reshape.471.b_back
  18.5 1.5 reshape.470.b_in
  20.0 1.2 reshape.472
  21.4 0.9 pad.15.tok
  22.3 0.9 pad.18.dout
  23.7 137.4 %dispatch.1 = (bf16[2,208,2304]{2,1,0:T(8,128)(2,1)}, bf16[2,208,768]{2,1,0:T(8,128)(2,1)}, f32[2,208,768]{2,1,0:T(8,128)}, f32[2,32,208]{2,1,0:T(8,128)}, f32[4...) custom-call(bf16[2,208,768]{2,1,0:T(8,128)(2,1)} %pad.15.tok, ...), custom_call_target="tpu_custom_call" | custom-call | tf_op jit(solution)/shard_map/dispatch/pallas_call | solution.py:671
  161.1 4.5 convert_element_type.62
  166.3 1.0 copy.80
  167.6 1.7 copy.76
  169.8 3.1 convert_element_type.59
  173.0 1.6 copy-done.37
  174.6 17.0 %convolution_convert_fusion.1 = bf16[4,768,3072]{2,1,0:T(8,128)(2,1)} fusion(bf16[4,384,768]{2,1,0:T(8,128)(2,1)S(1)} %copy-done.37, bf16[4,384,3072]{2,1,0:T(8,128)(2,1)} %get-tuple-element.36), kind=kOutput, calls=%fused_computation.2 | convolution fusion | flops 7257194496 | bytes 30670848 | tf_op jit(solution)/shard_map/erd,erf->edf/dot_general | solution.py:766
  191.8 1.4 copy-done.36
  193.2 16.2 %convolution_convert_fusion = bf16[4,3072,768]{2,1,0:T(8,128)(2,1)} fusion(bf16[4,384,3072]{2,1,0:T(8,128)(2,1)} %get-tuple-element.38, bf16[4,384,768]{2,1,0:T(8,128)(2,1)S(1)} %copy-done.36), kind=kOutput, calls=%fused_computation.1 | convolution fusion | flops 7257194496 | bytes 30670848 | tf_op jit(solution)/shard_map/erf,erd->efd/dot_general | solution.py:765
  209.5 4.1 all-to-all-start
  214.3 2.6 fusion.54
  217.3 1.6 copy.59
  218.9 0.9 pad_slice_fusion.3
  224.3 4.7 fusion.56
  229.8 2.3 copy.62
  232.1 0.9 multiply_reduce_fusion.7
  233.0 1.4 convolution_bitcast_fusion.1
  235.1 23.6 %reduce-scatter.13.cloned.1.call-done = f32[1,2,208,768]{3,2,1,0:T(8,128)} async-done(((f32[4,2,208,768]{3,2,1,0:T(8,128)}), f32[1,2,208,768]{3,2,1,0:T(8,128)}) %reduce-scatter.13.cloned.1.call-update) | async-done | bytes 1277968 | tf_op jit(solution)/shard_map/reduce_scatter | solution.py:717
  258.7 3.2 multiply_reduce_fusion.2
  261.9 1.9 convert_reduce_fusion.2
  264.5 0.9 slice.78
  265.4 2.2 copy.61
  267.6 3.6 fusion.18
  271.2 1.7 copy.68
  272.9 3.4 reshape.482
  276.3 4.0 multiply_reduce_fusion
  280.6 1.0 multiply_convert_fusion
  283.1 1.7 copy.64
  284.8 3.2 reshape.480
  288.0 2.8 fusion.17
  290.9 1.7 copy.66
  292.6 3.4 reshape.481
  296.0 1.3 constant_dynamic-update-slice_fusion.2
  298.8 5.3 fusion.36
  304.1 3.9 fusion.25
  308.1 3.3 convolution_bitcast_fusion
  311.4 1.5 copy.79
  312.9 25.6 %reduce-scatter.19.cloned.1.call-done = f32[384,4]{1,0:T(8,128)} async-done(((f32[3072,4]{1,0:T(8,128)}), f32[384,4]{1,0:T(8,128)}) %reduce-scatter.19.cloned.1.call-update) | async-done | bytes 6160
  338.5 1.6 copy.77
  340.1 1.1 slice.62
  341.2 91.1 %reduce-scatter.11.cloned.1.call-done = f32[1,2,208,768]{3,2,1,0:T(8,128)} async-done(((f32[4,2,208,768]{3,2,1,0:T(8,128)}), f32[1,2,208,768]{3,2,1,0:T(8,128)}) %reduce-scatter.11.cloned.1.call-update) | async-done | bytes 1277968 | tf_op jit(solution)/shard_map/reduce_scatter | solution.py:716
  432.3 2.4 fusion.29
  434.7 2.0 reshape.473
  436.8 2.8 fusion.24
  439.6 122.8 %reduce-scatter.15.cloned.1.call-done = bf16[4,96,3072]{2,1,0:T(8,128)(2,1)} async-done(((bf16[4,768,3072]{2,1,0:T(8,128)(2,1)}), bf16[4,96,3072]{2,1,0:T(8,128)(2,1)}) %reduce-scatter.15.cloned.1.call-update) | async-done | bytes 2359312 | tf_op jit(solution)/shard_map/reduce_scatter | solution.py:767
  562.4 4.4 convert_element_type.73
  566.8 125.2 %reduce-scatter.17.cloned.1.call-done = bf16[4,384,768]{2,1,0:T(8,128)(2,1)} async-done(((bf16[4,3072,768]{2,1,0:T(8,128)(2,1)}), bf16[4,384,768]{2,1,0:T(8,128)(2,1)}) %reduce-scatter.17.cloned.1.call-update) | async-done | bytes 2359312 | tf_op jit(solution)/shard_map/reduce_scatter | solution.py:767
  692.0 4.3 convert_element_type.75
  696.3 125.9 %all-reduce.9.cloned.1.call-done = (f32[768]{0:T(1024)}, f32[768]{0:T(1024)}, f32[2,768]{1,0:T(2,128)}, f32[768]{0:T(1024)}, f32[768]{0:T(1024)}, /*index=5*/f32[768]{0:T(1024)}, f32[768,16]{0,1:T(8,128)}) async-done(((f32[768]{0:T(1024)}, f32[768]{0:T(1024)}, f32[2,768]{1,0:T(2,128)}, f32[768]{0:T(1024)}, f32[768]{0:T(1024)}, /*index=5*/f32[768]{0:T(1024)}, f32[768,16]{0,1:T(8,128)}), (f32[768]{0:T(1024)}, ...) | async-done | bytes 70672 | tf_op jit(solution)/shard_map/psum | solution.py:768
  822.2 201.1 %all-reduce.11.cloned.1.call-done = (f32[768,2304]{1,0:T(8,128)}, f32[768,768]{1,0:T(8,128)}) async-done(((f32[768,2304]{1,0:T(8,128)}, f32[768,768]{1,0:T(8,128)}), (f32[768,2304]{1,0:T(8,128)}, f32[768,768]{1,0:T(8,128)})) %all-reduce.11.cloned.1.call-update) | async-done | bytes 9437200 | tf_op jit(solution)/shard_map/psum | solution.py:768
  1023.3 1.3 copy.111
  1024.6 1.3 copy.112
  1025.8 6.6 copy.113
  1033.0 1.4 copy.115
  (143 shorter events, 20.2 us)
Async XLA Ops:
  7.2 14.0 %copy-start.2 = (bf16[394,768]{1,0:T(8,128)(2,1)S(1)}, bf16[394,768]{1,0:T(8,128)(2,1)}, u32[]{:S(2)}) copy-start(bf16[394,768]{1,0:T(8,128)(2,1)} %param.16) | copy-start | bytes 1815556
  7.2 251.4 %reduce-scatter.13.cloned.1.call-start = ((), (), s32[]{:S(2)}) async-start(), calls=%async_computation.8 | async-start | bytes 6389760 | tf_op jit(solution)/shard_map/reduce_scatter | solution.py:717
  14.4 8.7 copy-start.23
  21.2 1.9 copy-start.3
  165.6 0.7 copy-start.29
  165.6 1.8 copy-start.22
  165.7 145.8 %reduce-scatter.21.cloned.1.call-start = ((), (), s32[]{:S(2)}) async-start(), calls=%async_computation.12 | async-start | bytes 442368
  167.3 171.1 %reduce-scatter.19.cloned.1.call-start = ((), (), s32[]{:S(2)}) async-start(), calls=%async_computation.11 | async-start | bytes 1769472
  167.6 2.3 copy-start.13
  169.2 263.0 %reduce-scatter.11.cloned.1.call-start = ((), (), s32[]{:S(2)}) async-start(), calls=%async_computation.7 | async-start | bytes 6389760 | tf_op jit(solution)/shard_map/reduce_scatter | solution.py:716
  172.9 1.7 copy-start.37
  173.0 389.4 %reduce-scatter.15.cloned.1.call-start = ((), (), s32[]{:S(2)}) async-start(), calls=%async_computation.9 | async-start | bytes 21233664 | tf_op jit(solution)/shard_map/reduce_scatter | solution.py:767
  191.6 1.7 copy-start.36
  191.6 500.4 %reduce-scatter.17.cloned.1.call-start = ((), (), s32[]{:S(2)}) async-start(), calls=%async_computation.10 | async-start | bytes 21233664 | tf_op jit(solution)/shard_map/reduce_scatter | solution.py:767
  209.5 4.1 copy-start
  209.5 22.6 %all-to-all-start = ((f32[4,2,8,208]{3,2,1,0:T(8,128)}), f32[4,2,8,208]{3,2,1,0:T(8,128)S(1)}, u32[]{:S(2)}, u32[]{:S(2)}) async-start(f32[4,2,8,208]{3,2,1,0:T(8,128)} %get-tuple-element.32), calls=%async_computation.2 | async-start | bytes 131072 | tf_op jit(solution)/shard_map/all_to_all | solution.py:718
  213.6 608.6 %all-reduce.9.cloned.1.call-start = ((), (), s32[]{:S(2)}) async-start(), calls=%async_computation.13 | async-start | bytes 151552 | tf_op jit(solution)/shard_map/psum | solution.py:768
  217.2 7.1 copy-start.10
  218.9 10.2 copy-start.11
  220.0 0.6 copy-start.26
  221.6 0.6 copy-start.19
  229.1 3.9 copy-start.15
  229.8 28.8 %copy-start.25 = (f32[2,208]{1,0:T(2,128)}, f32[2,208]{1,0:T(2,128)S(1)}, u32[]{:S(2)}) copy-start(f32[2,208]{1,0:T(2,128)S(1)} %add_rsqrt_fusion.1) | copy-start | bytes 4996
  229.8 28.8 %copy-start.16 = (pred[1,32,208]{2,1,0:T(32,128)(4,1)S(1)}, pred[1,32,208]{2,1,0:T(32,128)(4,1)}, u32[]{:S(2)}) copy-start(pred[1,32,208]{2,1,0:T(32,128)(4,1)} %get-tuple-element.71) | copy-start | bytes 19972
  229.8 28.8 %copy-start.17 = (pred[1,32,208]{2,1,0:T(32,128)(4,1)S(1)}, pred[1,32,208]{2,1,0:T(32,128)(4,1)}, u32[]{:S(2)}) copy-start(pred[1,32,208]{2,1,0:T(32,128)(4,1)} %get-tuple-element.72) | copy-start | bytes 19972
  229.8 28.8 %copy-start.18 = (f32[768]{0:T(1024)S(1)}, f32[768]{0:T(1024)}, u32[]{:S(2)}) copy-start(f32[768]{0:T(1024)} %param.24) | copy-start | bytes 9220
  229.8 28.8 %copy-start.20 = (f32[2,208]{1,0:T(2,128)S(1)}, f32[2,208]{1,0:T(2,128)}, u32[]{:S(2)}) copy-start(f32[2,208]{1,0:T(2,128)} %copy-done.19) | copy-start | bytes 4996
  258.7 3.2 copy-start.4
  261.8 1.9 copy-start.6
  264.5 3.1 copy-start.24
  276.3 4.1 slice-start
  276.3 4.3 slice-start.1
  280.6 1.1 copy-start.12
  281.7 1.4 copy-start.1
  296.0 1.4 copy-start.9
  296.0 1.6 copy-start.8
  297.7 1.1 copy-start.27
  297.7 1.1 copy-start.28
  297.7 1.1 copy-start.30
  297.7 1.1 copy-start.32
  298.8 5.3 copy-start.7
  308.0 715.3 %all-reduce.11.cloned.1.call-start = ((), (), s32[]{:S(2)}) async-start(), calls=%async_computation.14 | async-start | bytes 18874368 | tf_op jit(solution)/shard_map/psum | solution.py:768
  432.3 4.4 copy-start.5
  1025.8 6.6 copy-start.31
  1025.8 7.2 copy-start.14
  1033.0 1.4 copy-start.35
  1033.0 2.0 copy-start.34
  1033.0 2.6 copy-start.33
  1033.0 3.2 copy-start.21
Sparse Core Ops, SparseCore 0:
  165.8 92.7 reduce-scatter.12
  261.7 34.3 reduce-scatter.20
  299.9 38.4 reduce-scatter.18
  340.6 91.5 reduce-scatter.10
  435.7 126.6 reduce-scatter.14
  565.9 126.1 reduce-scatter.16
  699.6 122.5 all-reduce.8
  829.7 193.5 all-reduce.10

commit v2 on v1

--- a/solution.py
+++ b/solution.py
@@ -341,11 +341,11 @@
 
 
 def dispatch_kernel(
-    tok, rt, g1, s1, wqkv, bqkv, wout, bout, g2, s2, wrt, b_in, b_back, dout, w_in, w_back,
-    qkv_o, mixed_o, resid_o, rp_o, gg_o, bb_o, bi_o, x_o, gp_o, act_o, gh_o, pb_o, pg_o,
+    tok, rt, vec, wqkv, wout, wrt, b_in, b_back, dout, w_in, w_back,
+    qkv_o, mixed_o, resid_o, rp_o, gg_o, bb_o, bi_o, x_o, gp_o, act_o, gh_o, pb_o, pg_o, home_o,
     gi, gd, sg, qkv_s, mixed_s, inner_s, xs, gs, cs, rgs, ggs, wb1, wb2, act_st, gh_st, acc_o, acc_g,
     os_, grs, pb_s, pg_s,
-    send_sem, recv_sem, d_sem, w_sem, st_sem, x_sem, p_sem,
+    send_sem, recv_sem, d_sem, w_sem, st_sem, x_sem, p_sem, h_send, h_recv,
 ):
     dp = lax.axis_index("dp")
     z = lax.axis_index("expert")
@@ -407,15 +407,9 @@
     for copy in own:
         copy.start()
     barrier = pltpu.get_barrier_semaphore()
-    for up in (True, False):
-        @pl.when(leaves(up, 0))
-        def _():
-            pl.semaphore_signal(
-                barrier, inc=1, device_id=(dp, z + 1 if up else z - 1), device_id_type=MESH
-            )
-    pl.semaphore_wait(
-        barrier, (z >= 1).astype(jnp.int32) + (z + 1 < NZ).astype(jnp.int32)
-    )
+    for d in range(1, NZ):
+        pl.semaphore_signal(barrier, inc=1, device_id=(dp, lax.rem(z + d, NZ)), device_id_type=MESH)
+    pl.semaphore_wait(barrier, NZ - 1)
     for copy in own:
         copy.wait()
     start(0, 0, 0)
@@ -428,10 +422,14 @@
 
     def forward(mb, carry):
         x = tok[mb].astype(F32)
-        normed = (normal(x)[0] * g1[...] + s1[...]).astype(BF16)
+        normed = (normal(x)[0] * vec[0:1] + vec[1:2]).astype(BF16)
         for c in range(3):
             cols = slice(c * D, (c + 1) * D)
-            qkv_s[0:T, cols] = (dot(normed, wqkv[:, cols]) + bqkv[:, cols]).astype(BF16)
+            part = dot(normed, wqkv[:, cols])
+            if c != 1:
+                row = 5 if c == 0 else 6
+                part = part + vec[row : row + 1]
+            qkv_s[0:T, cols] = part.astype(BF16)
 
         def heads(p, carry):
             at = [pl.ds(pl.multiple_of(c * D + p * 128, 128), 128) for c in range(3)]
@@ -447,9 +445,9 @@
         lax.fori_loop(0, PAIRS, heads, 0)
         qkv_o[mb] = qkv_s[0:T, :]
         mixed_o[mb] = mixed_s[...]
-        resid = x + dot(mixed_s[...], wout[...]) + bout[...]
+        resid = x + dot(mixed_s[...], wout[...]) + vec[4:5]
         resid_o[mb] = resid
-        inner = (normal(resid)[0] * g2[...] + s2[...]).astype(BF16)
+        inner = (normal(resid)[0] * vec[2:3] + vec[3:4]).astype(BF16)
         gi[z, mb] = inner
         table, real = route_table(rt, mb)
         probs = route_softmax(dot(wrt[...], inner, NT), real)
@@ -500,7 +498,7 @@
                 gs[e, at, :] = grad
                 cs[e, here, :] = rows_c[part].astype(BF16)
                 rgs[e, here, :] = jnp.broadcast_to(gate_rows, (CAP_ROWS, 128))
-                bb_o[e] += jnp.sum(grad.astype(F32), axis=0, keepdims=True)
+                bb_o[e : e + 1, :] += jnp.sum(grad.astype(F32), axis=0, keepdims=True)
             return carry
 
         lax.fori_loop(0, NZ, spread, 0)
@@ -513,6 +511,7 @@
             def step(f, carry):
                 n = mb * 16 + e * 4 + f
                 slot = lax.rem(n, 2)
+                cols = pl.ds(pl.multiple_of(f * CHUNK, CHUNK), CHUNK)
 
                 @pl.when(n + 1 < 16 * MB)
                 def _():
@@ -521,7 +520,7 @@
 
                 for copy in weights(n, slot):
                     copy.wait()
-                hid = dot(xs[e, rows, :], wb1[slot]) + b_in[e * 4 + f]
+                hid = dot(xs[e, rows, :], wb1[slot]) + b_in[pl.ds(e, 1), cols]
                 square = hid * hid
                 bend = jnp.tanh(hid * (0.7978845608 + (0.7978845608 * 0.044715) * square))
                 half = 0.5 + 0.5 * bend
@@ -540,13 +539,13 @@
                 grad = (dot(gs[e, rows, :], wb2[slot], NT) * slope).astype(BF16)
                 gh_st[slot] = grad
                 acc_g[...] += dot(grad, wb1[slot], NT)
-                bi_o[e * 4 + f] += jnp.sum(grad.astype(F32), axis=0, keepdims=True)
+                bi_o[pl.ds(e, 1), cols] += jnp.sum(grad.astype(F32), axis=0, keepdims=True)
                 for copy in stores(n, slot):
                     copy.start()
                 return carry
 
             lax.fori_loop(0, 4, step, 0)
-            out = (acc_o[...] + b_back[e]).astype(BF16).astype(F32)
+            out = (acc_o[...] + b_back[pl.ds(e, 1), :]).astype(BF16).astype(F32)
             gg = jnp.sum(out * cs[e].astype(F32), axis=1, keepdims=True)
             scaled = (out * rgs[e][:, 0:1]).astype(BF16)
             back = acc_g[...].astype(BF16)
@@ -587,44 +586,63 @@
                 for copy in stores(16 * MB - 2 + slot, slot):
                     copy.wait()
 
+        @pl.when(mb == 1)
+        def _():
+            for src in range(NZ):
+                kept(0, src).wait()
+            for d in range(1, NZ):
+                sent_home(d).wait_send()
+            own_home().wait()
+
         def gather(src, carry):
             pick = pick_matrix(sg[src, mb, 0, z])
             low = pick.astype(BF16)
-            n = mb * NZ + src
-            slot = lax.rem(n, 2)
-
-            @pl.when(n >= 2)
-            def _():
-                for copy in parts(n - 2, slot):
-                    copy.wait()
-
-            pb_s[slot] = dot(low, os_[src], TN).astype(BF16)
-            pg_s[slot] = dot(low, grs[src], TN).astype(BF16)
-            for copy in parts(n, slot):
-                copy.start()
+            pb_s[src] = dot(low, os_[src], TN).astype(BF16)
+            pg_s[src] = dot(low, grs[src], TN).astype(BF16)
+            kept(mb, src).start()
             for e in range(LOCAL):
                 part = slice(e * CAP_ROWS, (e + 1) * CAP_ROWS)
                 gg_o[src, mb, e : e + 1, :] = jnp.sum(
                     pick[part] * ggs[src, part, 0:1], axis=0, keepdims=True
                 )
+
+            @pl.when(mb == 1)
+            def _():
+                kept_grad(src).start()
+
             return carry
 
-        def parts(n, slot):
-            src, m = lax.rem(n, NZ), n // NZ
-            return (
-                pltpu.make_async_copy(pb_s.at[slot], pb_o.at[src, m], p_sem.at[0, slot]),
-                pltpu.make_async_copy(pg_s.at[slot], pg_o.at[src, m], p_sem.at[1, slot]),
-            )
-
         lax.fori_loop(0, NZ, gather, 0)
+
+        @pl.when(mb == 0)
+        def _():
+            for d in range(1, NZ):
+                sent_home(d).start()
+            own_home().start()
 
         @pl.when(mb == 1)
         def _():
-            for slot in (0, 1):
-                for copy in parts(NZ * MB - 2 + slot, slot):
-                    copy.wait()
+            for src in range(NZ):
+                kept(1, src).wait()
+                kept_grad(src).wait()
 
         return carry
+
+    def kept(mb, src):
+        return pltpu.make_async_copy(pb_s.at[src], pb_o.at[mb, src], p_sem.at[0, src])
+
+    def kept_grad(src):
+        return pltpu.make_async_copy(pg_s.at[src], pg_o.at[src], p_sem.at[1, src])
+
+    def sent_home(d):
+        target = lax.rem(z + d, NZ)
+        return pltpu.make_async_remote_copy(
+            src_ref=pg_s.at[target], dst_ref=home_o.at[z], send_sem=h_send.at[d - 1], recv_sem=h_recv.at[d - 1],
+            device_id=(dp, target), device_id_type=MESH,
+        )
+
+    def own_home():
+        return pltpu.make_async_copy(pg_s.at[z], home_o.at[z], d_sem.at[0])
 
     gg_o[...] = jnp.zeros_like(gg_o)
     lax.fori_loop(0, MB, micro, 0)
@@ -636,6 +654,12 @@
         copy.start()
     for copy in last:
         copy.wait()
+    for d in range(1, NZ):
+        source = lax.rem(z + NZ - d, NZ)
+        pltpu.make_async_remote_copy(
+            src_ref=home_o.at[source], dst_ref=home_o.at[source], send_sem=h_send.at[d - 1],
+            recv_sem=h_recv.at[d - 1], device_id=(dp, source), device_id_type=MESH,
+        ).wait_recv()
     for mb in range(MB):
         for kind in range(3):
             for h in range(NZ - 1):
@@ -645,11 +669,10 @@
                         hop(up, kind, mb, h).wait_send()
 
 
-def dispatch_call(tok, rt, g1, s1, wqkv, bqkv, wout, bout, g2, s2, wrt, b_in, b_back, dout, w_in, w_back):
+def dispatch_call(*operands):
     vm = pl.BlockSpec(memory_space=pltpu.VMEM)
     hb = pl.BlockSpec(memory_space=pl.ANY)
     S = jax.ShapeDtypeStruct
-    D = 768
     rows = MB * ROWS
     outs = [
         (S((MB, T, 3 * D), BF16), vm),
@@ -657,21 +680,22 @@
         (S((MB, T, D), F32), vm),
         (S((MB, 32, T), F32), vm),
         (S((NZ, MB, 8, T), F32), vm),
-        (S((LOCAL, 1, D), F32), vm),
-        (S((LOCAL * 4, 1, CHUNK), F32), vm),
+        (S((LOCAL, D), F32), vm),
+        (S((LOCAL, 4 * CHUNK), F32), vm),
         (S((LOCAL, rows, D), BF16), hb),
         (S((LOCAL, rows, D), BF16), hb),
         (S((LOCAL, rows, 4 * CHUNK), BF16), hb),
         (S((LOCAL, rows, 4 * CHUNK), BF16), hb),
-        (S((NZ, MB, T, D), BF16), hb),
-        (S((NZ, MB, T, D), BF16), hb),
+        (S((MB, NZ, T, D), BF16), hb),
+        (S((NZ, T, D), BF16), hb),
+        (S((NZ, T, D), BF16), hb),
     ]
     V = pltpu.VMEM
     DMA = pltpu.SemaphoreType.DMA
     return pl.pallas_call(
         dispatch_kernel,
         out_shape=[o[0] for o in outs],
-        in_specs=[vm] * 13 + [hb] * 3,
+        in_specs=[vm] * 8 + [hb] * 3,
         out_specs=[o[1] for o in outs],
         scratch_shapes=[
             V((NZ, MB, T, D), BF16), V((NZ, MB, T, D), BF16), V((NZ, MB, 2, NZ, 8, T), F32),
@@ -682,15 +706,583 @@
             V((2, ROWS, CHUNK), BF16), V((2, ROWS, CHUNK), BF16),
             V((ROWS, D), F32), V((ROWS, D), F32),
             V((NZ, ROWS, D), BF16), V((NZ, ROWS, D), BF16),
-            V((2, T, D), BF16), V((2, T, D), BF16),
+            V((NZ, T, D), BF16), V((NZ, T, D), BF16),
             DMA((2, 3 * MB, NZ - 1)), DMA((2, 3 * MB, NZ - 1)), DMA((MB,)), DMA((2, 2)), DMA((2, 2)),
-            DMA((2,)), DMA((2, 2)),
+            DMA((2,)), DMA((2, NZ)), DMA((NZ - 1,)), DMA((NZ - 1,)),
         ],
         compiler_params=pltpu.CompilerParams(
             collective_id=1, has_side_effects=True, vmem_limit_bytes=58 << 20
         ),
         name="dispatch",
-    )(tok, rt, g1, s1, wqkv, bqkv, wout, bout, g2, s2, wrt, b_in, b_back, dout, w_in, w_back)
+    )(*operands)
+
+
+HIDDEN = 4 * CHUNK
+PART = HIDDEN // 8
+BAND = D // 8
+SHARE = 400
+EXTRA = 128
+TOTAL = 8 * SHARE
+
+
+def add_low(a, b):
+    return (a.astype(F32) + b.astype(F32)).astype(BF16)
+
+
+def grads_kernel(
+    vec, rt, wrt, bb, bi, rp,
+    tok, dout, wqkv, wout, qkv, mixed, resid, gg, xr, gp, act, gh, pb, pg, pg0,
+    block_o, ig_o, ar_o, wi_o, wb_o, land_o,
+    core_b, core_i, st1_b, st1_i, st2_b, st2_i, ar_core, ar_z, ar_xy1, ar_xy2, ar_t,
+    ggr, quad,
+    c_send, c_recv, s1_send, s1_recv, s2_send, s2_recv, r_send, r_recv, g_send, g_recv,
+    ac_send, ac_recv, az_send, az_recv, ax_send, ax_recv, zz_send, zz_recv, cc_send, cc_recv,
+    l_sem, o_sem, f_sem,
+):
+    dp = lax.axis_index("dp")
+    z = lax.axis_index("expert")
+    y, x, c = dp // 4, lax.rem(dp // 2, 2), lax.rem(dp, 2)
+    yx = y * 2 + x
+    partner = (yx * 2 + (1 - c), z)
+    flips = ((y * 2 + (1 - x)), ((1 - y) * 2 + x))
+    across = (1 - y) * 2 + (1 - x)
+
+    def remote(src, dst, ssem, rsem, target):
+        return pltpu.make_async_remote_copy(
+            src_ref=src, dst_ref=dst, send_sem=ssem, recv_sem=rsem, device_id=target, device_id_type=MESH
+        )
+
+    barrier = pltpu.get_barrier_semaphore()
+    for target in [partner, (flips[0] * 2 + c, z), (flips[1] * 2 + c, z)]:
+        pl.semaphore_signal(barrier, inc=1, device_id=target, device_id_type=MESH)
+    for d in range(1, NZ):
+        pl.semaphore_signal(barrier, inc=1, device_id=(dp, lax.rem(z + d, NZ)), device_id_type=MESH)
+    pl.semaphore_wait(barrier, 6)
+
+    def gate_copy(d):
+        return remote(gg.at[lax.rem(z + d, NZ)], ggr.at[z], g_send.at[d - 1], g_recv.at[d - 1], (dp, lax.rem(z + d, NZ)))
+
+    for d in range(1, NZ):
+        gate_copy(d).start()
+    own_gate = pltpu.make_async_copy(gg.at[z], ggr.at[z], l_sem.at[0])
+    own_gate.start()
+
+    def home(item, d):
+        target = lax.rem(z + d, NZ)
+        part = pg.at[target] if item == 0 else pb.at[item - 1, target]
+        return remote(
+            part, land_o.at[item, z], r_send.at[item, d - 1], r_recv.at[item, d - 1], (dp, target)
+        )
+
+    def arrived(item):
+        for d in range(1, NZ):
+            source = lax.rem(z + NZ - d, NZ)
+            ref = land_o.at[item, source]
+            remote(ref, ref, r_send.at[item, d - 1], r_recv.at[item, d - 1], (dp, source)).wait_recv()
+
+    def load(sources):
+        copies = [pltpu.make_async_copy(ref, quad.at[i], l_sem.at[1 + i]) for i, ref in enumerate(sources)]
+        for copy in copies:
+            copy.start()
+        for copy in copies:
+            copy.wait()
+
+    def load_item(item):
+        arrived(item)
+        own = pg.at[z] if item == 0 else pb.at[item - 1, z]
+        load([own] + [land_o.at[item, lax.rem(z + d, NZ)] for d in range(1, NZ)])
+
+    def quad_sum():
+        return (quad[0].astype(F32) + quad[1].astype(F32)) + (quad[2].astype(F32) + quad[3].astype(F32))
+
+    def middle(arr, flow, mb, dest):
+        return jnp.logical_and(z > dest, z < NZ - 1) if flow == 0 else jnp.logical_and(z < dest, z > 0)
+
+    cores, lands1, lands2 = (core_b, core_i), (st1_b, st1_i), (st2_b, st2_i)
+
+    def core_copy(kind, e, src):
+        return remote(src, cores[kind].at[e], c_send.at[kind, e], c_recv.at[kind, e], partner)
+
+    def hop1(kind, e, slot):
+        block = flips[kind] if slot == 0 else across
+        return remote(
+            cores[kind].at[e, block], lands1[kind].at[e, slot],
+            s1_send.at[kind, e, slot], s1_recv.at[kind, e, slot], (flips[kind] * 2 + c, z),
+        )
+
+    def hop2(kind, e):
+        return remote(
+            cores[kind].at[e, flips[1 - kind]], lands2[kind].at[e],
+            s2_send.at[kind, e], s2_recv.at[kind, e], (flips[1 - kind] * 2 + c, z),
+        )
+
+    def send1(kind, e):
+        for slot in (1, 0):
+            hop1(kind, e, slot).start()
+
+    def turn(kind, e):
+        ref = cores[kind]
+        hop1(kind, e, 1).wait_recv()
+        ref[e, flips[1 - kind]] = add_low(ref[e, flips[1 - kind]], lands1[kind][e, 1])
+        hop2(kind, e).start()
+        hop1(kind, e, 0).wait_recv()
+        ref[e, yx] = add_low(ref[e, yx], lands1[kind][e, 0])
+
+    outs = (wb_o, wi_o)
+
+    def result(kind, e):
+        return pltpu.make_async_copy(lands2[kind].at[e], outs[kind].at[e], f_sem.at[kind, e])
+
+    def finish(kind, e):
+        hop2(kind, e).wait_recv()
+        lands2[kind][e] = add_low(lands2[kind][e], cores[kind][e, yx])
+        result(kind, e).start()
+
+    for item in range(3):
+        for d in range(1, NZ):
+            home(item, d).start()
+
+    def weight_grads(wg_b, wg_i, act_s, gh_s, x_s, gp_s, xp):
+        def fetch(e, which):
+            pairs = ((act, act_s), (gp, gp_s), (xr, x_s), (gh, gh_s))
+            return [
+                pltpu.make_async_copy(pairs[i][0].at[e], pairs[i][1], o_sem.at[i]) for i in which
+            ]
+
+        def pull(e, which):
+            for copy in fetch(e, which):
+                copy.start()
+
+        def ready(e, which):
+            for copy in fetch(e, which):
+                copy.wait()
+
+        pull(0, (0, 1, 2, 3))
+
+        def one(e, carry):
+            def back_block(k, side):
+                at = pl.ds(pl.multiple_of((2 * k + side) * PART, 128), PART)
+                return dot(act_s[:, at], gp_s[...], TN)
+
+            ready(e, (0, 1))
+
+            @pl.when(e > 0)
+            def _():
+                core_copy(0, e - 1, wg_b).wait_send()
+
+            def other_b(k, carry):
+                wg_b[k] = back_block(k, 1 - c).astype(BF16)
+                return carry
+
+            lax.fori_loop(0, 4, other_b, 0)
+            core_copy(0, e, wg_b).start()
+            ready(e, (2, 3))
+            for side in (0, 1):
+                for k in range(4):
+                    band = (2 * k + side) * BAND
+                    xp[side, :, k * BAND : (k + 1) * BAND] = x_s[:, band : band + BAND]
+
+            @pl.when(e > 0)
+            def _():
+                core_copy(1, e - 1, wg_i).wait_send()
+
+            def other_i(f, carry):
+                at = pl.ds(pl.multiple_of(f * CHUNK, 128), CHUNK)
+                grad = dot(xp[1 - c], gh_s[:, at], TN).astype(BF16)
+                for k in range(4):
+                    wg_i[k, :, at] = grad[k * BAND : (k + 1) * BAND]
+                return carry
+
+            lax.fori_loop(0, 4, other_i, 0)
+            core_copy(1, e, wg_i).start()
+            core_copy(0, e, wg_b).wait_recv()
+
+            def own_b(k, carry):
+                core_b[e, k] = (core_b[e, k].astype(F32) + back_block(k, c)).astype(BF16)
+                return carry
+
+            lax.fori_loop(0, 4, own_b, 0)
+
+            @pl.when(e < LOCAL - 1)
+            def _():
+                send1(0, e)
+                pull(e + 1, (0, 1))
+
+            core_copy(1, e, wg_i).wait_recv()
+
+            def own_i(f, carry):
+                at = pl.ds(pl.multiple_of(f * CHUNK, 128), CHUNK)
+                grad = dot(xp[c], gh_s[:, at], TN)
+                for k in range(4):
+                    core_i[e, k, :, at] = (
+                        core_i[e, k, :, at].astype(F32) + grad[k * BAND : (k + 1) * BAND]
+                    ).astype(BF16)
+                return carry
+
+            lax.fori_loop(0, 4, own_i, 0)
+
+            @pl.when(e < LOCAL - 1)
+            def _():
+                send1(1, e)
+                pull(e + 1, (2, 3))
+
+            return carry
+
+        lax.fori_loop(0, LOCAL, one, 0)
+        core_copy(0, LOCAL - 1, wg_b).wait_send()
+        core_copy(1, LOCAL - 1, wg_i).wait_send()
+
+    V = pltpu.VMEM
+    rows = MB * ROWS
+    pl.run_scoped(
+        weight_grads,
+        V((4, PART, D), BF16), V((4, BAND, HIDDEN), BF16), V((rows, HIDDEN), BF16), V((rows, HIDDEN), BF16),
+        V((rows, D), BF16), V((rows, D), BF16), V((2, rows, D // 2), BF16),
+    )
+
+    def attention_grads(gqkv_s, nor_s, gat_s, mix_s, ext):
+        def inside(wqkv_s, wout_s, qkv_s, tok_s, dout_s, res_s, gres, gm_s):
+            loads = [
+                pltpu.make_async_copy(src, dst, o_sem.at[4 + i])
+                for i, (src, dst) in enumerate(
+                    ((wqkv, wqkv_s), (wout, wout_s), (resid, res_s), (mixed, mix_s))
+                )
+            ]
+            for copy in loads:
+                copy.start()
+            ext[...] = jnp.zeros_like(ext)
+            qkv_s[T:KEYS, :] = jnp.zeros((KEYS - T, 3 * D), BF16)
+            for d in range(1, NZ):
+                gate_copy(d).wait_send()
+                source = lax.rem(z + NZ - d, NZ)
+                remote(ggr.at[source], ggr.at[source], g_send.at[d - 1], g_recv.at[d - 1], (dp, source)).wait_recv()
+            own_gate.wait()
+            for copy in loads:
+                copy.wait()
+
+            def image(mb, carry):
+                @pl.when(mb == 0)
+                def _():
+                    load([pg0.at[p] for p in range(NZ)])
+
+                @pl.when(mb == 1)
+                def _():
+                    load_item(0)
+
+                fetches = [
+                    pltpu.make_async_copy(src.at[mb], dst, o_sem.at[8 + i])
+                    for i, (src, dst) in enumerate(((qkv, qkv_s.at[0:T]), (dout, dout_s), (tok, tok_s)))
+                ]
+                for fetch in fetches:
+                    fetch.start()
+                table, _ = route_table(rt, mb)
+                gates = jnp.concatenate([ggr[p, mb] for p in range(NZ)], axis=0)
+                g = jnp.where(table, gates, 0.0)
+                probs = rp[mb]
+                gl = (probs * (g - jnp.sum(probs * g, axis=0, keepdims=True))).astype(BF16)
+                n2, r2 = normal(res_s[mb])
+                inner = (n2 * vec[2:3] + vec[3:4]).astype(BF16)
+                wr = dot(gl, inner)
+                for p in range(NZ):
+                    ext[8 + LOCAL * p : 8 + LOCAL * (p + 1), :] += wr[8 * p : 8 * p + LOCAL]
+                gi = quad_sum() + dot(gl, wrt[...], TN)
+                ext[5:6, :] += jnp.sum(gi * n2, axis=0, keepdims=True)
+                ext[6:7, :] += jnp.sum(gi, axis=0, keepdims=True)
+                u = gi * vec[2:3]
+                fetches[1].wait()
+                grad = dout_s[...].astype(F32) + r2 * (
+                    u - jnp.mean(u, -1, keepdims=True) - n2 * jnp.mean(u * n2, -1, keepdims=True)
+                )
+                gres[mb] = grad
+                low = grad.astype(BF16)
+                gat_s[mb] = low
+                ext[4:5, :] += jnp.sum(low.astype(F32), axis=0, keepdims=True)
+                gm_s[...] = dot(low, wout_s[...], NT).astype(BF16)
+                fetches[0].wait()
+
+                def heads(p, carry):
+                    at = [pl.ds(pl.multiple_of(i * D + p * 128, 128), 128) for i in range(3)]
+                    q, k, v = qkv_s[0:T, at[0]], qkv_s[:, at[1]], qkv_s[:, at[2]]
+                    gm = gm_s[:, at[0]]
+                    gq = jnp.zeros((T, 128), F32)
+                    gk = jnp.zeros((KEYS, 128), F32)
+                    gv = jnp.zeros((KEYS, 128), F32)
+                    for which in (0, 1):
+                        mask = half_mask(which)
+                        km = k * mask
+                        prob = attention_probs(dot(q, km, NT) * HEAD_DIM ** (-0.5))
+                        gpr = dot(gm, v * mask, NT)
+                        gs = (prob * (gpr - jnp.sum(prob * gpr, axis=-1, keepdims=True))).astype(BF16)
+                        gq = gq + dot(gs, km)
+                        gk = gk + dot(gs, q * mask, TN)
+                        gv = gv + dot(prob.astype(BF16), gm * mask, TN)
+                    gqkv_s[mb, :, at[0]] = (gq * HEAD_DIM ** (-0.5)).astype(BF16)
+                    gqkv_s[mb, :, at[1]] = (gk[0:T] * HEAD_DIM ** (-0.5)).astype(BF16)
+                    gqkv_s[mb, :, at[2]] = gv[0:T].astype(BF16)
+                    return carry
+
+                lax.fori_loop(0, PAIRS, heads, 0)
+                for row, i in ((2, 0), (3, 2)):
+                    ext[row : row + 1, :] += jnp.sum(
+                        gqkv_s[mb, :, i * D : (i + 1) * D].astype(F32), axis=0, keepdims=True
+                    )
+                gn = dot(gqkv_s[mb], wqkv_s[...], NT)
+                fetches[2].wait()
+                n1, r1 = normal(tok_s[...].astype(F32))
+                nor_s[mb] = (n1 * vec[0:1] + vec[1:2]).astype(BF16)
+                ext[0:1, :] += jnp.sum(gn * n1, axis=0, keepdims=True)
+                ext[1:2, :] += jnp.sum(gn, axis=0, keepdims=True)
+                w = gn * vec[0:1]
+                gres[mb] += r1 * (
+                    w - jnp.mean(w, -1, keepdims=True) - n1 * jnp.mean(w * n1, -1, keepdims=True)
+                )
+                pltpu.make_async_copy(gres.at[mb], ig_o.at[mb], o_sem.at[11 + mb]).start()
+                return carry
+
+            lax.fori_loop(0, MB, image, 0)
+            for mb in range(MB):
+                pltpu.make_async_copy(gres.at[mb], ig_o.at[mb], o_sem.at[11 + mb]).wait()
+
+        pl.run_scoped(
+            inside,
+            V((D, 3 * D), BF16), V((D, D), BF16), V((KEYS, 3 * D), BF16), V((T, D), BF16), V((T, D), BF16),
+            V((MB, T, D), F32), V((MB, T, D), F32), V((T, D), BF16),
+        )
+
+        def shared(a):
+            for zz in range(NZ):
+                @pl.when(z == zz)
+                def _():
+                    at = 24 + 5 * LOCAL * zz
+                    ext[at : at + LOCAL, :] = bb[...]
+                    for f in range(4):
+                        ext[at + LOCAL * (f + 1) : at + LOCAL * (f + 2), :] = bi[:, f * CHUNK : (f + 1) * CHUNK]
+            for i in range(3):
+                total = jnp.zeros((D, D), F32)
+                for mb in range(MB):
+                    total = total + dot(nor_s[mb], gqkv_s[mb, :, i * D : (i + 1) * D], TN)
+                a[i * D : (i + 1) * D, :] = total.astype(BF16)
+            total = jnp.zeros((D, D), F32)
+            for mb in range(MB):
+                total = total + dot(mix_s[mb], gat_s[mb], TN)
+            a[3 * D : 4 * D, :] = total.astype(BF16)
+            a[4 * D : TOTAL, :] = ext[...].astype(BF16)
+
+            def share(side, zz):
+                return pl.ds(pl.multiple_of((side * NZ + zz) * SHARE, 16), SHARE)
+
+            def to_core(zz):
+                return remote(a.at[share(1 - c, zz)], ar_core.at[zz], ac_send.at[zz], ac_recv.at[zz], partner)
+
+            for zz in range(NZ):
+                to_core(zz).start()
+            for kind in (0, 1):
+                turn(kind, 0)
+
+            def along(flow, zz, slot):
+                return remote(
+                    a.at[share(c, zz)], ar_z.at[flow, slot], az_send.at[flow, slot], az_recv.at[flow, slot],
+                    (dp, z - 1 if flow == 0 else z + 1),
+                )
+
+            for j in range(NZ):
+                zz = j
+                to_core(zz).wait_recv()
+                a[share(c, zz), :] = add_low(a[share(c, zz), :], ar_core[zz])
+            for j in range(NZ - 1):
+                @pl.when(z == NZ - 1)
+                def _():
+                    along(0, j, j).start()
+
+                @pl.when(z == 0)
+                def _():
+                    along(1, NZ - 1 - j, NZ - 2 - j).start()
+
+            def sum_step(j):
+                for flow, dest in ((0, j), (1, NZ - 1 - j)):
+                    slot = dest if flow == 0 else dest - 1
+                    if 0 <= slot < NZ - 1:
+                        passes = middle(0, flow, 0, dest)
+
+                        @pl.when(jnp.logical_or(passes, z == dest))
+                        def _():
+                            along(flow, dest, slot).wait_recv()
+                            a[share(c, dest), :] = add_low(a[share(c, dest), :], ar_z[flow, slot])
+
+                        @pl.when(passes)
+                        def _():
+                            along(flow, dest, slot).start()
+
+            for j in range(NZ):
+                sum_step(j)
+                if j == 1:
+                    for kind in (0, 1):
+                        turn(kind, 1)
+
+            halves = (slice(0, 208), slice(208, SHARE))
+
+            def cross(stage_no, half, src):
+                dest = (ar_xy1, ar_xy2)[stage_no].at[halves[half]]
+                way = half if stage_no == 0 else 1 - half
+                return remote(
+                    src, dest, ax_send.at[stage_no, half], ax_recv.at[stage_no, half], (flips[way] * 2 + c, z)
+                )
+
+            def mine(half):
+                start_row = 0 if half == 0 else 208
+                size = 208 if half == 0 else SHARE - 208
+                return pl.ds(pl.multiple_of((c * NZ + z) * SHARE + start_row, 16), size)
+
+            for half in (0, 1):
+                cross(0, half, a.at[mine(half)]).start()
+            for kind in (0, 1):
+                turn(kind, 2)
+            for half in (0, 1):
+                cross(0, half, a.at[mine(half)]).wait_recv()
+                ar_t[halves[half], :] = add_low(a[mine(half), :], ar_xy1[halves[half], :])
+                cross(1, half, ar_t.at[halves[half]]).start()
+            for kind in (0, 1):
+                send1(kind, LOCAL - 1)
+            for half in (0, 1):
+                cross(1, half, ar_t.at[halves[half]]).wait()
+                ar_t[halves[half], :] = add_low(ar_t[halves[half], :], ar_xy2[halves[half], :])
+                cross(0, half, a.at[mine(half)]).wait_send()
+            for zz in range(NZ):
+                to_core(zz).wait_send()
+                for flow in (0, 1):
+                    slot = zz if flow == 0 else zz - 1
+                    if 0 <= slot < NZ - 1:
+                        goes = (z > zz) if flow == 0 else (z < zz)
+
+                        @pl.when(goes)
+                        def _():
+                            along(flow, zz, slot).wait_send()
+
+        pl.run_scoped(shared, V((TOTAL, D), BF16))
+
+    pl.run_scoped(
+        attention_grads,
+        V((MB, T, 3 * D), BF16), V((MB, T, D), BF16), V((MB, T, D), BF16), V((MB, T, D), BF16), V((EXTRA, D), F32),
+    )
+
+    def place(zz):
+        return ar_o.at[pl.ds(pl.multiple_of((c * NZ + zz) * SHARE, 16), SHARE)]
+
+    own_share = pltpu.make_async_copy(ar_t, place(z), l_sem.at[6])
+    own_share.start()
+
+    def spread(up, h):
+        source = z - h if up else z + h
+        index = (0 if up else 1, h)
+        return remote(
+            ar_t if h == 0 else place(source), place(source), zz_send.at[index], zz_recv.at[index],
+            (dp, z + 1 if up else z - 1),
+        )
+
+    def leaves(up, h):
+        return jnp.logical_and(z - h >= 0, z + 1 < NZ) if up else jnp.logical_and(z + h < NZ, z >= 1)
+
+    def to_partner(src, k, zz):
+        return remote(src, place(zz), cc_send.at[k], cc_recv.at[k], partner)
+
+    for up in (True, False):
+        @pl.when(leaves(up, 0))
+        def _():
+            spread(up, 0).start()
+
+    to_partner(ar_t, 0, z).start()
+    for mb in range(MB):
+        def image_out(base):
+            fetch = pltpu.make_async_copy(resid.at[mb], base, l_sem.at[5])
+            fetch.start()
+            load_item(1 + mb)
+            fetch.wait()
+            block_o[mb] = (base[...] + quad_sum()).astype(BF16)
+
+        pl.run_scoped(image_out, V((T, D), F32))
+    for h in range(NZ - 1):
+        for up in (True, False):
+            source = z - h - 1 if up else z + h + 1
+
+            @pl.when((z - h - 1 >= 0) if up else (z + h + 1 < NZ))
+            def _():
+                index = (0 if up else 1, h)
+                remote(
+                    place(source), place(source), zz_send.at[index], zz_recv.at[index],
+                    (dp, z - 1 if up else z + 1),
+                ).wait_recv()
+                k = lax.rem(source - z + NZ, NZ)
+                to_partner(place(source), k, source).start()
+
+            if h + 1 < NZ - 1:
+                @pl.when(leaves(up, h + 1))
+                def _():
+                    spread(up, h + 1).start()
+    for kind in (0, 1):
+        turn(kind, 3)
+    for kind in (0, 1):
+        for e in range(LOCAL):
+            finish(kind, e)
+    own_share.wait()
+    for k in range(NZ):
+        zz = lax.rem(z + k, NZ)
+        src = ar_t if k == 0 else place(zz)
+        to_partner(src, k, zz).wait_send()
+        other = ar_o.at[pl.ds(pl.multiple_of(((1 - c) * NZ + zz) * SHARE, 16), SHARE)]
+        remote(other, other, cc_send.at[k], cc_recv.at[k], partner).wait_recv()
+    for h in range(NZ - 1):
+        for up in (True, False):
+            @pl.when(leaves(up, h))
+            def _():
+                spread(up, h).wait_send()
+    for item in range(3):
+        for d in range(1, NZ):
+            home(item, d).wait_send()
+    for kind in (0, 1):
+        for e in range(LOCAL):
+            for slot in (0, 1):
+                hop1(kind, e, slot).wait_send()
+            hop2(kind, e).wait_send()
+            result(kind, e).wait()
+
+
+def grads_call(*operands):
+    vm = pl.BlockSpec(memory_space=pltpu.VMEM)
+    hb = pl.BlockSpec(memory_space=pl.ANY)
+    S = jax.ShapeDtypeStruct
+    V = pltpu.VMEM
+    DMA = pltpu.SemaphoreType.DMA
+    outs = [
+        (S((MB, T, D), BF16), vm),
+        (S((MB, T, D), F32), hb),
+        (S((TOTAL, D), BF16), hb),
+        (S((LOCAL, BAND, HIDDEN), BF16), hb),
+        (S((LOCAL, PART, D), BF16), hb),
+        (S((3, NZ, T, D), BF16), hb),
+    ]
+    return pl.pallas_call(
+        grads_kernel,
+        out_shape=[o[0] for o in outs],
+        in_specs=[vm] * 6 + [hb] * 15,
+        out_specs=[o[1] for o in outs],
+        scratch_shapes=[
+            V((LOCAL, 4, PART, D), BF16), V((LOCAL, 4, BAND, HIDDEN), BF16),
+            V((LOCAL, 2, PART, D), BF16), V((LOCAL, 2, BAND, HIDDEN), BF16),
+            V((LOCAL, PART, D), BF16), V((LOCAL, BAND, HIDDEN), BF16),
+            V((NZ, SHARE, D), BF16), V((2, NZ - 1, SHARE, D), BF16),
+            V((SHARE, D), BF16), V((SHARE, D), BF16), V((SHARE, D), BF16),
+            V((NZ, MB, 8, T), F32), V((NZ, T, D), BF16),
+            DMA((2, LOCAL)), DMA((2, LOCAL)), DMA((2, LOCAL, 2)), DMA((2, LOCAL, 2)), DMA((2, LOCAL)), DMA((2, LOCAL)),
+            DMA((3, NZ - 1)), DMA((3, NZ - 1)), DMA((NZ - 1,)), DMA((NZ - 1,)),
+            DMA((NZ,)), DMA((NZ,)), DMA((2, NZ - 1)), DMA((2, NZ - 1)), DMA((2, 2)), DMA((2, 2)),
+            DMA((2, NZ - 1)), DMA((2, NZ - 1)), DMA((NZ,)), DMA((NZ,)),
+            DMA((8,)), DMA((13,)), DMA((2, LOCAL)),
+        ],
+        compiler_params=pltpu.CompilerParams(
+            collective_id=2, has_side_effects=True, vmem_limit_bytes=60 << 20
+        ),
+        name="grads",
+    )(*operands)
 
 def fast_body(
     tokens, routes, gain_one, shift_one, w_qkv, qv_bias, w_out, out_bias, gain_two, shift_two,
@@ -704,73 +1296,41 @@
         jnp.transpose(routes.reshape(MB, SEQ, TOP), (0, 2, 1)),
         ((0, 0), (0, 8 - TOP), (0, T - SEQ)), constant_values=-1,
     )
-    row = lambda a: a.reshape(1, -1)
-    bqkv = jnp.concatenate([qv_bias[0], jnp.zeros_like(qv_bias[0]), qv_bias[1]])
+    vec = jnp.stack(
+        [gain_one, shift_one, gain_two, shift_two, out_bias, qv_bias[0], qv_bias[1], jnp.zeros_like(out_bias)]
+    )
     wrt = jnp.pad(w_route.T.reshape(NZ, LOCAL, D), ((0, 0), (0, 8 - LOCAL), (0, 0))).reshape(32, D)
-    (qkv, mixed, resid, rp, gg, bb, bi, xr, gp, act, gh, pb, pg) = dispatch_call(
-        tok, rt, row(gain_one), row(shift_one), w_qkv, row(bqkv), w_out, row(out_bias),
-        row(gain_two), row(shift_two), wrt, b_in.reshape(16, 1, CHUNK), b_back.reshape(LOCAL, 1, D),
-        dout, w_in, w_back,
+    (qkv, mixed, resid, rp, gg, bb, bi, xr, gp, act, gh, pb, pg, pg0) = dispatch_call(
+        tok, rt, vec, w_qkv, w_out, wrt, b_in, b_back, dout, w_in, w_back
     )
-    scale = HEAD_DIM ** (-0.5)
-    pb = lax.psum_scatter(pb.astype(F32), "expert", scatter_dimension=0, tiled=False)
-    pg = lax.psum_scatter(pg.astype(F32), "expert", scatter_dimension=0, tiled=False)
-    gg = lax.all_to_all(gg, "expert", 0, 0, tiled=True)
-    grad_gate = jnp.transpose(gg, (1, 0, 2, 3)).reshape(MB, 32, T)
-    block = (resid + pb).astype(BF16)[:, :SEQ].reshape(MB * SEQ, D)
-    table = jnp.stack([route_table(rt, mb)[0] for mb in range(MB)])
-    g = jnp.where(table, grad_gate, 0.0)
-    gl = rp * (g - jnp.sum(rp * g, axis=1, keepdims=True))
-    cot = dout.astype(F32)
-    n2, r2 = normal(resid)
-    inner = (n2 * gain_two + shift_two).astype(BF16)
-    acc_route = jnp.einsum("bet,btd->ed", gl, inner.astype(F32), precision=HIGH)
-    gi = pg + jnp.einsum("bet,ed->btd", gl, wrt.astype(F32), precision=HIGH)
-    acc_gain_two = jnp.sum(gi * n2, axis=(0, 1))
-    acc_shift_two = jnp.sum(gi, axis=(0, 1))
-    u = gi * gain_two
-    grad_resid = cot + r2 * (
-        u - jnp.mean(u, -1, keepdims=True) - n2 * jnp.mean(u * n2, -1, keepdims=True)
+    block, ig, ar, wi, wb, _ = grads_call(
+        vec, rt, wrt, bb, bi, rp, tok, dout, w_qkv, w_out, qkv, mixed, resid, gg, xr, gp, act, gh, pb, pg, pg0
     )
-    ga = grad_resid.astype(BF16)
-    acc_out = jnp.einsum("btd,bte->de", mixed, ga, preferred_element_type=F32)
-    acc_out_bias = jnp.sum(ga.astype(F32), axis=(0, 1))
-    gm = jnp.einsum("bte,de->btd", ga, w_out, preferred_element_type=F32).astype(BF16)
-    gm = gm[:, :SEQ].reshape(MB, SEQ, HEADS, HEAD_DIM)
-    query, keys, values = [
-        qkv[:, :SEQ, i * D : (i + 1) * D].reshape(MB, SEQ, HEADS, HEAD_DIM) for i in range(3)
-    ]
-    again = jnp.einsum("ishd,ithd->ihst", query, keys, preferred_element_type=F32) * scale
-    probs = jax.nn.softmax(again, axis=-1)
-    gpa = jnp.einsum("ishd,ithd->ihst", gm, values, preferred_element_type=F32)
-    gsc = (probs * (gpa - jnp.sum(probs * gpa, -1, keepdims=True))).astype(BF16)
-    gq = jnp.einsum("ihst,ithd->ishd", gsc, keys, preferred_element_type=F32) * scale
-    gk = jnp.einsum("ihst,ishd->ithd", gsc, query, preferred_element_type=F32) * scale
-    gv = jnp.einsum("ihst,ishd->ithd", probs.astype(BF16), gm, preferred_element_type=F32)
+    dp, z = lax.axis_index("dp"), lax.axis_index("expert")
     rows = MB * SEQ
-    gqkv = jnp.concatenate([a.reshape(rows, D) for a in (gq, gk, gv)], axis=1).astype(BF16)
-    x = tokens.astype(F32)
-    n1, r1 = normal(x)
-    normed = (n1 * gain_one + shift_one).astype(BF16)
-    acc_qkv = jnp.einsum("rd,re->de", normed, gqkv, preferred_element_type=F32)
-    cs = jnp.sum(gqkv.astype(F32), axis=0)
-    acc_qv = jnp.stack([cs[:D], cs[2 * D :]])
-    gn = jnp.einsum("re,de->rd", gqkv, w_qkv, preferred_element_type=F32)
-    acc_gain_one = jnp.sum(gn * n1, axis=0)
-    acc_shift_one = jnp.sum(gn, axis=0)
-    w = gn * gain_one
-    input_grad = grad_resid[:, :SEQ].reshape(rows, D) + r1 * (
-        w - jnp.mean(w, -1, keepdims=True) - n1 * jnp.mean(w * n1, -1, keepdims=True)
+    ext = ar[4 * D :].astype(F32)
+    qkv_grad = jnp.concatenate([ar[i * D : (i + 1) * D] for i in range(3)], axis=1).astype(F32)
+    biases = lax.dynamic_slice(ext, (24 + 5 * LOCAL * z, 0), (5 * LOCAL, D))
+    bb_grad = lax.dynamic_slice(biases[:LOCAL], (0, dp * BAND), (LOCAL, BAND))
+    bi_grad = jnp.transpose(biases[LOCAL:].reshape(4, LOCAL, D), (1, 0, 2)).reshape(LOCAL, HIDDEN)
+    bi_grad = lax.dynamic_slice(bi_grad, (0, dp * PART), (LOCAL, PART))
+    return (
+        block[:, :SEQ].reshape(rows, D),
+        ig[:, :SEQ].reshape(rows, D),
+        ext[0],
+        ext[1],
+        qkv_grad,
+        ext[2:4],
+        ar[3 * D : 4 * D].astype(F32),
+        ext[4],
+        ext[5],
+        ext[6],
+        ext[8 : 8 + NZ * LOCAL].T,
+        wi.astype(F32),
+        bi_grad,
+        wb.astype(F32),
+        bb_grad,
     )
-    wb = jnp.einsum("erf,erd->efd", act, gp, preferred_element_type=F32).astype(BF16)
-    wi = jnp.einsum("erd,erf->edf", xr, gh, preferred_element_type=F32).astype(BF16)
-    scat = lambda a: lax.psum_scatter(a, "dp", scatter_dimension=1, tiled=True).astype(F32)
-    shared = lax.psum(
-        (acc_gain_one, acc_shift_one, acc_qkv, acc_qv, acc_out, acc_out_bias, acc_gain_two,
-         acc_shift_two, acc_route.reshape(NZ, 8, D)[:, :LOCAL].reshape(16, D).T),
-        ("dp", "expert"),
-    )
-    return (block, input_grad, *shared, scat(wi), scat(bi.reshape(LOCAL, 4 * CHUNK)), scat(wb), scat(bb.reshape(LOCAL, D)))
 
 
 def solution(mesh):

time: 1050 us -> 435 us (0.41)
  waiting for transfers between devices: 715 us -> 0 us
  Pallas kernels: 137 us -> 409 us
  matrix products: 66.8 us -> 0 us
  local copies, waits for them, and re-layouts: 73.8 us -> 10.5 us
  other arithmetic: 31.1 us -> 13.7 us
  between operations: 15 us -> 0.86 us
    reduce_scatter x4 -> x0, waiting for transfers between devices: 363 us -> none  [the longest x2 248 us: fast_body(): lax.psum_scatter(a, 'dp', scatter_dimension=1, tiled=True).astype(F32)]
    psum x2 -> x0, waiting for transfers between devices: 327 us -> none  [fast_body(): lax.psum((acc_gain_one, acc_shift_one, acc_qkv, acc_qv, acc_out, acc_out_...]
    pallas_call x0 -> x1, Pallas kernels: none -> 255 us  [grads_call(): pl.pallas_call(grads_kernel, out_shape=[o[0] for o in outs], in_specs=[vm...]
    dot_general x12 -> x0, matrix products: 62.1 us -> none  [the longest x1 17 us: fast_body(): jnp.einsum('erd,erf->edf', xr, gh, preferred_element_type=F32).astype(BF16)]
    unnamed x95 -> x26, local copies, waits for them, and re-layouts: 27.5 us -> 0.05 us
    unnamed x10 -> x0, waiting for transfers between devices: 25.7 us -> none
    reshape x15 -> x3, local copies, waits for them, and re-layouts: 22.6 us -> 2.11 us  [the longest x1 1.15 us: fast_body(): ig[:, :SEQ].reshape(rows, D)]
    pallas_call x1, Pallas kernels: 137 us -> 154 us  [dispatch_call(): pl.pallas_call(dispatch_kernel, out_shape=[o[0] for o in outs], in_specs=...]
  transfers between devices with their start and end apart: 9 -> 0, of which waited for: 7 -> 0; matrix products, arithmetic and copies ran while one was open for 12% -> 0% of each run, Pallas kernels for 0% -> 0%
where the time goes in v2:
time: 435 us; the launch traced here: 434 us
  Pallas kernels  409 us (94%)
  other arithmetic  13.7 us (3%)
  local copies, waits for them, and re-layouts  10.5 us (2%)
    pallas_call x1, Pallas kernels, grads_call(): pl.pallas_call(grads_kernel, out_shape=[o[0] for o in outs], in_specs=[vm...  255 us
    pallas_call x1, Pallas kernels, dispatch_call(): pl.pallas_call(dispatch_kernel, out_shape=[o[0] for o in outs], in_specs=...  154 us

profile of v2, /device:TPU:0, one launch (start us, length us, event | category | flops | bytes accessed | tf_op | source)
XLA Modules:
  0.0 433.9 jit_solution(5277216893485345324)
XLA Ops:
  0.6 0.0 copy-start.3
  0.7 0.0 copy-start.5
  0.7 0.0 copy-start.7
  0.7 0.0 copy-start.8
  0.7 0.0 copy-start.9
  0.7 0.0 copy-start.10
  0.7 0.0 copy-start.11
  0.7 0.0 copy-start.6
  0.7 0.0 copy-start.12
  0.7 1.2 reshape.60
  2.0 0.9 pad.17.tok
  2.9 0.0 copy-done.3
  2.9 0.1 reshape.61
  3.0 0.9 pad.18.dout
  3.9 0.0 copy-done.5
  3.9 0.6 pad_bitcast_fusion.wrt
  4.5 0.0 copy-done.7
  4.5 0.0 copy-done.8
  4.5 0.0 copy-done.9
  4.6 0.0 copy-done.10
  4.6 0.0 copy-done.11
  4.6 0.0 copy-done.6
  4.6 0.6 stack.23.vec
  5.3 0.0 copy-done.12
  5.3 0.1 reshape.57
  5.4 0.6 pad.15.rt
  6.0 153.9 %dispatch.1 = (bf16[2,208,2304]{2,1,0:T(8,128)(2,1)}, bf16[2,208,768]{2,1,0:T(8,128)(2,1)}, f32[2,208,768]{2,1,0:T(8,128)}, f32[2,32,208]{2,1,0:T(8,128)}, f32[4...) custom-call(bf16[2,208,768]{2,1,0:T(8,128)(2,1)} %pad.17.tok, ...), custom_call_target="tpu_custom_call" | custom-call | tf_op jit(solution)/shard_map/dispatch/pallas_call | solution.py:695
  159.9 254.9 %grads.1 = (bf16[2,208,768]{2,1,0:T(8,128)(2,1)}, f32[2,208,768]{2,1,0:T(8,128)}, bf16[3200,768]{1,0:T(8,128)(2,1)}, bf16[4,96,3072]{2,1,0:T(8,128)(2,1)}, bf16[...) custom-call(f32[8,768]{1,0:T(8,128)} %stack.23.vec, s32[2,8,208]{2,1,0:T(8,128)} %pad.15.rt, ...), custom_call_target="tpu_custom_call" | custom-call | tf_op jit(solution)/shard_map/grads/pallas_call | solution.py:1263
  414.8 4.2 slice_convert_fusion
  419.0 0.0 copy-start.1
  419.0 3.2 maximum_convert_fusion
  422.2 0.0 copy-done.1
  422.2 0.0 copy-start
  422.2 2.8 convert_element_type.23
  425.0 0.0 copy-done
  425.0 0.0 copy-start.2
  425.0 2.6 convert_element_type.24
  427.6 0.0 copy-done.2
  427.6 0.0 copy-start.4
  427.6 0.1 slice.52
  427.6 1.1 reshape.63
  428.8 0.0 copy-done.4
  428.8 0.9 reshape.62
  429.8 1.0 slice_convert_fusion.1
  430.7 0.6 constant_dynamic-slice_fusion.1
  431.4 0.6 constant_dynamic-slice_fusion
  432.0 0.6 slice_reduce_fusion
  432.6 0.7 dynamic-slice.2
  433.3 0.6 slice.69
  (10 shorter events, 0.1 us)
Async XLA Ops:
  0.6 2.2 copy-start.3
  0.7 3.2 copy-start.5
  0.7 3.9 copy-start.7
  0.7 3.8 copy-start.8
  0.7 3.9 copy-start.9
  0.7 3.9 copy-start.10
  0.7 3.9 copy-start.11
  0.7 3.9 copy-start.6
  0.7 4.5 %copy-start.12 = (s32[394,2]{0,1:T(2,128)S(1)}, s32[394,2]{0,1:T(2,128)}, u32[]{:S(2)}) copy-start(s32[394,2]{0,1:T(2,128)} %param.17) | copy-start | bytes 9460
  419.0 3.2 copy-start.1
  422.2 2.8 copy-start
  425.0 2.6 copy-start.2
  427.6 1.2 copy-start.4

commit v3 on v2

--- a/solution.py
+++ b/solution.py
@@ -1,3 +1,5 @@
+import functools
+
 import jax
 import jax.numpy as jnp
 from jax import lax
@@ -518,6 +520,11 @@
                     for copy in weights(n + 1, 1 - slot):
                         copy.start()
 
+                @pl.when(n >= 2)
+                def _():
+                    for copy in stores(n - 2, slot):
+                        copy.wait()
+
                 for copy in weights(n, slot):
                     copy.wait()
                 hid = dot(xs[e, rows, :], wb1[slot]) + b_in[pl.ds(e, 1), cols]
@@ -528,11 +535,6 @@
                 slope = half + (0.5 * hid) * (1.0 - bend * bend) * (
                     0.7978845608 + (3 * 0.7978845608 * 0.044715) * square
                 )
-
-                @pl.when(n >= 2)
-                def _():
-                    for copy in stores(n - 2, slot):
-                        copy.wait()
 
                 act_st[slot] = act
                 acc_o[...] += dot(act, wb2[slot])
@@ -556,6 +558,12 @@
                 grs[src, at, :] = back[part]
                 ggs[src, at, :] = jnp.broadcast_to(gg[part], (CAP_ROWS, 128))
 
+            @pl.when(jnp.logical_and(mb == 1, e == 0))
+            def _():
+                for d in range(1, NZ):
+                    sent_home(d).start()
+                own_home().start()
+
             @pl.when(jnp.logical_and(mb == 0, e == 1))
             def _():
                 for kind in range(3):
@@ -613,12 +621,6 @@
             return carry
 
         lax.fori_loop(0, NZ, gather, 0)
-
-        @pl.when(mb == 0)
-        def _():
-            for d in range(1, NZ):
-                sent_home(d).start()
-            own_home().start()
 
         @pl.when(mb == 1)
         def _():
@@ -732,9 +734,9 @@
 def grads_kernel(
     vec, rt, wrt, bb, bi, rp,
     tok, dout, wqkv, wout, qkv, mixed, resid, gg, xr, gp, act, gh, pb, pg, pg0,
-    block_o, ig_o, ar_o, wi_o, wb_o, land_o,
-    core_b, core_i, st1_b, st1_i, st2_b, st2_i, ar_core, ar_z, ar_xy1, ar_xy2, ar_t,
-    ggr, quad,
+    block_o, ig_o, ar_o, kb_o, ki_o, lb_o, li_o, land_o,
+    core_b, core_i, st1_b, st1_i, ar_core, ar_z, ar_xy1, ar_xy2, ar_t,
+    ggr,
     c_send, c_recv, s1_send, s1_recv, s2_send, s2_recv, r_send, r_recv, g_send, g_recv,
     ac_send, ac_recv, az_send, az_recv, ax_send, ax_recv, zz_send, zz_recv, cc_send, cc_recv,
     l_sem, o_sem, f_sem,
@@ -780,25 +782,26 @@
             ref = land_o.at[item, source]
             remote(ref, ref, r_send.at[item, d - 1], r_recv.at[item, d - 1], (dp, source)).wait_recv()
 
-    def load(sources):
-        copies = [pltpu.make_async_copy(ref, quad.at[i], l_sem.at[1 + i]) for i, ref in enumerate(sources)]
+    def load(quad, sources):
+        copies = [pltpu.make_async_copy(ref, quad[i], l_sem.at[1 + i]) for i, ref in enumerate(sources)]
         for copy in copies:
             copy.start()
         for copy in copies:
             copy.wait()
 
-    def load_item(item):
+    def load_item(quad, item):
         arrived(item)
         own = pg.at[z] if item == 0 else pb.at[item - 1, z]
-        load([own] + [land_o.at[item, lax.rem(z + d, NZ)] for d in range(1, NZ)])
-
-    def quad_sum():
-        return (quad[0].astype(F32) + quad[1].astype(F32)) + (quad[2].astype(F32) + quad[3].astype(F32))
+        load(quad, [own] + [land_o.at[item, lax.rem(z + d, NZ)] for d in range(1, NZ)])
+
+    def quad_sum(quad):
+        parts = [ref[...].astype(F32) for ref in quad]
+        return (parts[0] + parts[1]) + (parts[2] + parts[3])
 
     def middle(arr, flow, mb, dest):
         return jnp.logical_and(z > dest, z < NZ - 1) if flow == 0 else jnp.logical_and(z < dest, z > 0)
 
-    cores, lands1, lands2 = (core_b, core_i), (st1_b, st1_i), (st2_b, st2_i)
+    cores, lands1, lands2, keeps = (core_b, core_i), (st1_b, st1_i), (lb_o, li_o), (kb_o, ki_o)
 
     def core_copy(kind, e, src):
         return remote(src, cores[kind].at[e], c_send.at[kind, e], c_recv.at[kind, e], partner)
@@ -827,125 +830,24 @@
         hop2(kind, e).start()
         hop1(kind, e, 0).wait_recv()
         ref[e, yx] = add_low(ref[e, yx], lands1[kind][e, 0])
-
-    outs = (wb_o, wi_o)
-
-    def result(kind, e):
-        return pltpu.make_async_copy(lands2[kind].at[e], outs[kind].at[e], f_sem.at[kind, e])
-
-    def finish(kind, e):
-        hop2(kind, e).wait_recv()
-        lands2[kind][e] = add_low(lands2[kind][e], cores[kind][e, yx])
-        result(kind, e).start()
+        keep(kind, e).start()
+
+    def keep(kind, e):
+        return pltpu.make_async_copy(cores[kind].at[e, yx], keeps[kind].at[e], f_sem.at[kind, e])
 
     for item in range(3):
         for d in range(1, NZ):
             home(item, d).start()
 
-    def weight_grads(wg_b, wg_i, act_s, gh_s, x_s, gp_s, xp):
-        def fetch(e, which):
-            pairs = ((act, act_s), (gp, gp_s), (xr, x_s), (gh, gh_s))
-            return [
-                pltpu.make_async_copy(pairs[i][0].at[e], pairs[i][1], o_sem.at[i]) for i in which
-            ]
-
-        def pull(e, which):
-            for copy in fetch(e, which):
-                copy.start()
-
-        def ready(e, which):
-            for copy in fetch(e, which):
-                copy.wait()
-
-        pull(0, (0, 1, 2, 3))
-
-        def one(e, carry):
-            def back_block(k, side):
-                at = pl.ds(pl.multiple_of((2 * k + side) * PART, 128), PART)
-                return dot(act_s[:, at], gp_s[...], TN)
-
-            ready(e, (0, 1))
-
-            @pl.when(e > 0)
-            def _():
-                core_copy(0, e - 1, wg_b).wait_send()
-
-            def other_b(k, carry):
-                wg_b[k] = back_block(k, 1 - c).astype(BF16)
-                return carry
-
-            lax.fori_loop(0, 4, other_b, 0)
-            core_copy(0, e, wg_b).start()
-            ready(e, (2, 3))
-            for side in (0, 1):
-                for k in range(4):
-                    band = (2 * k + side) * BAND
-                    xp[side, :, k * BAND : (k + 1) * BAND] = x_s[:, band : band + BAND]
-
-            @pl.when(e > 0)
-            def _():
-                core_copy(1, e - 1, wg_i).wait_send()
-
-            def other_i(f, carry):
-                at = pl.ds(pl.multiple_of(f * CHUNK, 128), CHUNK)
-                grad = dot(xp[1 - c], gh_s[:, at], TN).astype(BF16)
-                for k in range(4):
-                    wg_i[k, :, at] = grad[k * BAND : (k + 1) * BAND]
-                return carry
-
-            lax.fori_loop(0, 4, other_i, 0)
-            core_copy(1, e, wg_i).start()
-            core_copy(0, e, wg_b).wait_recv()
-
-            def own_b(k, carry):
-                core_b[e, k] = (core_b[e, k].astype(F32) + back_block(k, c)).astype(BF16)
-                return carry
-
-            lax.fori_loop(0, 4, own_b, 0)
-
-            @pl.when(e < LOCAL - 1)
-            def _():
-                send1(0, e)
-                pull(e + 1, (0, 1))
-
-            core_copy(1, e, wg_i).wait_recv()
-
-            def own_i(f, carry):
-                at = pl.ds(pl.multiple_of(f * CHUNK, 128), CHUNK)
-                grad = dot(xp[c], gh_s[:, at], TN)
-                for k in range(4):
-                    core_i[e, k, :, at] = (
-                        core_i[e, k, :, at].astype(F32) + grad[k * BAND : (k + 1) * BAND]
-                    ).astype(BF16)
-                return carry
-
-            lax.fori_loop(0, 4, own_i, 0)
-
-            @pl.when(e < LOCAL - 1)
-            def _():
-                send1(1, e)
-                pull(e + 1, (2, 3))
-
-            return carry
-
-        lax.fori_loop(0, LOCAL, one, 0)
-        core_copy(0, LOCAL - 1, wg_b).wait_send()
-        core_copy(1, LOCAL - 1, wg_i).wait_send()
-
     V = pltpu.VMEM
     rows = MB * ROWS
-    pl.run_scoped(
-        weight_grads,
-        V((4, PART, D), BF16), V((4, BAND, HIDDEN), BF16), V((rows, HIDDEN), BF16), V((rows, HIDDEN), BF16),
-        V((rows, D), BF16), V((rows, D), BF16), V((2, rows, D // 2), BF16),
-    )
-
-    def attention_grads(gqkv_s, nor_s, gat_s, mix_s, ext):
+
+    def attention_grads(one, gqkv_s, nor_s, gat_s, ext):
         def inside(wqkv_s, wout_s, qkv_s, tok_s, dout_s, res_s, gres, gm_s):
             loads = [
                 pltpu.make_async_copy(src, dst, o_sem.at[4 + i])
                 for i, (src, dst) in enumerate(
-                    ((wqkv, wqkv_s), (wout, wout_s), (resid, res_s), (mixed, mix_s))
+                    ((wqkv, wqkv_s), (wout, wout_s))
                 )
             ]
             for copy in loads:
@@ -961,17 +863,19 @@
                 copy.wait()
 
             def image(mb, carry):
+                quad = [gqkv_s.at[mb, :, i * D : (i + 1) * D] for i in range(3)] + [gm_s]
+
                 @pl.when(mb == 0)
                 def _():
-                    load([pg0.at[p] for p in range(NZ)])
+                    load(quad, [pg0.at[p] for p in range(NZ)])
 
                 @pl.when(mb == 1)
                 def _():
-                    load_item(0)
+                    load_item(quad, 0)
 
                 fetches = [
                     pltpu.make_async_copy(src.at[mb], dst, o_sem.at[8 + i])
-                    for i, (src, dst) in enumerate(((qkv, qkv_s.at[0:T]), (dout, dout_s), (tok, tok_s)))
+                    for i, (src, dst) in enumerate(((qkv, qkv_s.at[0:T]), (dout, dout_s), (tok, tok_s), (resid, res_s)))
                 ]
                 for fetch in fetches:
                     fetch.start()
@@ -980,12 +884,13 @@
                 g = jnp.where(table, gates, 0.0)
                 probs = rp[mb]
                 gl = (probs * (g - jnp.sum(probs * g, axis=0, keepdims=True))).astype(BF16)
-                n2, r2 = normal(res_s[mb])
+                fetches[3].wait()
+                n2, r2 = normal(res_s[...])
                 inner = (n2 * vec[2:3] + vec[3:4]).astype(BF16)
                 wr = dot(gl, inner)
                 for p in range(NZ):
                     ext[8 + LOCAL * p : 8 + LOCAL * (p + 1), :] += wr[8 * p : 8 * p + LOCAL]
-                gi = quad_sum() + dot(gl, wrt[...], TN)
+                gi = quad_sum(quad) + dot(gl, wrt[...], TN)
                 ext[5:6, :] += jnp.sum(gi * n2, axis=0, keepdims=True)
                 ext[6:7, :] += jnp.sum(gi, axis=0, keepdims=True)
                 u = gi * vec[2:3]
@@ -993,7 +898,12 @@
                 grad = dout_s[...].astype(F32) + r2 * (
                     u - jnp.mean(u, -1, keepdims=True) - n2 * jnp.mean(u * n2, -1, keepdims=True)
                 )
-                gres[mb] = grad
+
+                @pl.when(mb == 1)
+                def _():
+                    pltpu.make_async_copy(gres, ig_o.at[0], o_sem.at[12]).wait()
+
+                gres[...] = grad
                 low = grad.astype(BF16)
                 gat_s[mb] = low
                 ext[4:5, :] += jnp.sum(low.astype(F32), axis=0, keepdims=True)
@@ -1033,23 +943,29 @@
                 ext[0:1, :] += jnp.sum(gn * n1, axis=0, keepdims=True)
                 ext[1:2, :] += jnp.sum(gn, axis=0, keepdims=True)
                 w = gn * vec[0:1]
-                gres[mb] += r1 * (
+                gres[...] += r1 * (
                     w - jnp.mean(w, -1, keepdims=True) - n1 * jnp.mean(w * n1, -1, keepdims=True)
                 )
-                pltpu.make_async_copy(gres.at[mb], ig_o.at[mb], o_sem.at[11 + mb]).start()
+                pltpu.make_async_copy(gres, ig_o.at[mb], o_sem.at[12 + mb]).start()
+
+                @pl.when(mb == 0)
+                def _():
+                    one(1)
+
                 return carry
 
             lax.fori_loop(0, MB, image, 0)
-            for mb in range(MB):
-                pltpu.make_async_copy(gres.at[mb], ig_o.at[mb], o_sem.at[11 + mb]).wait()
+            pltpu.make_async_copy(gres, ig_o.at[1], o_sem.at[13]).wait()
 
         pl.run_scoped(
             inside,
             V((D, 3 * D), BF16), V((D, D), BF16), V((KEYS, 3 * D), BF16), V((T, D), BF16), V((T, D), BF16),
-            V((MB, T, D), F32), V((MB, T, D), F32), V((T, D), BF16),
-        )
-
-        def shared(a):
+            V((T, D), F32), V((T, D), F32), V((T, D), BF16),
+        )
+
+        def shared(a, mix_s):
+            mix = pltpu.make_async_copy(mixed, mix_s, o_sem.at[4])
+            mix.start()
             for zz in range(NZ):
                 @pl.when(z == zz)
                 def _():
@@ -1062,6 +978,7 @@
                 for mb in range(MB):
                     total = total + dot(nor_s[mb], gqkv_s[mb, :, i * D : (i + 1) * D], TN)
                 a[i * D : (i + 1) * D, :] = total.astype(BF16)
+            mix.wait()
             total = jnp.zeros((D, D), F32)
             for mb in range(MB):
                 total = total + dot(mix_s[mb], gat_s[mb], TN)
@@ -1113,6 +1030,7 @@
                         def _():
                             along(flow, dest, slot).start()
 
+            one(2)
             for j in range(NZ):
                 sum_step(j)
                 if j == 1:
@@ -1135,14 +1053,11 @@
 
             for half in (0, 1):
                 cross(0, half, a.at[mine(half)]).start()
-            for kind in (0, 1):
-                turn(kind, 2)
             for half in (0, 1):
                 cross(0, half, a.at[mine(half)]).wait_recv()
                 ar_t[halves[half], :] = add_low(a[mine(half), :], ar_xy1[halves[half], :])
                 cross(1, half, ar_t.at[halves[half]]).start()
-            for kind in (0, 1):
-                send1(kind, LOCAL - 1)
+            one(3)
             for half in (0, 1):
                 cross(1, half, ar_t.at[halves[half]]).wait()
                 ar_t[halves[half], :] = add_low(ar_t[halves[half], :], ar_xy2[halves[half], :])
@@ -1158,11 +1073,100 @@
                         def _():
                             along(flow, zz, slot).wait_send()
 
-        pl.run_scoped(shared, V((TOTAL, D), BF16))
+        pl.run_scoped(shared, V((TOTAL, D), BF16), V((MB, T, D), BF16))
+
+    def body(wg_b, wg_i, act_s, gh_s, x_s, gp_s, xp):
+        def fetch(e, which):
+            pairs = ((act, act_s), (gp, gp_s), (xr, x_s), (gh, gh_s))
+            return [
+                pltpu.make_async_copy(pairs[i][0].at[e], pairs[i][1], o_sem.at[i]) for i in which
+            ]
+
+        def pull(e, which):
+            for copy in fetch(e, which):
+                copy.start()
+
+        def ready(e, which):
+            for copy in fetch(e, which):
+                copy.wait()
+
+        pull(0, (0, 1, 2, 3))
+
+        def one(e):
+            def back_block(k, side):
+                at = pl.ds(pl.multiple_of((2 * k + side) * PART, 128), PART)
+                return dot(act_s[:, at], gp_s[...], TN)
+
+            ready(e, (0, 1))
+
+            if e > 0:
+                core_copy(0, e - 1, wg_b).wait_send()
+
+            def other_b(k, carry):
+                wg_b[k] = back_block(k, 1 - c).astype(BF16)
+                return carry
+
+            lax.fori_loop(0, 4, other_b, 0)
+            core_copy(0, e, wg_b).start()
+            ready(e, (2, 3))
+            for side in (0, 1):
+                for k in range(4):
+                    band = (2 * k + side) * BAND
+                    xp[side, :, k * BAND : (k + 1) * BAND] = x_s[:, band : band + BAND]
+
+            if e > 0:
+                core_copy(1, e - 1, wg_i).wait_send()
+
+            def other_i(f, carry):
+                at = pl.ds(pl.multiple_of(f * CHUNK, 128), CHUNK)
+                grad = dot(xp[1 - c], gh_s[:, at], TN).astype(BF16)
+                for k in range(4):
+                    wg_i[k, :, at] = grad[k * BAND : (k + 1) * BAND]
+                return carry
+
+            lax.fori_loop(0, 4, other_i, 0)
+            core_copy(1, e, wg_i).start()
+            core_copy(0, e, wg_b).wait_recv()
+
+            def own_b(k, carry):
+                core_b[e, k] = (core_b[e, k].astype(F32) + back_block(k, c)).astype(BF16)
+                return carry
+
+            lax.fori_loop(0, 4, own_b, 0)
+
+            send1(0, e)
+            if e < LOCAL - 1:
+                pull(e + 1, (0, 1))
+
+            core_copy(1, e, wg_i).wait_recv()
+
+            def own_i(f, carry):
+                at = pl.ds(pl.multiple_of(f * CHUNK, 128), CHUNK)
+                grad = dot(xp[c], gh_s[:, at], TN)
+                for k in range(4):
+                    core_i[e, k, :, at] = (
+                        core_i[e, k, :, at].astype(F32) + grad[k * BAND : (k + 1) * BAND]
+                    ).astype(BF16)
+                return carry
+
+            lax.fori_loop(0, 4, own_i, 0)
+
+            send1(1, e)
+            if e < LOCAL - 1:
+                pull(e + 1, (2, 3))
+
+        one(0)
+        pl.run_scoped(
+            functools.partial(attention_grads, one),
+            V((MB, T, 3 * D), BF16), V((MB, T, D), BF16), V((MB, T, D), BF16), V((EXTRA, D), F32),
+        )
+        core_copy(0, LOCAL - 1, wg_b).wait_send()
+        core_copy(1, LOCAL - 1, wg_i).wait_send()
 
     pl.run_scoped(
-        attention_grads,
-        V((MB, T, 3 * D), BF16), V((MB, T, D), BF16), V((MB, T, D), BF16), V((MB, T, D), BF16), V((EXTRA, D), F32),
+        body,
+        V((4, PART, D), BF16), V((4, BAND, HIDDEN), BF16), V((rows, HIDDEN), BF16), V((rows, HIDDEN), BF16),
+        V((rows, D), BF16), V((rows, D), BF16), V((2, rows, D // 2), BF16),
     )
 
     def place(zz):
@@ -1192,14 +1196,18 @@
 
     to_partner(ar_t, 0, z).start()
     for mb in range(MB):
-        def image_out(base):
+        def image_out(base, quad_s, low):
+            quad = [quad_s.at[i] for i in range(NZ)]
             fetch = pltpu.make_async_copy(resid.at[mb], base, l_sem.at[5])
             fetch.start()
-            load_item(1 + mb)
+            load_item(quad, 1 + mb)
             fetch.wait()
-            block_o[mb] = (base[...] + quad_sum()).astype(BF16)
-
-        pl.run_scoped(image_out, V((T, D), F32))
+            low[...] = (base[...] + quad_sum(quad)).astype(BF16)
+            store = pltpu.make_async_copy(low, block_o.at[mb], l_sem.at[7])
+            store.start()
+            store.wait()
+
+        pl.run_scoped(image_out, V((T, D), F32), V((NZ, T, D), BF16), V((T, D), BF16))
     for h in range(NZ - 1):
         for up in (True, False):
             source = z - h - 1 if up else z + h + 1
@@ -1218,11 +1226,9 @@
                 @pl.when(leaves(up, h + 1))
                 def _():
                     spread(up, h + 1).start()
-    for kind in (0, 1):
-        turn(kind, 3)
-    for kind in (0, 1):
-        for e in range(LOCAL):
-            finish(kind, e)
+        if h < 2:
+            for kind in (0, 1):
+                turn(kind, 2 + h)
     own_share.wait()
     for k in range(NZ):
         zz = lax.rem(z + k, NZ)
@@ -1242,8 +1248,8 @@
         for e in range(LOCAL):
             for slot in (0, 1):
                 hop1(kind, e, slot).wait_send()
-            hop2(kind, e).wait_send()
-            result(kind, e).wait()
+            hop2(kind, e).wait()
+            keep(kind, e).wait()
 
 
 def grads_call(*operands):
@@ -1253,11 +1259,13 @@
     V = pltpu.VMEM
     DMA = pltpu.SemaphoreType.DMA
     outs = [
-        (S((MB, T, D), BF16), vm),
+        (S((MB, T, D), BF16), hb),
         (S((MB, T, D), F32), hb),
         (S((TOTAL, D), BF16), hb),
+        (S((LOCAL, PART, D), BF16), hb),
         (S((LOCAL, BAND, HIDDEN), BF16), hb),
         (S((LOCAL, PART, D), BF16), hb),
+        (S((LOCAL, BAND, HIDDEN), BF16), hb),
         (S((3, NZ, T, D), BF16), hb),
     ]
     return pl.pallas_call(
@@ -1268,18 +1276,17 @@
         scratch_shapes=[
             V((LOCAL, 4, PART, D), BF16), V((LOCAL, 4, BAND, HIDDEN), BF16),
             V((LOCAL, 2, PART, D), BF16), V((LOCAL, 2, BAND, HIDDEN), BF16),
-            V((LOCAL, PART, D), BF16), V((LOCAL, BAND, HIDDEN), BF16),
             V((NZ, SHARE, D), BF16), V((2, NZ - 1, SHARE, D), BF16),
             V((SHARE, D), BF16), V((SHARE, D), BF16), V((SHARE, D), BF16),
-            V((NZ, MB, 8, T), F32), V((NZ, T, D), BF16),
+            V((NZ, MB, 8, T), F32),
             DMA((2, LOCAL)), DMA((2, LOCAL)), DMA((2, LOCAL, 2)), DMA((2, LOCAL, 2)), DMA((2, LOCAL)), DMA((2, LOCAL)),
             DMA((3, NZ - 1)), DMA((3, NZ - 1)), DMA((NZ - 1,)), DMA((NZ - 1,)),
             DMA((NZ,)), DMA((NZ,)), DMA((2, NZ - 1)), DMA((2, NZ - 1)), DMA((2, 2)), DMA((2, 2)),
             DMA((2, NZ - 1)), DMA((2, NZ - 1)), DMA((NZ,)), DMA((NZ,)),
-            DMA((8,)), DMA((13,)), DMA((2, LOCAL)),
+            DMA((8,)), DMA((14,)), DMA((2, LOCAL)),
         ],
         compiler_params=pltpu.CompilerParams(
-            collective_id=2, has_side_effects=True, vmem_limit_bytes=60 << 20
+            collective_id=2, has_side_effects=True, vmem_limit_bytes=63 << 20
         ),
         name="grads",
     )(*operands)
@@ -1303,7 +1310,7 @@
     (qkv, mixed, resid, rp, gg, bb, bi, xr, gp, act, gh, pb, pg, pg0) = dispatch_call(
         tok, rt, vec, w_qkv, w_out, wrt, b_in, b_back, dout, w_in, w_back
     )
-    block, ig, ar, wi, wb, _ = grads_call(
+    block, ig, ar, kb, ki, lb, li, _ = grads_call(
         vec, rt, wrt, bb, bi, rp, tok, dout, w_qkv, w_out, qkv, mixed, resid, gg, xr, gp, act, gh, pb, pg, pg0
     )
     dp, z = lax.axis_index("dp"), lax.axis_index("expert")
@@ -1326,9 +1333,9 @@
         ext[5],
         ext[6],
         ext[8 : 8 + NZ * LOCAL].T,
-        wi.astype(F32),
+        ki.astype(F32) + li.astype(F32),
         bi_grad,
-        wb.astype(F32),
+        kb.astype(F32) + lb.astype(F32),
         bb_grad,
     )
 

time: 435 us -> 397 us (0.913); the launches traced: 434 us -> 389 us
  Pallas kernels: 409 us -> 364 us
    pallas_call x1, Pallas kernels: 255 us -> 219 us  [grads_call(): pl.pallas_call(grads_kernel, out_shape=[o[0] for o in outs], in_specs=[vm...]
    pallas_call x1, Pallas kernels: 154 us -> 144 us  [dispatch_call(): pl.pallas_call(dispatch_kernel, out_shape=[o[0] for o in outs], in_specs=...]
    add x0 -> x2, other arithmetic: none -> 8.47 us  [the longest x1 5.45 us: fast_body(): kb.astype(F32) + lb.astype(F32)]
    convert_element_type x2 -> x0, other arithmetic: 5.36 us -> none  [the longest x1 2.77 us: fast_body(): wi.astype(F32)]
where the time goes in v3:
time: 397 us; the launch traced here: 389 us
  Pallas kernels  364 us (92%)
  other arithmetic  14.4 us (4%)
  local copies, waits for them, and re-layouts  10.5 us (3%)
    pallas_call x1, Pallas kernels, grads_call(): pl.pallas_call(grads_kernel, out_shape=[o[0] for o in outs], in_specs=[vm...  219 us
    pallas_call x1, Pallas kernels, dispatch_call(): pl.pallas_call(dispatch_kernel, out_shape=[o[0] for o in outs], in_specs=...  144 us

profile of v3, /device:TPU:0, one launch (start us, length us, event | category | flops | bytes accessed | tf_op | source)
XLA Modules:
  0.0 389.4 jit_solution(15898343840886029628)
XLA Ops:
  0.6 0.0 copy-start.3
  0.7 0.0 copy-start.5
  0.7 0.0 copy-start.7
  0.7 0.0 copy-start.8
  0.7 0.0 copy-start.9
  0.7 0.0 copy-start.10
  0.7 0.0 copy-start.11
  0.7 0.0 copy-start.6
  0.7 0.0 copy-start.12
  0.7 1.2 reshape.60
  2.0 0.9 pad.17.tok
  2.9 0.0 copy-done.3
  2.9 0.1 reshape.61
  3.0 0.9 pad.18.dout
  3.9 0.0 copy-done.5
  3.9 0.6 pad_bitcast_fusion.wrt
  4.5 0.0 copy-done.7
  4.5 0.0 copy-done.8
  4.5 0.0 copy-done.9
  4.6 0.0 copy-done.10
  4.6 0.0 copy-done.11
  4.6 0.0 copy-done.6
  4.6 0.6 stack.23.vec
  5.3 0.0 copy-done.12
  5.3 0.1 reshape.57
  5.4 0.6 pad.15.rt
  6.0 144.5 %dispatch.1 = (bf16[2,208,2304]{2,1,0:T(8,128)(2,1)}, bf16[2,208,768]{2,1,0:T(8,128)(2,1)}, f32[2,208,768]{2,1,0:T(8,128)}, f32[2,32,208]{2,1,0:T(8,128)}, f32[4...) custom-call(bf16[2,208,768]{2,1,0:T(8,128)(2,1)} %pad.17.tok, ...), custom_call_target="tpu_custom_call" | custom-call | tf_op jit(solution)/shard_map/dispatch/pallas_call | solution.py:697
  150.4 219.1 %grads.1 = (bf16[2,208,768]{2,1,0:T(8,128)(2,1)}, f32[2,208,768]{2,1,0:T(8,128)}, bf16[3200,768]{1,0:T(8,128)(2,1)}, bf16[4,384,768]{2,1,0:T(8,128)(2,1)}, bf16[...) custom-call(f32[8,768]{1,0:T(8,128)} %stack.23.vec, ...), custom_call_target="tpu_custom_call" | custom-call | tf_op jit(solution)/shard_map/grads/pallas_call | solution.py:1271
  369.5 0.0 copy-start
  369.5 0.0 copy-start.1
  369.6 0.0 slice-start
  369.6 5.4 %convert_add_fusion = f32[4,384,768]{2,1,0:T(8,128)} fusion(bf16[4,384,768]{2,1,0:T(8,128)(2,1)} %get-tuple-element.56, bf16[4,384,768]{2,1,0:T(8,128)(2,1)} %get-tuple-element.55), kind=kLoop, calls=%fused_computation | loop fusion | flops 3538944 | bytes 9437184 | tf_op jit(solution)/shard_map/add | solution.py:1338
  375.0 0.0 slice-start.1
  375.0 0.0 copy-done
  375.0 0.0 copy-done.1
  375.0 3.0 convert_add_fusion.1
  378.0 0.0 slice-done
  378.0 0.0 slice-done.1
  378.1 1.8 slice_convert_fusion
  379.9 0.0 copy-start.2
  379.9 3.2 maximum_convert_fusion
  383.1 0.0 copy-done.2
  383.1 0.0 copy-start.4
  383.1 0.1 slice.52
  383.1 1.1 reshape.63
  384.3 0.0 copy-done.4
  384.3 0.9 reshape.62
  385.3 1.0 slice_convert_fusion.1
  386.3 0.6 constant_dynamic-slice_fusion.1
  386.9 0.6 constant_dynamic-slice_fusion
  387.5 0.6 slice_reduce_fusion
  388.1 0.7 dynamic-slice.2
  388.8 0.6 slice.69
  (11 shorter events, 0.1 us)
Async XLA Ops:
  0.6 2.2 copy-start.3
  0.7 3.2 copy-start.5
  0.7 3.9 copy-start.7
  0.7 3.8 copy-start.8
  0.7 3.9 copy-start.9
  0.7 3.9 copy-start.10
  0.7 3.9 copy-start.11
  0.7 3.9 %copy-start.6 = (f32[2,768]{1,0:T(2,128)S(1)}, f32[2,768]{1,0:T(2,128)}, u32[]{:S(2)}) copy-start(f32[2,768]{1,0:T(2,128)} %param.21) | copy-start | bytes 18436
  0.7 4.5 %copy-start.12 = (s32[394,2]{0,1:T(2,128)S(1)}, s32[394,2]{0,1:T(2,128)}, u32[]{:S(2)}) copy-start(s32[394,2]{0,1:T(2,128)} %param.17) | copy-start | bytes 9460
  369.5 5.5 %copy-start = (bf16[4,96,3072]{2,1,0:T(8,128)(2,1)S(1)}, bf16[4,96,3072]{2,1,0:T(8,128)(2,1)}, u32[]{:S(2)}) copy-start(bf16[4,96,3072]{2,1,0:T(8,128)(2,1)} %get-tuple-element.53) | copy-start | bytes 7077892
  369.5 5.5 %copy-start.1 = (bf16[4,96,3072]{2,1,0:T(8,128)(2,1)S(1)}, bf16[4,96,3072]{2,1,0:T(8,128)(2,1)}, u32[]{:S(2)}) copy-start(bf16[4,96,3072]{2,1,0:T(8,128)(2,1)} %get-tuple-element.54) | copy-start | bytes 7077892
  369.6 8.5 %slice-start = ((s8[4915200]{0:T(1024)(128)(4,1)}), s8[4194304]{0:T(1024)(128)(4,1)S(1)}, s32[]{:S(2)}) async-start(s8[4915200]{0:T(1024)(128)(4,1)} %bitcast.13), calls=%async_computation | async-start | bytes 8388608
  375.0 3.0 slice-start.1
  379.9 3.2 copy-start.2
  383.1 1.2 copy-start.4

commit v4 on v3

--- a/solution.py
+++ b/solution.py
@@ -288,7 +288,9 @@
 PAIRS = HEADS // 2
 T = 208
 KEYS = 256
+CAP = 41
 CAP_ROWS = 48
+PACKED = 176
 ROWS = NZ * CAP_ROWS
 CHUNK = 768
 MESH = pl.DeviceIdType.MESH
@@ -319,15 +321,6 @@
     return raised / jnp.sum(raised, axis=-1, keepdims=True)
 
 
-def route_table(rt_ref, mb):
-    row = lax.broadcasted_iota(jnp.int32, (32, T), 0)
-    part = lax.rem(row, 8)
-    expert = jnp.where(part < LOCAL, (row // 8) * LOCAL + part, -7)
-    first = rt_ref[mb, 0:1, :]
-    second = rt_ref[mb, 1:2, :]
-    return jnp.logical_or(expert == first, expert == second), part < LOCAL
-
-
 def route_softmax(logits, real):
     logits = jnp.where(real, logits, -1e30)
     raised = jnp.exp(logits - jnp.max(logits, axis=0, keepdims=True))
@@ -343,9 +336,9 @@
 
 
 def dispatch_kernel(
-    tok, rt, vec, wqkv, wout, wrt, b_in, b_back, dout, w_in, w_back,
-    qkv_o, mixed_o, resid_o, rp_o, gg_o, bb_o, bi_o, x_o, gp_o, act_o, gh_o, pb_o, pg_o, home_o,
-    gi, gd, sg, qkv_s, mixed_s, inner_s, xs, gs, cs, rgs, ggs, wb1, wb2, act_st, gh_st, acc_o, acc_g,
+    tok, dout, routes, v0, v1, v2, v3, v4, qv, wqkv, wout, wrt, b_in, b_back, w_in, w_back,
+    vec, tab_o, tw_o, qkv_o, mixed_o, resid_o, rp_o, gg_o, bb_o, bi_o, dw_o, x_o, gp_o, act_o, gh_o, pb_o, pg_o, home_o,
+    gi, gd, sl, sg, dense, qkv_s, mixed_s, inner_s, xs, gs, cs, rgs, ggs, wb1, wb2, act_st, gh_st, acc_o, acc_g,
     os_, grs, pb_s, pg_s,
     send_sem, recv_sem, d_sem, w_sem, st_sem, x_sem, p_sem, h_send, h_recv,
 ):
@@ -353,20 +346,21 @@
     z = lax.axis_index("expert")
 
     def item_ref(kind, source, mb):
-        return (gd, sg, gi)[kind].at[source, mb]
-
-    def hop(up, kind, mb, h):
-        source = z - h if up else z + h
-        target = z + 1 if up else z - 1
+        return (gd, sg, gi, sl)[kind].at[source, mb]
+
+    def copy_of(up, kind, mb, h, source, target, packed):
         index = (0 if up else 1, kind * MB + mb, h)
+        dst = item_ref(kind, source, mb)
+        src = dst
+        if packed:
+            src, dst = dense.at[kind // 2, mb, h], dst.at[0:PACKED]
         return pltpu.make_async_remote_copy(
-            src_ref=item_ref(kind, source, mb),
-            dst_ref=item_ref(kind, source, mb),
-            send_sem=send_sem.at[index],
-            recv_sem=recv_sem.at[index],
-            device_id=(dp, target),
-            device_id_type=MESH,
-        )
+            src_ref=src, dst_ref=dst, send_sem=send_sem.at[index], recv_sem=recv_sem.at[index],
+            device_id=(dp, target), device_id_type=MESH,
+        )
+
+    def hop(up, kind, mb, h, packed):
+        return copy_of(up, kind, mb, h, z - h if up else z + h, z + 1 if up else z - 1, packed)
 
     def leaves(up, h):
         return jnp.logical_and(z - h >= 0, z + 1 < NZ) if up else jnp.logical_and(z + h < NZ, z >= 1)
@@ -374,27 +368,52 @@
     def arrives(up, h):
         return (z - h - 1 >= 0) if up else (z + h + 1 < NZ)
 
+    def to_end(up):
+        return (z + 1 == NZ - 1) if up else (z == 1)
+
+    def at_end(up):
+        return (z == NZ - 1) if up else (z == 0)
+
+    def each(kind, condition, where, action):
+        if kind in (0, 2):
+            @pl.when(jnp.logical_and(condition, where))
+            def _():
+                action(True)
+
+            @pl.when(jnp.logical_and(condition, jnp.logical_not(where)))
+            def _():
+                action(False)
+        else:
+            @pl.when(condition)
+            def _():
+                action(False)
+
     def start(kind, mb, h):
         for up in (True, False):
-            @pl.when(leaves(up, h))
-            def _():
-                hop(up, kind, mb, h).start()
+            def go(packed):
+                if packed:
+                    source = z - h if up else z + h
+                    slots = sl[source, mb, NZ - 1 if up else 0]
+                    row = lax.broadcasted_iota(jnp.int32, (PACKED, T), 0)
+                    owner = row // CAP
+                    wanted = jnp.full((PACKED, T), -5.0, F32)
+                    for e in range(LOCAL):
+                        wanted = jnp.where(owner == e, slots[e : e + 1, :], wanted)
+                    chosen = (wanted == (row - owner * CAP).astype(F32)).astype(F32).astype(BF16)
+                    dense[kind // 2, mb, h] = dot(chosen, item_ref(kind, source, mb)[...]).astype(BF16)
+                hop(up, kind, mb, h, packed).start()
+
+            each(kind, leaves(up, h), to_end(up), go)
 
     def pass_on(kind, mb, h):
         for up in (True, False):
-            @pl.when(arrives(up, h))
-            def _():
+            def take(packed):
                 source = z - h - 1 if up else z + h + 1
-                index = (0 if up else 1, kind * MB + mb, h)
-                ref = item_ref(kind, source, mb)
-                pltpu.make_async_remote_copy(
-                    src_ref=ref, dst_ref=ref, send_sem=send_sem.at[index], recv_sem=recv_sem.at[index],
-                    device_id=(dp, z - 1 if up else z + 1), device_id_type=MESH,
-                ).wait_recv()
-            if h + 1 < NZ - 1:
-                @pl.when(leaves(up, h + 1))
-                def _():
-                    hop(up, kind, mb, h + 1).start()
+                copy_of(up, kind, mb, h, source, z - 1 if up else z + 1, packed).wait_recv()
+
+            each(kind, arrives(up, h), at_end(up), take)
+        if h + 1 < NZ - 1:
+            start(kind, mb, h + 1)
 
     def weights(n, slot):
         e = lax.rem(n, 16) // 4
@@ -405,17 +424,42 @@
             pltpu.make_async_copy(w_back.at[e, cols, :], wb2.at[slot], w_sem.at[1, slot]),
         )
 
-    own = [pltpu.make_async_copy(dout.at[mb], gd.at[z, mb], d_sem.at[mb]) for mb in range(MB)]
-    for copy in own:
+    for copy in weights(0, 0):
         copy.start()
+    for ref in (gi, gd):
+        for source in range(NZ):
+            for mb in range(MB):
+                ref[source, mb, PACKED:T, :] = jnp.zeros((T - PACKED, D), BF16)
+    for row, ref in enumerate((v0, v1, v2, v3, v4)):
+        vec[row : row + 1, :] = ref[...].reshape(1, D)
+    vec[5:7, :] = qv[...]
+    vec[7:8, :] = jnp.zeros((1, D), F32)
+    lane = lax.broadcasted_iota(jnp.int32, (1, 32), 1)
+    part = lax.rem(lane, 8)
+    expert_of = jnp.where(part < LOCAL, (lane // 8) * LOCAL + part, -7)
+    chosen_all = jnp.logical_or(routes[:, 0:1] == expert_of, routes[:, 1:2] == expert_of)
+    chosen_all = chosen_all.astype(F32).astype(BF16)
+    token = lax.broadcasted_iota(jnp.int32, (MB * SEQ, T), 0)
+    column = lax.broadcasted_iota(jnp.int32, (MB * SEQ, T), 1)
+    for mb in range(MB):
+        here = jnp.logical_and(token == column + mb * SEQ, column < SEQ).astype(F32).astype(BF16)
+        ahead = jnp.logical_and(token >= mb * SEQ, token < column + mb * SEQ).astype(F32).astype(BF16)
+        table = dot(chosen_all, here, TN)
+        tab_o[mb] = table
+        slots = jnp.where(table > 0.5, dot(chosen_all, ahead, TN), -1.0)
+        for p in range(NZ):
+            sl[z, mb, p] = slots[8 * p : 8 * p + 8, :]
+        tw_o[mb] = dot(here, tok[...], TN).astype(BF16)
+        gd[z, mb] = dot(here, dout[...], TN).astype(BF16)
     barrier = pltpu.get_barrier_semaphore()
     for d in range(1, NZ):
         pl.semaphore_signal(barrier, inc=1, device_id=(dp, lax.rem(z + d, NZ)), device_id_type=MESH)
     pl.semaphore_wait(barrier, NZ - 1)
+    start(3, 0, 0)
+    start(0, 0, 0)
+    start(3, 1, 0)
+    own = [pltpu.make_async_copy(gd.at[z, mb], dw_o.at[mb], d_sem.at[mb]) for mb in range(MB)]
     for copy in own:
-        copy.wait()
-    start(0, 0, 0)
-    for copy in weights(0, 0):
         copy.start()
 
     qkv_s[T:KEYS, :] = jnp.zeros((KEYS - T, 3 * D), BF16)
@@ -423,7 +467,7 @@
     bi_o[...] = jnp.zeros_like(bi_o)
 
     def forward(mb, carry):
-        x = tok[mb].astype(F32)
+        x = tw_o[mb].astype(F32)
         normed = (normal(x)[0] * vec[0:1] + vec[1:2]).astype(BF16)
         for c in range(3):
             cols = slice(c * D, (c + 1) * D)
@@ -451,18 +495,12 @@
         resid_o[mb] = resid
         inner = (normal(resid)[0] * vec[2:3] + vec[3:4]).astype(BF16)
         gi[z, mb] = inner
-        table, real = route_table(rt, mb)
+        real = lax.rem(lax.broadcasted_iota(jnp.int32, (32, T), 0), 8) < LOCAL
         probs = route_softmax(dot(wrt[...], inner, NT), real)
         rp_o[mb] = probs
-        earlier = (
-            lax.broadcasted_iota(jnp.int32, (T, T), 0) < lax.broadcasted_iota(jnp.int32, (T, T), 1)
-        ).astype(F32).astype(BF16)
-        before = dot(table.astype(F32).astype(BF16), earlier)
-        slots = jnp.where(table, before, -1.0)
-        gates = jnp.where(table, probs, 0.0)
+        gates = tab_o[mb] * probs
         for p in range(NZ):
-            sg[z, mb, 0, p] = slots[8 * p : 8 * p + 8, :]
-            sg[z, mb, 1, p] = gates[8 * p : 8 * p + 8, :]
+            sg[z, mb, p] = gates[8 * p : 8 * p + 8, :]
 
         @pl.when(mb == 0)
         def _():
@@ -473,8 +511,9 @@
 
     lax.fori_loop(0, MB, forward, 0)
     for h in range(NZ - 1):
-        for kind in range(3):
+        for kind in (3, 0, 1, 2):
             pass_on(kind, 0, h)
+        pass_on(3, 1, h)
     for kind in range(3):
         start(kind, 1, 0)
 
@@ -485,9 +524,16 @@
                 pass_on(kind, 1, 2)
 
         def spread(src, carry):
-            pick = pick_matrix(sg[src, mb, 0, z])
-            gate = sg[src, mb, 1, z]
-            low = pick.astype(BF16)
+            pick = pick_matrix(sl[src, mb, z])
+            gate = sg[src, mb, z]
+            row = lax.broadcasted_iota(jnp.int32, (ROWS, T), 0)
+            owner = row // CAP_ROWS
+            place = row - owner * CAP_ROWS
+            unpack = jnp.logical_and(
+                place < CAP, lax.broadcasted_iota(jnp.int32, (ROWS, T), 1) == owner * CAP + place
+            ).astype(F32)
+            packed = jnp.logical_and(jnp.logical_or(z == 0, z == NZ - 1), src != z)
+            low = jnp.where(packed, unpack, pick).astype(BF16)
             rows_x = dot(low, gi[src, mb]).astype(BF16)
             rows_c = dot(low, gd[src, mb])
             at = pl.ds(pl.multiple_of(mb * ROWS + src * CAP_ROWS, 16), CAP_ROWS)
@@ -603,7 +649,7 @@
             own_home().wait()
 
         def gather(src, carry):
-            pick = pick_matrix(sg[src, mb, 0, z])
+            pick = pick_matrix(sl[src, mb, z])
             low = pick.astype(BF16)
             pb_s[src] = dot(low, os_[src], TN).astype(BF16)
             pg_s[src] = dot(low, grs[src], TN).astype(BF16)
@@ -644,7 +690,7 @@
         )
 
     def own_home():
-        return pltpu.make_async_copy(pg_s.at[z], home_o.at[z], d_sem.at[0])
+        return pltpu.make_async_copy(pg_s.at[z], home_o.at[z], d_sem.at[MB])
 
     gg_o[...] = jnp.zeros_like(gg_o)
     lax.fori_loop(0, MB, micro, 0)
@@ -662,13 +708,16 @@
             src_ref=home_o.at[source], dst_ref=home_o.at[source], send_sem=h_send.at[d - 1],
             recv_sem=h_recv.at[d - 1], device_id=(dp, source), device_id_type=MESH,
         ).wait_recv()
+    for copy in own:
+        copy.wait()
     for mb in range(MB):
-        for kind in range(3):
+        for kind in range(4):
             for h in range(NZ - 1):
                 for up in (True, False):
-                    @pl.when(leaves(up, h))
-                    def _():
-                        hop(up, kind, mb, h).wait_send()
+                    each(
+                        kind, leaves(up, h), to_end(up),
+                        lambda packed: hop(up, kind, mb, h, packed).wait_send(),
+                    )
 
 
 def dispatch_call(*operands):
@@ -677,6 +726,9 @@
     S = jax.ShapeDtypeStruct
     rows = MB * ROWS
     outs = [
+        (S((8, D), F32), vm),
+        (S((MB, 32, T), F32), vm),
+        (S((MB, T, D), BF16), vm),
         (S((MB, T, 3 * D), BF16), vm),
         (S((MB, T, D), BF16), vm),
         (S((MB, T, D), F32), vm),
@@ -684,6 +736,7 @@
         (S((NZ, MB, 8, T), F32), vm),
         (S((LOCAL, D), F32), vm),
         (S((LOCAL, 4 * CHUNK), F32), vm),
+        (S((MB, T, D), BF16), hb),
         (S((LOCAL, rows, D), BF16), hb),
         (S((LOCAL, rows, D), BF16), hb),
         (S((LOCAL, rows, 4 * CHUNK), BF16), hb),
@@ -697,10 +750,10 @@
     return pl.pallas_call(
         dispatch_kernel,
         out_shape=[o[0] for o in outs],
-        in_specs=[vm] * 8 + [hb] * 3,
+        in_specs=[vm] * 14 + [hb] * 2,
         out_specs=[o[1] for o in outs],
         scratch_shapes=[
-            V((NZ, MB, T, D), BF16), V((NZ, MB, T, D), BF16), V((NZ, MB, 2, NZ, 8, T), F32),
+            V((NZ, MB, T, D), BF16), V((NZ, MB, T, D), BF16), V((NZ, MB, NZ, 8, T), F32), V((NZ, MB, NZ, 8, T), F32), V((2, MB, NZ - 1, PACKED, D), BF16),
             V((KEYS, 3 * D), BF16), V((T, D), BF16), V((8, 128), F32),
             V((LOCAL, rows, D), BF16), V((LOCAL, rows, D), BF16), V((LOCAL, ROWS, D), BF16),
             V((LOCAL, ROWS, 128), F32), V((NZ, ROWS, 128), F32),
@@ -709,7 +762,7 @@
             V((ROWS, D), F32), V((ROWS, D), F32),
             V((NZ, ROWS, D), BF16), V((NZ, ROWS, D), BF16),
             V((NZ, T, D), BF16), V((NZ, T, D), BF16),
-            DMA((2, 3 * MB, NZ - 1)), DMA((2, 3 * MB, NZ - 1)), DMA((MB,)), DMA((2, 2)), DMA((2, 2)),
+            DMA((2, 4 * MB, NZ - 1)), DMA((2, 4 * MB, NZ - 1)), DMA((MB + 1,)), DMA((2, 2)), DMA((2, 2)),
             DMA((2,)), DMA((2, NZ)), DMA((NZ - 1,)), DMA((NZ - 1,)),
         ],
         compiler_params=pltpu.CompilerParams(
@@ -732,7 +785,7 @@
 
 
 def grads_kernel(
-    vec, rt, wrt, bb, bi, rp,
+    vec, tab, wrt, bb, bi, rp,
     tok, dout, wqkv, wout, qkv, mixed, resid, gg, xr, gp, act, gh, pb, pg, pg0,
     block_o, ig_o, ar_o, kb_o, ki_o, lb_o, li_o, land_o,
     core_b, core_i, st1_b, st1_i, ar_core, ar_z, ar_xy1, ar_xy2, ar_t,
@@ -797,9 +850,6 @@
     def quad_sum(quad):
         parts = [ref[...].astype(F32) for ref in quad]
         return (parts[0] + parts[1]) + (parts[2] + parts[3])
-
-    def middle(arr, flow, mb, dest):
-        return jnp.logical_and(z > dest, z < NZ - 1) if flow == 0 else jnp.logical_and(z < dest, z > 0)
 
     cores, lands1, lands2, keeps = (core_b, core_i), (st1_b, st1_i), (lb_o, li_o), (kb_o, ki_o)
 
@@ -879,9 +929,8 @@
                 ]
                 for fetch in fetches:
                     fetch.start()
-                table, _ = route_table(rt, mb)
                 gates = jnp.concatenate([ggr[p, mb] for p in range(NZ)], axis=0)
-                g = jnp.where(table, gates, 0.0)
+                g = tab[mb] * gates
                 probs = rp[mb]
                 gl = (probs * (g - jnp.sum(probs * g, axis=0, keepdims=True))).astype(BF16)
                 fetches[3].wait()
@@ -1015,25 +1064,25 @@
                 def _():
                     along(1, NZ - 1 - j, NZ - 2 - j).start()
 
-            def sum_step(j):
-                for flow, dest in ((0, j), (1, NZ - 1 - j)):
-                    slot = dest if flow == 0 else dest - 1
-                    if 0 <= slot < NZ - 1:
-                        passes = middle(0, flow, 0, dest)
-
-                        @pl.when(jnp.logical_or(passes, z == dest))
-                        def _():
-                            along(flow, dest, slot).wait_recv()
-                            a[share(c, dest), :] = add_low(a[share(c, dest), :], ar_z[flow, slot])
-
-                        @pl.when(passes)
-                        def _():
-                            along(flow, dest, slot).start()
+            def sum_one(flow, dest, at):
+                slot = dest if flow == 0 else dest - 1
+
+                @pl.when(z == at)
+                def _():
+                    along(flow, dest, slot).wait_recv()
+                    a[share(c, dest), :] = add_low(a[share(c, dest), :], ar_z[flow, slot])
+                    if at != dest:
+                        along(flow, dest, slot).start()
 
             one(2)
-            for j in range(NZ):
-                sum_step(j)
-                if j == 1:
+            for step, order in enumerate((
+                ((0, 0, 2), (1, 3, 1)),
+                ((0, 1, 2), (1, 3, 2), (1, 2, 1), (0, 0, 1)),
+                ((0, 2, 2), (1, 2, 2), (1, 1, 1), (0, 1, 1), (0, 0, 0), (1, 3, 3)),
+            )):
+                for flow, dest, at in order:
+                    sum_one(flow, dest, at)
+                if step == 1:
                     for kind in (0, 1):
                         turn(kind, 1)
 
@@ -1291,53 +1340,134 @@
         name="grads",
     )(*operands)
 
+
+def finish_kernel(
+    ar, kb, ki, lb, li, block, ig,
+    block_o, ig_o, g1_o, s1_o, qkv_o, qv_o, wout_o, bout_o, g2_o, s2_o, route_o, wi_o, bi_o, wb_o, bb_o,
+    ar_s, kb_s, ki_s, lb_s, li_s, block_s, ig_s, wide, narrow, out_i, out_b, tall,
+    in_sem, out_sem,
+):
+    dp = lax.axis_index("dp")
+    z = lax.axis_index("expert")
+
+    def fetch(src, dst, i):
+        copy = pltpu.make_async_copy(src, dst, in_sem.at[i])
+        copy.start()
+        return copy
+
+    back = [(fetch(kb.at[e], kb_s.at[e], e), fetch(lb.at[e], lb_s.at[e], 4 + e)) for e in range(LOCAL)]
+    ahead = [(fetch(ki.at[e], ki_s.at[e], 8 + e), fetch(li.at[e], li_s.at[e], 12 + e)) for e in range(LOCAL)]
+    dense = [
+        fetch(ar.at[i * D : (i + 1) * D], ar_s.at[i * D : (i + 1) * D], 16 + i) for i in range(4)
+    ]
+    few = fetch(ar.at[4 * D : TOTAL], ar_s.at[4 * D : TOTAL], 20)
+    rows_in = (fetch(block, block_s, 21), fetch(ig, ig_s, 22))
+    sent = []
+
+    def send(src, dst):
+        copy = pltpu.make_async_copy(src, dst, out_sem.at[len(sent)])
+        copy.start()
+        sent.append(copy)
+
+    for pairs, kept, landed, out, dst in ((back, kb_s, lb_s, out_b, wb_o), (ahead, ki_s, li_s, out_i, wi_o)):
+        for e in range(LOCAL):
+            for copy in pairs[e]:
+                copy.wait()
+            out[e] = kept[e].astype(F32) + landed[e].astype(F32)
+            send(out.at[e], dst.at[e])
+    for i in range(4):
+        dense[i].wait()
+        part = ar_s[i * D : (i + 1) * D, :].astype(F32)
+        if i < 3:
+            wide[i] = part
+            send(wide.at[i], qkv_o.at[:, i * D : (i + 1) * D])
+        else:
+            narrow[...] = part
+            send(narrow, wout_o)
+    few.wait()
+    low = ar_s[4 * D : TOTAL, :]
+    ext = low.astype(F32)
+    for row, ref in ((0, g1_o), (1, s1_o), (4, bout_o), (5, g2_o), (6, s2_o)):
+        ref[...] = ext[row]
+    qv_o[...] = ext[2:4]
+    route_o[...] = ext[8 : 8 + NZ * LOCAL]
+
+    def pick(first):
+        at = lax.broadcasted_iota(jnp.int32, (8, EXTRA), 0) + first
+        return dot((at == lax.broadcasted_iota(jnp.int32, (8, EXTRA), 1)).astype(F32).astype(BF16), low)
+
+    base = 24 + 5 * LOCAL * z
+    column = lax.broadcasted_iota(jnp.int32, (D, BAND), 1) + dp * BAND
+    chosen = (column == lax.broadcasted_iota(jnp.int32, (D, BAND), 0)).astype(F32).astype(BF16)
+    bb_o[...] = dot(pick(base).astype(BF16), chosen)[:LOCAL]
+    rows = pick(base + LOCAL * (dp // 2 + 1))
+    bi_o[...] = jnp.where(lax.rem(dp, 2) == 0, rows[:, :PART], rows[:, PART:])[:LOCAL]
+    for copy in rows_in:
+        copy.wait()
+    for mb in range(MB):
+        at = slice(mb * SEQ, (mb + 1) * SEQ)
+        tall[at, :] = block_s[mb].astype(F32)[:SEQ]
+        ig_o[at, :] = ig_s[mb, :SEQ, :]
+    block_o[...] = tall[0 : MB * SEQ, :].astype(BF16)
+    for copy in sent:
+        copy.wait()
+
+
+def finish_call(*operands):
+    vm = pl.BlockSpec(memory_space=pltpu.VMEM)
+    hb = pl.BlockSpec(memory_space=pl.ANY)
+    S = jax.ShapeDtypeStruct
+    V = pltpu.VMEM
+    rows = MB * SEQ
+    vector = (S((D,), F32), vm)
+    outs = [
+        (S((rows, D), BF16), vm),
+        (S((rows, D), F32), vm),
+        vector,
+        vector,
+        (S((D, 3 * D), F32), hb),
+        (S((2, D), F32), vm),
+        (S((D, D), F32), hb),
+        vector,
+        vector,
+        vector,
+        (S((NZ * LOCAL, D), F32), vm),
+        (S((LOCAL, BAND, HIDDEN), F32), hb),
+        (S((LOCAL, PART), F32), vm),
+        (S((LOCAL, PART, D), F32), hb),
+        (S((LOCAL, BAND), F32), vm),
+    ]
+    return pl.pallas_call(
+        finish_kernel,
+        out_shape=[o[0] for o in outs],
+        in_specs=[hb] * 7,
+        out_specs=[o[1] for o in outs],
+        scratch_shapes=[
+            V((TOTAL, D), BF16),
+            V((LOCAL, PART, D), BF16), V((LOCAL, BAND, HIDDEN), BF16), V((LOCAL, PART, D), BF16), V((LOCAL, BAND, HIDDEN), BF16),
+            V((MB, T, D), BF16), V((MB, T, D), F32), V((3, D, D), F32), V((D, D), F32),
+            V((LOCAL, BAND, HIDDEN), F32), V((LOCAL, PART, D), F32), V((400, D), F32),
+            pltpu.SemaphoreType.DMA((23,)), pltpu.SemaphoreType.DMA((12,)),
+        ],
+        compiler_params=pltpu.CompilerParams(vmem_limit_bytes=58 << 20),
+        name="finish",
+    )(*operands)
+
 def fast_body(
     tokens, routes, gain_one, shift_one, w_qkv, qv_bias, w_out, out_bias, gain_two, shift_two,
     w_route, w_in, b_in, w_back, b_back, d_out,
 ):
-    def windows(a):
-        return jnp.pad(a.reshape(MB, SEQ, a.shape[1]), ((0, 0), (0, T - SEQ), (0, 0)))
-
-    tok, dout = windows(tokens), windows(d_out)
-    rt = jnp.pad(
-        jnp.transpose(routes.reshape(MB, SEQ, TOP), (0, 2, 1)),
-        ((0, 0), (0, 8 - TOP), (0, T - SEQ)), constant_values=-1,
-    )
-    vec = jnp.stack(
-        [gain_one, shift_one, gain_two, shift_two, out_bias, qv_bias[0], qv_bias[1], jnp.zeros_like(out_bias)]
-    )
     wrt = jnp.pad(w_route.T.reshape(NZ, LOCAL, D), ((0, 0), (0, 8 - LOCAL), (0, 0))).reshape(32, D)
-    (qkv, mixed, resid, rp, gg, bb, bi, xr, gp, act, gh, pb, pg, pg0) = dispatch_call(
-        tok, rt, vec, w_qkv, w_out, wrt, b_in, b_back, dout, w_in, w_back
+    (vec, tab, tw, qkv, mixed, resid, rp, gg, bb, bi, dw, xr, gp, act, gh, pb, pg, pg0) = dispatch_call(
+        tokens, d_out, routes, gain_one, shift_one, gain_two, shift_two, out_bias, qv_bias,
+        w_qkv, w_out, wrt, b_in, b_back, w_in, w_back,
     )
     block, ig, ar, kb, ki, lb, li, _ = grads_call(
-        vec, rt, wrt, bb, bi, rp, tok, dout, w_qkv, w_out, qkv, mixed, resid, gg, xr, gp, act, gh, pb, pg, pg0
+        vec, tab, wrt, bb, bi, rp, tw, dw, w_qkv, w_out, qkv, mixed, resid, gg, xr, gp, act, gh, pb, pg, pg0
     )
-    dp, z = lax.axis_index("dp"), lax.axis_index("expert")
-    rows = MB * SEQ
-    ext = ar[4 * D :].astype(F32)
-    qkv_grad = jnp.concatenate([ar[i * D : (i + 1) * D] for i in range(3)], axis=1).astype(F32)
-    biases = lax.dynamic_slice(ext, (24 + 5 * LOCAL * z, 0), (5 * LOCAL, D))
-    bb_grad = lax.dynamic_slice(biases[:LOCAL], (0, dp * BAND), (LOCAL, BAND))
-    bi_grad = jnp.transpose(biases[LOCAL:].reshape(4, LOCAL, D), (1, 0, 2)).reshape(LOCAL, HIDDEN)
-    bi_grad = lax.dynamic_slice(bi_grad, (0, dp * PART), (LOCAL, PART))
-    return (
-        block[:, :SEQ].reshape(rows, D),
-        ig[:, :SEQ].reshape(rows, D),
-        ext[0],
-        ext[1],
-        qkv_grad,
-        ext[2:4],
-        ar[3 * D : 4 * D].astype(F32),
-        ext[4],
-        ext[5],
-        ext[6],
-        ext[8 : 8 + NZ * LOCAL].T,
-        ki.astype(F32) + li.astype(F32),
-        bi_grad,
-        kb.astype(F32) + lb.astype(F32),
-        bb_grad,
-    )
+    out = list(finish_call(ar, kb, ki, lb, li, block, ig))
+    out[10] = out[10].T
+    return tuple(out)
 
 
 def solution(mesh):

time: 397 us -> 352 us (0.89)
  Pallas kernels: 364 us -> 342 us
  other arithmetic: 14.4 us -> 0 us
  local copies, waits for them, and re-layouts: 10.5 us -> 2.89 us
    pallas_call x1, Pallas kernels: 219 us -> 188 us  [grads_call(): pl.pallas_call(grads_kernel, out_shape=[o[0] for o in outs], in_specs=[vm...]
    pallas_call x0 -> x1, Pallas kernels: none -> 13.7 us  [finish_call(): pl.pallas_call(finish_kernel, out_shape=[o[0] for o in outs], in_specs=[h...]
    add x2 -> x0, other arithmetic: 8.47 us -> none  [the longest x1 5.45 us: fast_body(): kb.astype(F32) + lb.astype(F32)]
    convert_element_type x3 -> x0, other arithmetic: 5.95 us -> none  [the longest x1 3.19 us: fast_body(): jnp.concatenate([ar[i * D:(i + 1) * D] for i in range(3)], axis=1)]
where the time goes in v4:
time: 352 us; the launch traced here: 346 us
  Pallas kernels  342 us (97%)
    pallas_call x1, Pallas kernels, grads_call(): pl.pallas_call(grads_kernel, out_shape=[o[0] for o in outs], in_specs=[vm...  188 us
    pallas_call x1, Pallas kernels, dispatch_call(): pl.pallas_call(dispatch_kernel, out_shape=[o[0] for o in outs], in_specs=...  141 us
    pallas_call x1, Pallas kernels, finish_call(): pl.pallas_call(finish_kernel, out_shape=[o[0] for o in outs], in_specs=[h...  13.7 us

profile of v4, /device:TPU:0, one launch (start us, length us, event | category | flops | bytes accessed | tf_op | source)
XLA Modules:
  0.0 345.7 jit_solution(13850030934600671613)
XLA Ops:
  0.6 0.8 reshape.36
  1.4 0.6 pad_bitcast_fusion.wrt
  2.0 1.5 copy.31.routes
  3.5 140.6 %dispatch.1 = (f32[8,768]{1,0:T(8,128)}, f32[2,32,208]{2,1,0:T(8,128)}, bf16[2,208,768]{2,1,0:T(8,128)(2,1)}, bf16[2,208,2304]{2,1,0:T(8,128)(2,1)}, bf16[2,208,...) custom-call(bf16[394,768]{1,0:T(8,128)(2,1)} %tok.1, ...), custom_call_target="tpu_custom_call" | custom-call | tf_op jit(solution)/shard_map/dispatch/pallas_call | solution.py:750
  144.2 187.6 %grads.1 = (bf16[2,208,768]{2,1,0:T(8,128)(2,1)}, f32[2,208,768]{2,1,0:T(8,128)}, bf16[3200,768]{1,0:T(8,128)(2,1)}, bf16[4,384,768]{2,1,0:T(8,128)(2,1)}, bf16[...) custom-call(f32[8,768]{1,0:T(8,128)} %get-tuple-element.55.vec, ...), custom_call_target="tpu_custom_call" | custom-call | tf_op jit(solution)/shard_map/grads/pallas_call | solution.py:1320
  331.8 13.7 %finish.1 = (bf16[394,768]{1,0:T(8,128)(2,1)}, f32[394,768]{1,0:T(8,128)}, f32[768]{0:T(1024)}, f32[768]{0:T(1024)}, f32[768,2304]{1,0:T(8,128)}, /*index=5*/f32...) custom-call(bf16[3200,768]{1,0:T(8,128)(2,1)} %get-tuple-element.73., ...), custom_call_target="tpu_custom_call" | custom-call | tf_op jit(solution)/shard_map/finish/pallas_call | solution.py:1440

commit v5 on v4

--- a/solution.py
+++ b/solution.py
@@ -293,6 +293,8 @@
 PACKED = 176
 ROWS = NZ * CAP_ROWS
 CHUNK = 768
+PIECE = 1536
+PIECES = 4 * CHUNK // PIECE
 MESH = pl.DeviceIdType.MESH
 NT = (((1,), (1,)), ((), ()))
 TN = (((0,), (0,)), ((), ()))
@@ -416,9 +418,9 @@
             start(kind, mb, h + 1)
 
     def weights(n, slot):
-        e = lax.rem(n, 16) // 4
-        f = lax.rem(n, 4)
-        cols = pl.ds(pl.multiple_of(f * CHUNK, CHUNK), CHUNK)
+        e = lax.rem(n, LOCAL * PIECES) // PIECES
+        f = lax.rem(n, PIECES)
+        cols = pl.ds(pl.multiple_of(f * PIECE, PIECE), PIECE)
         return (
             pltpu.make_async_copy(w_in.at[e, :, cols], wb1.at[slot], w_sem.at[0, slot]),
             pltpu.make_async_copy(w_back.at[e, cols, :], wb2.at[slot], w_sem.at[1, slot]),
@@ -488,7 +490,7 @@
             mixed_s[:, at[0]] = mixed.astype(BF16)
             return carry
 
-        lax.fori_loop(0, PAIRS, heads, 0)
+        lax.fori_loop(0, PAIRS, heads, 0, unroll=3)
         qkv_o[mb] = qkv_s[0:T, :]
         mixed_o[mb] = mixed_s[...]
         resid = x + dot(mixed_s[...], wout[...]) + vec[4:5]
@@ -510,12 +512,22 @@
         return carry
 
     lax.fori_loop(0, MB, forward, 0)
+    middle = jnp.logical_and(z > 0, z < NZ - 1)
+
+    @pl.when(jnp.logical_not(middle))
+    def _():
+        for kind in range(3):
+            start(kind, 1, 0)
+
     for h in range(NZ - 1):
         for kind in (3, 0, 1, 2):
             pass_on(kind, 0, h)
         pass_on(3, 1, h)
-    for kind in range(3):
-        start(kind, 1, 0)
+
+    @pl.when(middle)
+    def _():
+        for kind in range(3):
+            start(kind, 1, 0)
 
     def micro(mb, carry):
         @pl.when(mb == 1)
@@ -557,11 +569,11 @@
             acc_g[...] = jnp.zeros_like(acc_g)
 
             def step(f, carry):
-                n = mb * 16 + e * 4 + f
+                n = (mb * LOCAL + e) * PIECES + f
                 slot = lax.rem(n, 2)
-                cols = pl.ds(pl.multiple_of(f * CHUNK, CHUNK), CHUNK)
-
-                @pl.when(n + 1 < 16 * MB)
+                cols = pl.ds(pl.multiple_of(f * PIECE, PIECE), PIECE)
+
+                @pl.when(n + 1 < LOCAL * PIECES * MB)
                 def _():
                     for copy in weights(n + 1, 1 - slot):
                         copy.start()
@@ -592,7 +604,7 @@
                     copy.start()
                 return carry
 
-            lax.fori_loop(0, 4, step, 0)
+            lax.fori_loop(0, PIECES, step, 0)
             out = (acc_o[...] + b_back[pl.ds(e, 1), :]).astype(BF16).astype(F32)
             gg = jnp.sum(out * cs[e].astype(F32), axis=1, keepdims=True)
             scaled = (out * rgs[e][:, 0:1]).astype(BF16)
@@ -604,18 +616,18 @@
                 grs[src, at, :] = back[part]
                 ggs[src, at, :] = jnp.broadcast_to(gg[part], (CAP_ROWS, 128))
 
-            @pl.when(jnp.logical_and(mb == 1, e == 0))
+            @pl.when(jnp.logical_and(mb == 1, e == jnp.where(middle, 1, 0)))
             def _():
                 for d in range(1, NZ):
                     sent_home(d).start()
                 own_home().start()
 
-            @pl.when(jnp.logical_and(mb == 0, e == 1))
+            @pl.when(jnp.logical_and(mb == 0, e == 0))
             def _():
                 for kind in range(3):
                     pass_on(kind, 1, 0)
 
-            @pl.when(jnp.logical_and(mb == 0, e == 3))
+            @pl.when(jnp.logical_and(mb == 0, e == 2))
             def _():
                 for kind in range(3):
                     pass_on(kind, 1, 1)
@@ -623,10 +635,10 @@
             return carry
 
         def stores(n, slot):
-            m = n // 16
-            e = lax.rem(n, 16) // 4
-            f = lax.rem(n, 4)
-            at = (e, pl.ds(pl.multiple_of(m * ROWS, 16), ROWS), pl.ds(pl.multiple_of(f * CHUNK, CHUNK), CHUNK))
+            m = n // (LOCAL * PIECES)
+            e = lax.rem(n, LOCAL * PIECES) // PIECES
+            f = lax.rem(n, PIECES)
+            at = (e, pl.ds(pl.multiple_of(m * ROWS, 16), ROWS), pl.ds(pl.multiple_of(f * PIECE, PIECE), PIECE))
             return (
                 pltpu.make_async_copy(act_st.at[slot], act_o.at[at], st_sem.at[0, slot]),
                 pltpu.make_async_copy(gh_st.at[slot], gh_o.at[at], st_sem.at[1, slot]),
@@ -637,7 +649,7 @@
         @pl.when(mb == 1)
         def _():
             for slot in (0, 1):
-                for copy in stores(16 * MB - 2 + slot, slot):
+                for copy in stores(LOCAL * PIECES * MB - 2 + slot, slot):
                     copy.wait()
 
         @pl.when(mb == 1)
@@ -757,8 +769,8 @@
             V((KEYS, 3 * D), BF16), V((T, D), BF16), V((8, 128), F32),
             V((LOCAL, rows, D), BF16), V((LOCAL, rows, D), BF16), V((LOCAL, ROWS, D), BF16),
             V((LOCAL, ROWS, 128), F32), V((NZ, ROWS, 128), F32),
-            V((2, D, CHUNK), BF16), V((2, CHUNK, D), BF16),
-            V((2, ROWS, CHUNK), BF16), V((2, ROWS, CHUNK), BF16),
+            V((2, D, PIECE), BF16), V((2, PIECE, D), BF16),
+            V((2, ROWS, PIECE), BF16), V((2, ROWS, PIECE), BF16),
             V((ROWS, D), F32), V((ROWS, D), F32),
             V((NZ, ROWS, D), BF16), V((NZ, ROWS, D), BF16),
             V((NZ, T, D), BF16), V((NZ, T, D), BF16),
@@ -885,7 +897,7 @@
     def keep(kind, e):
         return pltpu.make_async_copy(cores[kind].at[e, yx], keeps[kind].at[e], f_sem.at[kind, e])
 
-    for item in range(3):
+    for item in range(2):
         for d in range(1, NZ):
             home(item, d).start()
 
@@ -980,7 +992,7 @@
                     gqkv_s[mb, :, at[2]] = gv[0:T].astype(BF16)
                     return carry
 
-                lax.fori_loop(0, PAIRS, heads, 0)
+                lax.fori_loop(0, PAIRS, heads, 0, unroll=2)
                 for row, i in ((2, 0), (3, 2)):
                     ext[row : row + 1, :] += jnp.sum(
                         gqkv_s[mb, :, i * D : (i + 1) * D].astype(F32), axis=0, keepdims=True
@@ -1074,7 +1086,11 @@
                     if at != dest:
                         along(flow, dest, slot).start()
 
+            for d in range(1, NZ):
+                home(2, d).start()
             one(2)
+            for kind in (0, 1):
+                turn(kind, 1)
             for step, order in enumerate((
                 ((0, 0, 2), (1, 3, 1)),
                 ((0, 1, 2), (1, 3, 2), (1, 2, 1), (0, 0, 1)),
@@ -1082,9 +1098,6 @@
             )):
                 for flow, dest, at in order:
                     sum_one(flow, dest, at)
-                if step == 1:
-                    for kind in (0, 1):
-                        turn(kind, 1)
 
             halves = (slice(0, 208), slice(208, SHARE))
 
@@ -1155,7 +1168,7 @@
                 wg_b[k] = back_block(k, 1 - c).astype(BF16)
                 return carry
 
-            lax.fori_loop(0, 4, other_b, 0)
+            lax.fori_loop(0, 4, other_b, 0, unroll=2)
             core_copy(0, e, wg_b).start()
             ready(e, (2, 3))
             for side in (0, 1):
@@ -1173,7 +1186,7 @@
                     wg_i[k, :, at] = grad[k * BAND : (k + 1) * BAND]
                 return carry
 
-            lax.fori_loop(0, 4, other_i, 0)
+            lax.fori_loop(0, 4, other_i, 0, unroll=2)
             core_copy(1, e, wg_i).start()
             core_copy(0, e, wg_b).wait_recv()
 
@@ -1181,7 +1194,7 @@
                 core_b[e, k] = (core_b[e, k].astype(F32) + back_block(k, c)).astype(BF16)
                 return carry
 
-            lax.fori_loop(0, 4, own_b, 0)
+            lax.fori_loop(0, 4, own_b, 0, unroll=2)
 
             send1(0, e)
             if e < LOCAL - 1:
@@ -1198,7 +1211,7 @@
                     ).astype(BF16)
                 return carry
 
-            lax.fori_loop(0, 4, own_i, 0)
+            lax.fori_loop(0, 4, own_i, 0, unroll=2)
 
             send1(1, e)
             if e < LOCAL - 1:
@@ -1244,7 +1257,7 @@
             spread(up, 0).start()
 
     to_partner(ar_t, 0, z).start()
-    for mb in range(MB):
+    def block_out(mb):
         def image_out(base, quad_s, low):
             quad = [quad_s.at[i] for i in range(NZ)]
             fetch = pltpu.make_async_copy(resid.at[mb], base, l_sem.at[5])
@@ -1257,6 +1270,8 @@
             store.wait()
 
         pl.run_scoped(image_out, V((T, D), F32), V((NZ, T, D), BF16), V((T, D), BF16))
+
+    block_out(0)
     for h in range(NZ - 1):
         for up in (True, False):
             source = z - h - 1 if up else z + h + 1
@@ -1278,6 +1293,7 @@
         if h < 2:
             for kind in (0, 1):
                 turn(kind, 2 + h)
+    block_out(1)
     own_share.wait()
     for k in range(NZ):
         zz = lax.rem(z + k, NZ)

time: 352 us -> 340 us (0.966)
  Pallas kernels: 342 us -> 332 us
    pallas_call x1, Pallas kernels: 141 us -> 123 us  [dispatch_call(): pl.pallas_call(dispatch_kernel, out_shape=[o[0] for o in outs], in_specs=...]
    pallas_call x1, Pallas kernels: 188 us -> 195 us  [grads_call(): pl.pallas_call(grads_kernel, out_shape=[o[0] for o in outs], in_specs=[vm...]
where the time goes in v5:
time: 340 us; the launch traced here: 336 us
  Pallas kernels  332 us (98%)
    pallas_call x1, Pallas kernels, grads_call(): pl.pallas_call(grads_kernel, out_shape=[o[0] for o in outs], in_specs=[vm...  195 us
    pallas_call x1, Pallas kernels, dispatch_call(): pl.pallas_call(dispatch_kernel, out_shape=[o[0] for o in outs], in_specs=...  123 us
    pallas_call x1, Pallas kernels, finish_call(): pl.pallas_call(finish_kernel, out_shape=[o[0] for o in outs], in_specs=[h...  13.7 us

profile of v5, /device:TPU:0, one launch (start us, length us, event | category | flops | bytes accessed | tf_op | source)
XLA Modules:
  0.0 335.6 jit_solution(17263447175731105089)
XLA Ops:
  0.6 0.8 reshape.36
  1.4 0.6 pad_bitcast_fusion.wrt
  2.0 1.5 copy.31.routes
  3.5 122.9 %dispatch.1 = (f32[8,768]{1,0:T(8,128)}, f32[2,32,208]{2,1,0:T(8,128)}, bf16[2,208,768]{2,1,0:T(8,128)(2,1)}, bf16[2,208,2304]{2,1,0:T(8,128)(2,1)}, bf16[2,208,...) custom-call(bf16[394,768]{1,0:T(8,128)(2,1)} %tok.1, ...), custom_call_target="tpu_custom_call" | custom-call | tf_op jit(solution)/shard_map/dispatch/pallas_call | solution.py:762
  126.5 194.9 %grads.1 = (bf16[2,208,768]{2,1,0:T(8,128)(2,1)}, f32[2,208,768]{2,1,0:T(8,128)}, bf16[3200,768]{1,0:T(8,128)(2,1)}, bf16[4,384,768]{2,1,0:T(8,128)(2,1)}, bf16[...) custom-call(f32[8,768]{1,0:T(8,128)} %get-tuple-element.55.vec, ...), custom_call_target="tpu_custom_call" | custom-call | tf_op jit(solution)/shard_map/grads/pallas_call | solution.py:1336
  321.4 13.7 %finish.1 = (bf16[394,768]{1,0:T(8,128)(2,1)}, f32[394,768]{1,0:T(8,128)}, f32[768]{0:T(1024)}, f32[768]{0:T(1024)}, f32[768,2304]{1,0:T(8,128)}, /*index=5*/f32...) custom-call(bf16[3200,768]{1,0:T(8,128)(2,1)} %get-tuple-element.73., ...), custom_call_target="tpu_custom_call" | custom-call | tf_op jit(solution)/shard_map/finish/pallas_call | solution.py:1456

commit v6 on v5

--- a/solution.py
+++ b/solution.py
@@ -1293,7 +1293,8 @@
         if h < 2:
             for kind in (0, 1):
                 turn(kind, 2 + h)
-    block_out(1)
+        if h == 1:
+            block_out(1)
     own_share.wait()
     for k in range(NZ):
         zz = lax.rem(z + k, NZ)

time: 340 us -> 340 us (level)
  no operation moved by 1% of the time
where the time goes in v6:
time: 340 us; the launch traced here: 336 us
  Pallas kernels  332 us (98%)
    pallas_call x1, Pallas kernels, grads_call(): pl.pallas_call(grads_kernel, out_shape=[o[0] for o in outs], in_specs=[vm...  195 us
    pallas_call x1, Pallas kernels, dispatch_call(): pl.pallas_call(dispatch_kernel, out_shape=[o[0] for o in outs], in_specs=...  123 us
    pallas_call x1, Pallas kernels, finish_call(): pl.pallas_call(finish_kernel, out_shape=[o[0] for o in outs], in_specs=[h...  13.7 us

profile of v6, /device:TPU:0, one launch (start us, length us, event | category | flops | bytes accessed | tf_op | source)
XLA Modules:
  0.0 335.6 jit_solution(14943288744553047509)
XLA Ops:
  0.6 0.8 reshape.36
  1.4 0.6 pad_bitcast_fusion.wrt
  2.0 1.5 copy.31.routes
  3.5 122.9 %dispatch.1 = (f32[8,768]{1,0:T(8,128)}, f32[2,32,208]{2,1,0:T(8,128)}, bf16[2,208,768]{2,1,0:T(8,128)(2,1)}, bf16[2,208,2304]{2,1,0:T(8,128)(2,1)}, bf16[2,208,...) custom-call(bf16[394,768]{1,0:T(8,128)(2,1)} %tok.1, ...), custom_call_target="tpu_custom_call" | custom-call | tf_op jit(solution)/shard_map/dispatch/pallas_call | solution.py:762
  126.5 194.9 %grads.1 = (bf16[2,208,768]{2,1,0:T(8,128)(2,1)}, f32[2,208,768]{2,1,0:T(8,128)}, bf16[3200,768]{1,0:T(8,128)(2,1)}, bf16[4,384,768]{2,1,0:T(8,128)(2,1)}, bf16[...) custom-call(f32[8,768]{1,0:T(8,128)} %get-tuple-element.55.vec, ...), custom_call_target="tpu_custom_call" | custom-call | tf_op jit(solution)/shard_map/grads/pallas_call | solution.py:1337
  321.4 13.7 %finish.1 = (bf16[394,768]{1,0:T(8,128)(2,1)}, f32[394,768]{1,0:T(8,128)}, f32[768]{0:T(1024)}, f32[768]{0:T(1024)}, f32[768,2304]{1,0:T(8,128)}, /*index=5*/f32...) custom-call(bf16[3200,768]{1,0:T(8,128)(2,1)} %get-tuple-element.73., ...), custom_call_target="tpu_custom_call" | custom-call | tf_op jit(solution)/shard_map/finish/pallas_call | solution.py:1457
